TPU v7x, 32 devices: a whole 2x2x4 slice. The times are simulated.
32 devices in a mesh: batch: 8 (over y, x, core), head: 4 (over z).
Axes of the slice: x: 2, y: 2, z: 4, core: 2. Of those that a mesh axis runs over, the one named last changes fastest.
Arguments:
- tokens: bfloat16 [4608, 1024], P('batch'), may hold values from -6 to 6
- page_lengths: int32 [8], P('batch'), may hold values from 144 to 576
- corners: int32 [2, 4608], P(None, 'batch'), may hold values from 0 to 1023
- w_query: bfloat16 [1024, 1024], P(None, 'head'), may hold values from -0.1875 to 0.1875
- w_key: bfloat16 [1024, 1024], P(None, 'head'), may hold values from -0.1875 to 0.1875
- w_value: bfloat16 [1024, 1024], P(None, 'head'), may hold values from -0.1875 to 0.1875
- w_output: bfloat16 [1024, 1024], P('head'), may hold values from -0.75 to 0.75
- b_output: float32 [1024], replicated, may hold values from -1.5 to 1.5
- gain_attn: float32 [1024], replicated, may hold values from 0.1 to 1.9
- shift_attn: float32 [1024], replicated, may hold values from -2.5 to 2.5
- w_inner: bfloat16 [1024, 4096], P(None, 'head'), may hold values from -0.1875 to 0.1875
- b_inner: float32 [4096], P('head'), may hold values from -2.5 to 2.5
- w_outer: bfloat16 [4096, 1024], P('head'), may hold values from -0.125 to 0.125
- b_outer: float32 [1024], replicated, may hold values from -1.5 to 1.5
- gain_ffn: float32 [1024], replicated, may hold values from 0.1 to 1.9
- shift_ffn: float32 [1024], replicated, may hold values from -2.5 to 2.5
- rel_tables: bfloat16 [3, 128, 1024], replicated, may hold values from -6 to 6
- cotangent: bfloat16 [4608, 1024], P('batch'), may hold values from -6 to 6
Outputs:
- output: bfloat16 [4608, 1024], P('batch')
- grad_tokens: bfloat16 [4608, 1024], P('batch')
- grad_w_query: float32 [1024, 1024], P('batch', 'head')
- grad_w_key: float32 [1024, 1024], P('batch', 'head')
- grad_w_value: float32 [1024, 1024], P('batch', 'head')
- grad_w_output: float32 [1024, 1024], P('head', 'batch')
- grad_b_output: float32 [1024], replicated
- grad_gain_attn: float32 [1024], replicated
- grad_shift_attn: float32 [1024], replicated
- grad_w_inner: float32 [1024, 4096], P('batch', 'head')
- grad_b_inner: float32 [4096], P('head')
- grad_w_outer: float32 [4096, 1024], P('head', 'batch')
- grad_b_outer: float32 [1024], replicated
- grad_gain_ffn: float32 [1024], replicated
- grad_shift_ffn: float32 [1024], replicated
- grad_rel: float32 [3, 128, 1024], replicated
All inputs are finite; a program needn't handle non-finite values.
Results may differ from a plain program's by a relative error of at most 0.02.
Values sent between devices are 32-bit elements; how exact they have to be, the bound alone decides.
A program may use at most 128 MiB of HBM per device.

v0:
```python
import jax
import jax.numpy as jnp
from jax import lax
from jax.sharding import PartitionSpec as P

HEAD = 64
NB = 128
BOX_STEP = 8


NEG_FILL = -1000000000.0


def bucket_table(coord_row, step_size):
    difference = coord_row[:, None] - coord_row[None, :]
    return jnp.clip(difference // step_size, -(NB // 2), NB // 2 - 1) + NB // 2


def mixed(form, wide, narrow):
    upper = wide.astype(jnp.bfloat16)
    lower = (wide - upper.astype(jnp.float32)).astype(jnp.bfloat16)
    return jnp.einsum(form, upper, narrow, preferred_element_type=jnp.float32) + jnp.einsum(
        form, lower, narrow, preferred_element_type=jnp.float32
    )


def layer_stats(values):
    average = jnp.mean(values, axis=-1, keepdims=True)
    centered = values - average
    spread_squared = jnp.mean(centered * centered, axis=-1, keepdims=True)
    scaling = lax.rsqrt(spread_squared + 1e-05)
    return (centered * scaling, scaling)


def norm_back(upstream, normed, scaling, gain_in):
    scaled = upstream * gain_in
    inward = scaling * (
        scaled
        - jnp.mean(scaled, axis=-1, keepdims=True)
        - normed * jnp.mean(scaled * normed, axis=-1, keepdims=True)
    )
    return (inward, jnp.sum(upstream * normed, axis=0), jnp.sum(upstream, axis=0))


def block_rows():
    return 64


def onehot_rows(table_rows):
    return (table_rows[..., None] == jnp.arange(NB, dtype=jnp.int32)).astype(jnp.bfloat16)


def relative_terms(forward_offset, beside, tables):
    heads_dev = forward_offset.shape[1]
    slots_page = forward_offset.shape[2]
    rows_block = block_rows()
    blocks = slots_page // rows_block
    stacked = jnp.moveaxis(jnp.stack(tables).reshape(3, blocks, rows_block, slots_page), 1, 0)
    toward_blocks = jnp.moveaxis(forward_offset.reshape(3, heads_dev, blocks, rows_block, NB), 2, 0)
    beside_blocks = jnp.moveaxis(beside.reshape(3, heads_dev, blocks, rows_block, NB), 2, 0)

    def one_block(carry, pieces):
        table_block, toward_block, adjacent_block = pieces
        onehot = onehot_rows(table_block)
        row_part = mixed("thib,tijb->hij", toward_block, onehot)
        col_part = mixed("thjb,tjib->hij", adjacent_block, onehot)
        return (carry, (row_part, col_part))

    _, (row_parts, col_parts) = lax.scan(one_block, 0, (stacked, toward_blocks, beside_blocks))
    row_whole = jnp.transpose(row_parts, (1, 0, 2, 3)).reshape(heads_dev, slots_page, slots_page)
    col_whole = jnp.transpose(col_parts, (1, 2, 0, 3)).reshape(heads_dev, slots_page, slots_page)
    return row_whole + col_whole


def relative_back(grad_logit, tables, scale_factor):
    heads_dev = grad_logit.shape[0]
    slots_page = grad_logit.shape[1]
    rows_block = block_rows()
    blocks = slots_page // rows_block
    stacked = jnp.moveaxis(jnp.stack(tables).reshape(3, blocks, rows_block, slots_page), 1, 0)
    gradient_row_values = jnp.moveaxis(
        grad_logit.reshape(heads_dev, blocks, rows_block, slots_page), 1, 0
    )
    grad_cols = jnp.moveaxis(grad_logit.reshape(heads_dev, slots_page, blocks, rows_block), 2, 0)

    def one_block(carry, pieces):
        table_block, row_block, col_block = pieces
        onehot = onehot_rows(table_block)
        toward_part = jnp.einsum(
            "hij,tijb->thib", row_block, onehot, preferred_element_type=jnp.float32
        )
        beside_part = jnp.einsum(
            "hij,tjib->thjb", col_block, onehot, preferred_element_type=jnp.float32
        )
        return (carry, (toward_part, beside_part))

    _, (toward_parts, beside_parts) = lax.scan(
        one_block, 0, (stacked, gradient_row_values, grad_cols)
    )
    grad_toward = (
        jnp.transpose(toward_parts, (1, 2, 0, 3, 4)).reshape(3, heads_dev, slots_page, NB)
        * scale_factor
    )
    grad_beside = (
        jnp.transpose(beside_parts, (1, 2, 0, 3, 4)).reshape(3, heads_dev, slots_page, NB)
        * scale_factor
    )
    return (grad_toward, grad_beside)


def page_logits(
    query_page_rows, key_page, key_relative_table, query_rel, length, corner_x, corner_y
):
    slots_page = query_page_rows.shape[0]
    positions = jnp.arange(slots_page, dtype=jnp.int32)
    tables = (
        bucket_table(positions, 1),
        bucket_table(corner_x, BOX_STEP),
        bucket_table(corner_y, BOX_STEP),
    )
    forward_offset = jnp.einsum(
        "ihd,tbhd->thib", query_page_rows, key_relative_table, preferred_element_type=jnp.float32
    )
    beside = jnp.einsum("jhd,tbhd->thjb", key_page, query_rel, preferred_element_type=jnp.float32)
    content = jnp.einsum(
        "ihd,jhd->hij", query_page_rows, key_page, preferred_element_type=jnp.float32
    )
    logits = (content + relative_terms(forward_offset, beside, tables)) * (7.0 * HEAD) ** (-0.5)
    masked = jnp.where(positions[None, None, :] < length, logits, NEG_FILL)
    return (masked, tables)


def shards(
    tokens,
    page_lengths,
    corners,
    w_query,
    w_key,
    w_value,
    w_output,
    b_output,
    gain_attn,
    shift_attn,
    w_inner,
    b_inner,
    w_outer,
    b_outer,
    gain_ffn,
    shift_ffn,
    rel_tables,
    cotangent,
):
    rows_dev = tokens.shape[0]
    pages_dev = page_lengths.shape[0]
    slots_page = rows_dev // pages_dev
    heads_dev = w_query.shape[1] // HEAD
    scale_factor = (7.0 * HEAD) ** (-0.5)

    def by_page(matrix):
        return matrix.reshape(pages_dev, slots_page, heads_dev, HEAD)

    queries = jnp.dot(tokens, w_query, preferred_element_type=jnp.float32).astype(jnp.bfloat16)
    key_rows = jnp.dot(tokens, w_key, preferred_element_type=jnp.float32).astype(jnp.bfloat16)
    value_rows = jnp.dot(tokens, w_value, preferred_element_type=jnp.float32).astype(jnp.bfloat16)
    key_relative_table = (
        jnp.einsum("tbc,cd->tbd", rel_tables, w_key, preferred_element_type=jnp.float32)
        .astype(jnp.bfloat16)
        .reshape(3, NB, heads_dev, HEAD)
    )
    query_rel = (
        jnp.einsum("tbc,cd->tbd", rel_tables, w_query, preferred_element_type=jnp.float32)
        .astype(jnp.bfloat16)
        .reshape(3, NB, heads_dev, HEAD)
    )
    corner_x = corners[0].reshape(pages_dev, slots_page)
    corner_y = corners[1].reshape(pages_dev, slots_page)

    def page_forward(pieces):
        query_page_rows, key_page, value_page, length, row_x, row_y = pieces
        masked, tables = page_logits(
            query_page_rows, key_page, key_relative_table, query_rel, length, row_x, row_y
        )
        row_peak = jnp.max(masked, axis=-1, keepdims=True)
        log_total = row_peak + jnp.log(jnp.sum(jnp.exp(masked - row_peak), axis=-1, keepdims=True))
        attend = jnp.exp(masked - log_total).astype(jnp.bfloat16)
        context_page = jnp.einsum(
            "hij,jhd->ihd", attend, value_page, preferred_element_type=jnp.float32
        ).astype(jnp.bfloat16)
        return (context_page, log_total)

    context, log_total = lax.map(
        page_forward,
        (
            by_page(queries),
            by_page(key_rows),
            by_page(value_rows),
            page_lengths,
            corner_x,
            corner_y,
        ),
    )
    context = context.reshape(rows_dev, heads_dev * HEAD)
    partial_attn = jnp.dot(context, w_output, preferred_element_type=jnp.float32)
    token_float = tokens.astype(jnp.float32)
    attention_total = lax.psum(partial_attn, "head")
    normed_one, scale_one = layer_stats(attention_total + b_output + token_float)
    hidden_one = normed_one * gain_attn + shift_attn
    hidden_low = hidden_one.astype(jnp.bfloat16)
    inner_pre = jnp.dot(hidden_low, w_inner, preferred_element_type=jnp.float32) + b_inner
    active = jax.nn.gelu(inner_pre, approximate=False).astype(jnp.bfloat16)
    partial_ffn = jnp.dot(active, w_outer, preferred_element_type=jnp.float32)
    ffn_total = lax.psum(partial_ffn, "head")
    normed_two, scale_two = layer_stats(ffn_total + b_outer + hidden_one)
    output = (normed_two * gain_ffn + shift_ffn).astype(jnp.bfloat16)
    grad_out = cotangent.astype(jnp.float32)
    grad_mid, grad_gain_ffn, grad_shift_ffn = norm_back(grad_out, normed_two, scale_two, gain_ffn)
    grad_b_outer = jnp.sum(grad_mid, axis=0)
    grad_mid_low = grad_mid.astype(jnp.bfloat16)
    grad_w_outer = jnp.einsum("tf,td->fd", active, grad_mid_low, preferred_element_type=jnp.float32)
    grad_active = jnp.einsum("td,fd->tf", grad_mid_low, w_outer, preferred_element_type=jnp.float32)
    _, gelu_pull = jax.vjp(lambda pre_value: jax.nn.gelu(pre_value, approximate=False), inner_pre)
    grad_inner = gelu_pull(grad_active)[0]
    grad_b_inner = jnp.sum(grad_inner, axis=0)
    grad_inner_low = grad_inner.astype(jnp.bfloat16)
    grad_w_inner = jnp.einsum(
        "td,tf->df", hidden_low, grad_inner_low, preferred_element_type=jnp.float32
    )
    partial_hidden = jnp.einsum(
        "tf,df->td", grad_inner_low, w_inner, preferred_element_type=jnp.float32
    )
    grad_hidden = lax.psum(partial_hidden, "head") + grad_mid
    grad_attn, grad_gain_attn, grad_shift_attn = norm_back(
        grad_hidden, normed_one, scale_one, gain_attn
    )
    grad_b_output = jnp.sum(grad_attn, axis=0)
    grad_attn_low = grad_attn.astype(jnp.bfloat16)
    grad_w_output = jnp.einsum(
        "tc,td->cd", context, grad_attn_low, preferred_element_type=jnp.float32
    )
    grad_context = jnp.einsum(
        "td,cd->tc", grad_attn_low, w_output, preferred_element_type=jnp.float32
    ).astype(jnp.bfloat16)

    def page_backward(pieces):
        query_page_rows, key_page, value_page, length, row_x, row_y, total_page, grad_page = pieces
        masked, tables = page_logits(
            query_page_rows, key_page, key_relative_table, query_rel, length, row_x, row_y
        )
        attend = jnp.exp(masked - total_page)
        grad_attend = jnp.einsum(
            "ihd,jhd->hij", grad_page, value_page, preferred_element_type=jnp.float32
        )
        grad_value = jnp.einsum(
            "hij,ihd->jhd",
            attend.astype(jnp.bfloat16),
            grad_page,
            preferred_element_type=jnp.float32,
        )
        grad_masked = attend * (grad_attend - jnp.sum(grad_attend * attend, axis=-1, keepdims=True))
        grad_logit = grad_masked.astype(jnp.bfloat16)
        grad_toward, grad_beside = relative_back(grad_logit, tables, scale_factor)
        grad_query = jnp.einsum(
            "hij,jhd->ihd", grad_logit, key_page, preferred_element_type=jnp.float32
        ) * scale_factor + mixed("thib,tbhd->ihd", grad_toward, key_relative_table)
        grad_key = jnp.einsum(
            "hij,ihd->jhd", grad_logit, query_page_rows, preferred_element_type=jnp.float32
        ) * scale_factor + mixed("thjb,tbhd->jhd", grad_beside, query_rel)
        grad_krel = mixed("thib,ihd->tbhd", grad_toward, query_page_rows)
        grad_qrel = mixed("thjb,jhd->tbhd", grad_beside, key_page)
        return (
            grad_query.astype(jnp.bfloat16),
            grad_key.astype(jnp.bfloat16),
            grad_value.astype(jnp.bfloat16),
            grad_krel,
            grad_qrel,
        )

    paged_grads = lax.map(
        page_backward,
        (
            by_page(queries),
            by_page(key_rows),
            by_page(value_rows),
            page_lengths,
            corner_x,
            corner_y,
            log_total,
            by_page(grad_context),
        ),
    )
    grad_queries = paged_grads[0].reshape(rows_dev, heads_dev * HEAD)
    grad_keys = paged_grads[1].reshape(rows_dev, heads_dev * HEAD)
    grad_values = paged_grads[2].reshape(rows_dev, heads_dev * HEAD)
    grad_key_rel = jnp.sum(paged_grads[3], axis=0).reshape(3, NB, heads_dev * HEAD)
    grad_query_rel = jnp.sum(paged_grads[4], axis=0).reshape(3, NB, heads_dev * HEAD)
    grad_w_query = jnp.einsum(
        "tc,td->cd", tokens, grad_queries, preferred_element_type=jnp.float32
    ) + mixed("tbd,tbc->cd", grad_query_rel, rel_tables)
    grad_w_key = jnp.einsum(
        "tc,td->cd", tokens, grad_keys, preferred_element_type=jnp.float32
    ) + mixed("tbd,tbc->cd", grad_key_rel, rel_tables)
    grad_w_value = jnp.einsum("tc,td->cd", tokens, grad_values, preferred_element_type=jnp.float32)
    partial_input = jnp.einsum(
        "td,cd->tc", grad_queries, w_query, preferred_element_type=jnp.float32
    )
    partial_input = partial_input + jnp.einsum(
        "td,cd->tc", grad_keys, w_key, preferred_element_type=jnp.float32
    )
    partial_input = partial_input + jnp.einsum(
        "td,cd->tc", grad_values, w_value, preferred_element_type=jnp.float32
    )
    grad_tokens = (lax.psum(partial_input, "head") + grad_attn).astype(jnp.bfloat16)
    partial_rel = mixed("tbd,cd->tbc", grad_key_rel, w_key) + mixed(
        "tbd,cd->tbc", grad_query_rel, w_query
    )
    grad_rel = lax.psum(partial_rel, ("batch", "head"))
    summed_weights = (
        lax.psum_scatter(grad_w_query, "batch", scatter_dimension=0, tiled=True),
        lax.psum_scatter(grad_w_key, "batch", scatter_dimension=0, tiled=True),
        lax.psum_scatter(grad_w_value, "batch", scatter_dimension=0, tiled=True),
        lax.psum_scatter(grad_w_output, "batch", scatter_dimension=1, tiled=True),
        lax.psum_scatter(grad_w_inner, "batch", scatter_dimension=0, tiled=True),
        lax.psum_scatter(grad_w_outer, "batch", scatter_dimension=1, tiled=True),
    )
    summed_small = lax.psum(
        (
            grad_b_output,
            grad_gain_attn,
            grad_shift_attn,
            grad_b_inner,
            grad_b_outer,
            grad_gain_ffn,
            grad_shift_ffn,
        ),
        "batch",
    )
    return (
        output,
        grad_tokens,
        summed_weights[0],
        summed_weights[1],
        summed_weights[2],
        summed_weights[3],
        summed_small[0],
        summed_small[1],
        summed_small[2],
        summed_weights[4],
        summed_small[3],
        summed_weights[5],
        summed_small[4],
        summed_small[5],
        summed_small[6],
        grad_rel,
    )


def solution(mesh):
    in_specs = (
        P("batch", None),
        P("batch"),
        P(None, "batch"),
        P(None, "head"),
        P(None, "head"),
        P(None, "head"),
        P("head", None),
        P(),
        P(),
        P(),
        P(None, "head"),
        P("head"),
        P("head", None),
        P(),
        P(),
        P(),
        P(),
        P("batch", None),
    )
    out_specs = (
        P("batch", None),
        P("batch", None),
        P("batch", "head"),
        P("batch", "head"),
        P("batch", "head"),
        P("head", "batch"),
        P(),
        P(),
        P(),
        P("batch", "head"),
        P("head"),
        P("head", "batch"),
        P(),
        P(),
        P(),
        P(),
    )
    return jax.shard_map(shards, mesh=mesh, in_specs=in_specs, out_specs=out_specs, check_vma=False)
```

profile of v0, /device:TPU:1, one launch (start us, length us, event | category | flops | bytes accessed | tf_op | source)
XLA Modules:
  0.0 2189.3 jit_solution(12772967095110467035)
XLA Ops:
  43.6 794.7 %while.41 = (s32[]{:T(128)}, f32[9,4,64,576]{3,2,0,1:T(8,128)}, f32[9,4,576,64]{2,1,3,0:T(4,128)}, s32[9,3,64,576]{3,1,2,0:T(4,128)}, f32[9,3,4,64,128]{4,2,1,3,...) while((s32[]{:T(128)}, f32[9,4,64,576]{3,2,0,1:T(8,128)}, f32[9,4,576,64]{2,1,3,0:T(4,128)}, ...), condition=%wide.region_1.2_spmd, body=%wide.region_0.1_spmd.sunk | while | flops 510689280 | bytes 8684649 | solution.py:69
  108.9 22.1 %fusion.242 = f32[9,4,576,64]{2,1,3,0:T(4,128)} fusion(f32[9,4,576,64]{2,1,3,0:T(4,128)} %get-tuple-element.398, s32[]{:T(128)S(6)} %copy.258, f32[64,576,4]{1,2,0:T(4,128)S(1)} %fusion.241, s32[3,64,576]{2,0,1:T(4,128)S(1)} %dynamic-slice_bitcast_fusion.4, f32[9,3,4,64,128]{4,2,1,3,0:T(4,128)} %get-tuple-element.408), kind=kOutput, calls=%fused_computation.15.clone.3 | convolution fusion | flops 127942656 | bytes 2081792 | tf_op jit(solution)/shard_map/while/body/eval_jaxpr/while/body/eval_jaxpr/thjb,tjib->hij/dot_general | solution.py:22
  197.1 22.1 %fusion.242 = f32[9,4,576,64]{2,1,3,0:T(4,128)} fusion(f32[9,4,576,64]{2,1,3,0:T(4,128)} %get-tuple-element.398, s32[]{:T(128)S(6)} %copy.258, f32[64,576,4]{1,2,0:T(4,128)S(1)} %fusion.241, s32[3,64,576]{2,0,1:T(4,128)S(1)} %dynamic-slice_bitcast_fusion.4, f32[9,3,4,64,128]{4,2,1,3,0:T(4,128)} %get-tuple-element.408), kind=kOutput, calls=%fused_computation.15.clone.3 | convolution fusion | flops 127942656 | bytes 2081792 | tf_op jit(solution)/shard_map/while/body/eval_jaxpr/while/body/eval_jaxpr/thjb,tjib->hij/dot_general | solution.py:22
  285.4 22.1 %fusion.242 = f32[9,4,576,64]{2,1,3,0:T(4,128)} fusion(f32[9,4,576,64]{2,1,3,0:T(4,128)} %get-tuple-element.398, s32[]{:T(128)S(6)} %copy.258, f32[64,576,4]{1,2,0:T(4,128)S(1)} %fusion.241, s32[3,64,576]{2,0,1:T(4,128)S(1)} %dynamic-slice_bitcast_fusion.4, f32[9,3,4,64,128]{4,2,1,3,0:T(4,128)} %get-tuple-element.408), kind=kOutput, calls=%fused_computation.15.clone.3 | convolution fusion | flops 127942656 | bytes 2081792 | tf_op jit(solution)/shard_map/while/body/eval_jaxpr/while/body/eval_jaxpr/thjb,tjib->hij/dot_general | solution.py:22
  373.7 22.1 %fusion.242 = f32[9,4,576,64]{2,1,3,0:T(4,128)} fusion(f32[9,4,576,64]{2,1,3,0:T(4,128)} %get-tuple-element.398, s32[]{:T(128)S(6)} %copy.258, f32[64,576,4]{1,2,0:T(4,128)S(1)} %fusion.241, s32[3,64,576]{2,0,1:T(4,128)S(1)} %dynamic-slice_bitcast_fusion.4, f32[9,3,4,64,128]{4,2,1,3,0:T(4,128)} %get-tuple-element.408), kind=kOutput, calls=%fused_computation.15.clone.3 | convolution fusion | flops 127942656 | bytes 2081792 | tf_op jit(solution)/shard_map/while/body/eval_jaxpr/while/body/eval_jaxpr/thjb,tjib->hij/dot_general | solution.py:22
  462.0 22.1 %fusion.242 = f32[9,4,576,64]{2,1,3,0:T(4,128)} fusion(f32[9,4,576,64]{2,1,3,0:T(4,128)} %get-tuple-element.398, s32[]{:T(128)S(6)} %copy.258, f32[64,576,4]{1,2,0:T(4,128)S(1)} %fusion.241, s32[3,64,576]{2,0,1:T(4,128)S(1)} %dynamic-slice_bitcast_fusion.4, f32[9,3,4,64,128]{4,2,1,3,0:T(4,128)} %get-tuple-element.408), kind=kOutput, calls=%fused_computation.15.clone.3 | convolution fusion | flops 127942656 | bytes 2081792 | tf_op jit(solution)/shard_map/while/body/eval_jaxpr/while/body/eval_jaxpr/thjb,tjib->hij/dot_general | solution.py:22
  550.3 22.1 %fusion.242 = f32[9,4,576,64]{2,1,3,0:T(4,128)} fusion(f32[9,4,576,64]{2,1,3,0:T(4,128)} %get-tuple-element.398, s32[]{:T(128)S(6)} %copy.258, f32[64,576,4]{1,2,0:T(4,128)S(1)} %fusion.241, s32[3,64,576]{2,0,1:T(4,128)S(1)} %dynamic-slice_bitcast_fusion.4, f32[9,3,4,64,128]{4,2,1,3,0:T(4,128)} %get-tuple-element.408), kind=kOutput, calls=%fused_computation.15.clone.3 | convolution fusion | flops 127942656 | bytes 2081792 | tf_op jit(solution)/shard_map/while/body/eval_jaxpr/while/body/eval_jaxpr/thjb,tjib->hij/dot_general | solution.py:22
  638.6 22.1 %fusion.242 = f32[9,4,576,64]{2,1,3,0:T(4,128)} fusion(f32[9,4,576,64]{2,1,3,0:T(4,128)} %get-tuple-element.398, s32[]{:T(128)S(6)} %copy.258, f32[64,576,4]{1,2,0:T(4,128)S(1)} %fusion.241, s32[3,64,576]{2,0,1:T(4,128)S(1)} %dynamic-slice_bitcast_fusion.4, f32[9,3,4,64,128]{4,2,1,3,0:T(4,128)} %get-tuple-element.408), kind=kOutput, calls=%fused_computation.15.clone.3 | convolution fusion | flops 127942656 | bytes 2081792 | tf_op jit(solution)/shard_map/while/body/eval_jaxpr/while/body/eval_jaxpr/thjb,tjib->hij/dot_general | solution.py:22
  726.9 22.1 %fusion.242 = f32[9,4,576,64]{2,1,3,0:T(4,128)} fusion(f32[9,4,576,64]{2,1,3,0:T(4,128)} %get-tuple-element.398, s32[]{:T(128)S(6)} %copy.258, f32[64,576,4]{1,2,0:T(4,128)S(1)} %fusion.241, s32[3,64,576]{2,0,1:T(4,128)S(1)} %dynamic-slice_bitcast_fusion.4, f32[9,3,4,64,128]{4,2,1,3,0:T(4,128)} %get-tuple-element.408), kind=kOutput, calls=%fused_computation.15.clone.3 | convolution fusion | flops 127942656 | bytes 2081792 | tf_op jit(solution)/shard_map/while/body/eval_jaxpr/while/body/eval_jaxpr/thjb,tjib->hij/dot_general | solution.py:22
  815.2 22.1 %fusion.242 = f32[9,4,576,64]{2,1,3,0:T(4,128)} fusion(f32[9,4,576,64]{2,1,3,0:T(4,128)} %get-tuple-element.398, s32[]{:T(128)S(6)} %copy.258, f32[64,576,4]{1,2,0:T(4,128)S(1)} %fusion.241, s32[3,64,576]{2,0,1:T(4,128)S(1)} %dynamic-slice_bitcast_fusion.4, f32[9,3,4,64,128]{4,2,1,3,0:T(4,128)} %get-tuple-element.408), kind=kOutput, calls=%fused_computation.15.clone.3 | convolution fusion | flops 127942656 | bytes 2081792 | tf_op jit(solution)/shard_map/while/body/eval_jaxpr/while/body/eval_jaxpr/thjb,tjib->hij/dot_general | solution.py:22
  863.8 97.4 %all-reduce.7.cloned.1.call-done = f32[576,1024]{1,0:T(8,128)} async-done(((f32[576,1024]{1,0:T(8,128)}), f32[576,1024]{1,0:T(8,128)}) %all-reduce.7.cloned.1.call-update) | async-done | bytes 2359312 | tf_op jit(solution)/shard_map/psum | solution.py:205
  976.0 94.8 %all-reduce.9.cloned.1.call-done = f32[576,1024]{1,0:T(8,128)} async-done(((f32[576,1024]{1,0:T(8,128)}), f32[576,1024]{1,0:T(8,128)}) %all-reduce.9.cloned.1.call-update) | async-done | bytes 2359312 | tf_op jit(solution)/shard_map/psum | solution.py:212
  1086.2 94.6 %all-reduce.11.cloned.1.call-done = f32[576,1024]{1,0:T(8,128)} async-done(((f32[576,1024]{1,0:T(8,128)}), f32[576,1024]{1,0:T(8,128)}) %all-reduce.11.cloned.1.call-update) | async-done | bytes 2359312 | tf_op jit(solution)/shard_map/psum | solution.py:231
  1210.5 463.7 %while.42 = (s32[]{:T(128)}, f32[9,3,4,64,128]{4,2,1,3,0:T(4,128)}, f32[9,3,4,64,128]{4,2,1,3,0:T(4,128)}, s32[9,3,64,576]{3,1,2,0:T(4,128)}, bf16[9,4,64,576]{3...) while((s32[]{:T(128)}, f32[9,3,4,64,128]{4,2,1,3,0:T(4,128)}, ...), condition=%wide.region_17.18_spmd, body=%wide.region_16.17_spmd.sunk | while | flops 254803968 | bytes 3769441 | solution.py:97
  1212.7 27.4 %fusion.244 = f32[9,3,4,64,128]{4,2,1,3,0:T(4,128)} fusion(f32[9,3,4,64,128]{4,2,1,3,0:T(4,128)} %get-tuple-element.418, s32[]{:T(128)S(6)} %copy.270, s32[3,64,576]{2,0,1:T(4,128)S(1)} %dynamic-slice_bitcast_fusion.5, bf16[1,4,64,576]{3,2,0,1:T(8,128)(2,1)S(1)} %constant_dynamic-slice_fusion.2), kind=kOutput, calls=%fused_computation.36.clone.2 | convolution fusion | flops 127401984 | bytes 1130500 | tf_op jit(solution)/shard_map/while/body/eval_jaxpr/while/body/eval_jaxpr/hij,tijb->thib/dot_general | solution.py:89
  1264.2 27.4 %fusion.244 = f32[9,3,4,64,128]{4,2,1,3,0:T(4,128)} fusion(f32[9,3,4,64,128]{4,2,1,3,0:T(4,128)} %get-tuple-element.418, s32[]{:T(128)S(6)} %copy.270, s32[3,64,576]{2,0,1:T(4,128)S(1)} %dynamic-slice_bitcast_fusion.5, bf16[1,4,64,576]{3,2,0,1:T(8,128)(2,1)S(1)} %constant_dynamic-slice_fusion.2), kind=kOutput, calls=%fused_computation.36.clone.2 | convolution fusion | flops 127401984 | bytes 1130500 | tf_op jit(solution)/shard_map/while/body/eval_jaxpr/while/body/eval_jaxpr/hij,tijb->thib/dot_general | solution.py:89
  1315.7 27.4 %fusion.244 = f32[9,3,4,64,128]{4,2,1,3,0:T(4,128)} fusion(f32[9,3,4,64,128]{4,2,1,3,0:T(4,128)} %get-tuple-element.418, s32[]{:T(128)S(6)} %copy.270, s32[3,64,576]{2,0,1:T(4,128)S(1)} %dynamic-slice_bitcast_fusion.5, bf16[1,4,64,576]{3,2,0,1:T(8,128)(2,1)S(1)} %constant_dynamic-slice_fusion.2), kind=kOutput, calls=%fused_computation.36.clone.2 | convolution fusion | flops 127401984 | bytes 1130500 | tf_op jit(solution)/shard_map/while/body/eval_jaxpr/while/body/eval_jaxpr/hij,tijb->thib/dot_general | solution.py:89
  1343.1 21.9 %fusion.245 = f32[9,3,4,64,128]{4,2,1,3,0:T(4,128)} fusion(f32[9,3,4,64,128]{4,2,1,3,0:T(4,128)} %get-tuple-element.419, s32[]{:T(128)S(6)} %copy.270, s32[3,64,576]{2,0,1:T(4,128)S(1)} %dynamic-slice_bitcast_fusion.5, bf16[9,4,576,64]{2,1,3,0:T(4,128)(2,1)} %get-tuple-element.429), kind=kOutput, calls=%fused_computation.38.clone.3 | convolution fusion | flops 127401984 | bytes 1164288 | tf_op jit(solution)/shard_map/while/body/eval_jaxpr/while/body/eval_jaxpr/hij,tjib->thjb/dot_general | solution.py:92
  1367.3 27.4 %fusion.244 = f32[9,3,4,64,128]{4,2,1,3,0:T(4,128)} fusion(f32[9,3,4,64,128]{4,2,1,3,0:T(4,128)} %get-tuple-element.418, s32[]{:T(128)S(6)} %copy.270, s32[3,64,576]{2,0,1:T(4,128)S(1)} %dynamic-slice_bitcast_fusion.5, bf16[1,4,64,576]{3,2,0,1:T(8,128)(2,1)S(1)} %constant_dynamic-slice_fusion.2), kind=kOutput, calls=%fused_computation.36.clone.2 | convolution fusion | flops 127401984 | bytes 1130500 | tf_op jit(solution)/shard_map/while/body/eval_jaxpr/while/body/eval_jaxpr/hij,tijb->thib/dot_general | solution.py:89
  1394.6 21.9 %fusion.245 = f32[9,3,4,64,128]{4,2,1,3,0:T(4,128)} fusion(f32[9,3,4,64,128]{4,2,1,3,0:T(4,128)} %get-tuple-element.419, s32[]{:T(128)S(6)} %copy.270, s32[3,64,576]{2,0,1:T(4,128)S(1)} %dynamic-slice_bitcast_fusion.5, bf16[9,4,576,64]{2,1,3,0:T(4,128)(2,1)} %get-tuple-element.429), kind=kOutput, calls=%fused_computation.38.clone.3 | convolution fusion | flops 127401984 | bytes 1164288 | tf_op jit(solution)/shard_map/while/body/eval_jaxpr/while/body/eval_jaxpr/hij,tjib->thjb/dot_general | solution.py:92
  1418.8 27.4 %fusion.244 = f32[9,3,4,64,128]{4,2,1,3,0:T(4,128)} fusion(f32[9,3,4,64,128]{4,2,1,3,0:T(4,128)} %get-tuple-element.418, s32[]{:T(128)S(6)} %copy.270, s32[3,64,576]{2,0,1:T(4,128)S(1)} %dynamic-slice_bitcast_fusion.5, bf16[1,4,64,576]{3,2,0,1:T(8,128)(2,1)S(1)} %constant_dynamic-slice_fusion.2), kind=kOutput, calls=%fused_computation.36.clone.2 | convolution fusion | flops 127401984 | bytes 1130500 | tf_op jit(solution)/shard_map/while/body/eval_jaxpr/while/body/eval_jaxpr/hij,tijb->thib/dot_general | solution.py:89
  1470.3 27.4 %fusion.244 = f32[9,3,4,64,128]{4,2,1,3,0:T(4,128)} fusion(f32[9,3,4,64,128]{4,2,1,3,0:T(4,128)} %get-tuple-element.418, s32[]{:T(128)S(6)} %copy.270, s32[3,64,576]{2,0,1:T(4,128)S(1)} %dynamic-slice_bitcast_fusion.5, bf16[1,4,64,576]{3,2,0,1:T(8,128)(2,1)S(1)} %constant_dynamic-slice_fusion.2), kind=kOutput, calls=%fused_computation.36.clone.2 | convolution fusion | flops 127401984 | bytes 1130500 | tf_op jit(solution)/shard_map/while/body/eval_jaxpr/while/body/eval_jaxpr/hij,tijb->thib/dot_general | solution.py:89
  1521.8 27.4 %fusion.244 = f32[9,3,4,64,128]{4,2,1,3,0:T(4,128)} fusion(f32[9,3,4,64,128]{4,2,1,3,0:T(4,128)} %get-tuple-element.418, s32[]{:T(128)S(6)} %copy.270, s32[3,64,576]{2,0,1:T(4,128)S(1)} %dynamic-slice_bitcast_fusion.5, bf16[1,4,64,576]{3,2,0,1:T(8,128)(2,1)S(1)} %constant_dynamic-slice_fusion.2), kind=kOutput, calls=%fused_computation.36.clone.2 | convolution fusion | flops 127401984 | bytes 1130500 | tf_op jit(solution)/shard_map/while/body/eval_jaxpr/while/body/eval_jaxpr/hij,tijb->thib/dot_general | solution.py:89
  1573.3 27.4 %fusion.244 = f32[9,3,4,64,128]{4,2,1,3,0:T(4,128)} fusion(f32[9,3,4,64,128]{4,2,1,3,0:T(4,128)} %get-tuple-element.418, s32[]{:T(128)S(6)} %copy.270, s32[3,64,576]{2,0,1:T(4,128)S(1)} %dynamic-slice_bitcast_fusion.5, bf16[1,4,64,576]{3,2,0,1:T(8,128)(2,1)S(1)} %constant_dynamic-slice_fusion.2), kind=kOutput, calls=%fused_computation.36.clone.2 | convolution fusion | flops 127401984 | bytes 1130500 | tf_op jit(solution)/shard_map/while/body/eval_jaxpr/while/body/eval_jaxpr/hij,tijb->thib/dot_general | solution.py:89
  1624.9 27.4 %fusion.244 = f32[9,3,4,64,128]{4,2,1,3,0:T(4,128)} fusion(f32[9,3,4,64,128]{4,2,1,3,0:T(4,128)} %get-tuple-element.418, s32[]{:T(128)S(6)} %copy.270, s32[3,64,576]{2,0,1:T(4,128)S(1)} %dynamic-slice_bitcast_fusion.5, bf16[1,4,64,576]{3,2,0,1:T(8,128)(2,1)S(1)} %constant_dynamic-slice_fusion.2), kind=kOutput, calls=%fused_computation.36.clone.2 | convolution fusion | flops 127401984 | bytes 1130500 | tf_op jit(solution)/shard_map/while/body/eval_jaxpr/while/body/eval_jaxpr/hij,tijb->thib/dot_general | solution.py:89
  1732.6 22.1 %all-reduce = (f32[1024]{0:T(1024)}, f32[1024]{0:T(1024)}, f32[1024]{0:T(1024)}, f32[1024]{0:T(1024)}, f32[1024]{0:T(1024)}, /*index=5*/f32[1024]{0:T(1024)}, f32[1024]{0:T(1024)}) all-reduce(f32[1024]{0:T(1024)S(1)} %copy-done.60, f32[1024]{0:T(1024)S(1)} %copy-done.57, ...), channel_id=1, replica_groups=mesh['batch'=8,'head'=4] {'batch'}, use_global_device_ids=true, to_apply=%region_24.25 | all-reduce | flops 7168 | bytes 57344 | tf_op jit(solution)/shard_map/psum | solution.py:325
  1758.0 37.0 %reduce-scatter.9.cloned.1.call-done = f32[128,256]{0,1:T(8,128)} async-done(((f32[1024,256]{0,1:T(8,128)}), f32[128,256]{0,1:T(8,128)}) %reduce-scatter.9.cloned.1.call-update) | async-done | bytes 131088 | tf_op jit(solution)/shard_map/reduce_scatter | solution.py:319
  1796.7 96.4 %all-reduce.13.cloned.1.call-done = f32[576,1024]{1,0:T(8,128)} async-done(((f32[576,1024]{1,0:T(8,128)}), f32[576,1024]{1,0:T(8,128)}) %all-reduce.13.cloned.1.call-update) | async-done | bytes 2359312 | tf_op jit(solution)/shard_map/psum | solution.py:312
  1896.9 132.3 %all-reduce.15.cloned.1.call-done = f32[3,128,1024]{2,1,0:T(8,128)} async-done(((f32[3,128,1024]{2,1,0:T(8,128)}), f32[3,128,1024]{2,1,0:T(8,128)}) %all-reduce.15.cloned.1.call-update) | async-done | bytes 1572880 | tf_op jit(solution)/shard_map/psum | solution.py:316
  2029.2 39.5 %reduce-scatter.13.cloned.1.call-done = f32[256,128]{1,0:T(8,128)} async-done(((f32[256,1024]{1,0:T(8,128)}), f32[256,128]{1,0:T(8,128)}) %reduce-scatter.13.cloned.1.call-update) | async-done | bytes 131088 | tf_op jit(solution)/shard_map/reduce_scatter | solution.py:321
  2068.7 55.2 %reduce-scatter.15.cloned.1.call-done = f32[128,1024]{1,0:T(8,128)} async-done(((f32[1024,1024]{1,0:T(8,128)}), f32[128,1024]{1,0:T(8,128)}) %reduce-scatter.15.cloned.1.call-update) | async-done | bytes 524304 | tf_op jit(solution)/shard_map/reduce_scatter | solution.py:322
  2123.9 55.7 %reduce-scatter.17.cloned.1.call-done = f32[1024,128]{1,0:T(8,128)} async-done(((f32[1024,1024]{1,0:T(8,128)}), f32[1024,128]{1,0:T(8,128)}) %reduce-scatter.17.cloned.1.call-update) | async-done | bytes 524304 | tf_op jit(solution)/shard_map/reduce_scatter | solution.py:323
  (357 shorter events, 959.1 us)
Async XLA Ops:
  7.2 956.5 %copy-start = (bf16[1024,1024]{1,0:T(8,128)(2,1)S(1)}, bf16[1024,1024]{1,0:T(8,128)(2,1)}, u32[]{:S(2)}) copy-start(bf16[1024,1024]{1,0:T(8,128)(2,1)} %param.32) | copy-start | bytes 6291460
  7.2 4.9 copy-start.12
  7.2 954.0 %all-reduce.7.cloned.1.call-start = ((), (), s32[]{:S(2)}) async-start(), calls=%async_computation.6 | async-start | bytes 4718592 | tf_op jit(solution)/shard_map/psum | solution.py:205
  7.3 4.9 copy-start.26
  7.3 6.0 copy-start.24
  17.0 16.9 copy-start.38
  24.1 10.5 copy-start.17
  25.3 8.5 copy-start.20
  844.2 6.5 copy-start.18
  844.2 6.5 copy-start.21
  844.2 6.5 copy-start.71
  861.5 99.7 %copy-start.13 = (bf16[576,1024]{1,0:T(8,128)(2,1)S(1)}, bf16[576,1024]{1,0:T(8,128)(2,1)}, u32[]{:S(2)}) copy-start(bf16[576,1024]{1,0:T(8,128)(2,1)} %param.22) | copy-start | bytes 3538948
  861.5 99.7 %copy-start.70 = (f32[1024]{0:T(1024)S(1)}, f32[1024]{0:T(1024)}, u32[]{:S(2)}) copy-start(f32[1024]{0:T(1024)} %param.29) | copy-start | bytes 12292
  863.4 207.4 %all-reduce.9.cloned.1.call-start = ((), (), s32[]{:S(2)}) async-start(), calls=%async_computation.7 | async-start | bytes 4718592 | tf_op jit(solution)/shard_map/psum | solution.py:212
  963.3 8.9 copy-start.4
  964.1 221.7 %copy-start.53 = (f32[576]{0:T(1024)}, f32[576]{0:T(1024)S(1)}, u32[]{:S(2)}) copy-start(f32[576]{0:T(1024)S(1)} %add_rsqrt_fusion.1) | copy-start | bytes 6916
  964.1 9.1 copy-start.72
  975.9 94.8 %copy-start.65 = (f32[1024]{0:T(1024)S(1)}, f32[1024]{0:T(1024)}, u32[]{:S(2)}) copy-start(f32[1024]{0:T(1024)} %param.35) | copy-start | bytes 12292
  976.0 204.8 %all-reduce.11.cloned.1.call-start = ((), (), s32[]{:S(2)}) async-start(), calls=%async_computation.8 | async-start | bytes 4718592 | tf_op jit(solution)/shard_map/psum | solution.py:231
  1085.9 668.8 %reduce-scatter.11.cloned.1.call-start = ((), (), s32[]{:S(2)}) async-start(), calls=%async_computation.12 | async-start | bytes 1179648 | tf_op jit(solution)/shard_map/reduce_scatter | solution.py:320
  1180.7 5.1 copy-start.5
  1189.3 3.9 copy-start.32
  1189.3 8.0 slice-start
  1193.1 4.2 slice-start.1
  1681.7 74.7 %reduce-scatter.7.cloned.1.call-start = ((), (), s32[]{:S(2)}) async-start(), calls=%async_computation.10 | async-start | bytes 1179648 | tf_op jit(solution)/shard_map/reduce_scatter | solution.py:318
  1696.3 98.8 %reduce-scatter.9.cloned.1.call-start = ((), (), s32[]{:S(2)}) async-start(), calls=%async_computation.11 | async-start | bytes 1179648 | tf_op jit(solution)/shard_map/reduce_scatter | solution.py:319
  1696.4 4.4 copy-start.47
  1706.5 186.7 %all-reduce.13.cloned.1.call-start = ((), (), s32[]{:S(2)}) async-start(), calls=%async_computation.9 | async-start | bytes 4718592 | tf_op jit(solution)/shard_map/psum | solution.py:312
  1711.3 317.9 %all-reduce.15.cloned.1.call-start = ((), (), s32[]{:S(2)}) async-start(), calls=%async_computation.16 | async-start | bytes 3145728 | tf_op jit(solution)/shard_map/psum | solution.py:316
  1715.2 353.5 %reduce-scatter.13.cloned.1.call-start = ((), (), s32[]{:S(2)}) async-start(), calls=%async_computation.13 | async-start | bytes 1179648 | tf_op jit(solution)/shard_map/reduce_scatter | solution.py:321
  1718.5 405.4 %reduce-scatter.15.cloned.1.call-start = ((), (), s32[]{:S(2)}) async-start(), calls=%async_computation.14 | async-start | bytes 4718592 | tf_op jit(solution)/shard_map/reduce_scatter | solution.py:322
  1724.9 454.7 %reduce-scatter.17.cloned.1.call-start = ((), (), s32[]{:S(2)}) async-start(), calls=%async_computation.15 | async-start | bytes 4718592 | tf_op jit(solution)/shard_map/reduce_scatter | solution.py:323
  (61 other events, 113.9 us)
Sparse Core Ops, SparseCore 0:
  863.5 97.6 all-reduce.6
  976.1 94.6 all-reduce.8
  1086.0 94.6 all-reduce.10
  1681.8 34.9 reduce-scatter.10
  1719.8 36.1 reduce-scatter.6
  1759.0 35.9 reduce-scatter.8
  1797.4 95.6 all-reduce.12
  1899.0 130.1 all-reduce.14
  2033.0 35.6 reduce-scatter.12
  2072.5 51.4 reduce-scatter.14
  2128.2 51.3 reduce-scatter.16
where the time goes:
time: 2200 us; the launch traced here: 2190 us
  matrix products  1300 us (59%)
  waiting for transfers between devices  703 us (32%)
  local copies, waits for them, and re-layouts  108 us (5%)
  other arithmetic  34.2 us (2%)
  blocking collectives  22.1 us (1%)
    dot_general x26, matrix products, mixed(): jnp.einsum(form, lower, narrow, preferred_element_type=jnp.float32)  398 us
    dot_general x26, matrix products, mixed(): jnp.einsum(form, upper, narrow, preferred_element_type=jnp.float32)  392 us
    dot_general x9, matrix products, one_block(): jnp.einsum('hij,tijb->thib', row_block, onehot, preferred_element_type=jn...  246 us
    dot_general x9, matrix products, one_block(): jnp.einsum('hij,tjib->thjb', col_block, onehot, preferred_element_type=jn...  197 us
    psum x1, waiting for transfers between devices, shards(): grad_rel = lax.psum(partial_rel, ('batch', 'head'))  132 us
    psum x1, waiting for transfers between devices, shards(): attention_total = lax.psum(partial_attn, 'head')  97.4 us
    psum x1, waiting for transfers between devices, shards(): lax.psum(partial_input, 'head') + grad_attn  96.4 us
    psum x1, waiting for transfers between devices, shards(): ffn_total = lax.psum(partial_ffn, 'head')  94.8 us
  transfers between devices with their start and end apart: 11, of which 9 were waited for; matrix products, arithmetic and copies ran while one was open for 2% of the time, Pallas kernels for 0%

commit v1 on v0

v1 whole, which is shorter than its diff:
```python
import functools

import jax
import jax.numpy as jnp
from jax import lax
from jax.experimental import pallas as pl
from jax.experimental.pallas import tpu as pltpu
from jax.sharding import PartitionSpec as P

HEAD = 64
NB = 128
BOX_STEP = 8
NEG_FILL = -1000000000.0
LANES = 128
VMEM_LIMIT = 60 * 1024 * 1024


def dot_nn(a, b):
    return lax.dot_general(a, b, (((1,), (0,)), ((), ())), preferred_element_type=jnp.float32)


def dot_nt(a, b):
    return lax.dot_general(a, b, (((1,), (1,)), ((), ())), preferred_element_type=jnp.float32)


def dot_tn(a, b):
    return lax.dot_general(a, b, (((0,), (0,)), ((), ())), preferred_element_type=jnp.float32)


def lane_gather(table, index):
    return jnp.take_along_axis(table, index, axis=1, mode="promise_in_bounds")


def attention_forward_kernel(
    length_ref, tok_ref, wq_ref, wk_ref, wv_ref, rel_ref, col_ref, row_ref, wo_ref,
    q_ref, k_ref, v_ref, krel_ref, qrel_ref, attend_ref, ctx_ref, part_ref,
    idx_ref, log_ref, col_part_ref, tq_ref, tk_ref, kv_ref,
):
    slots = tok_ref.shape[0]
    wide = row_ref.shape[1]
    heads = wq_ref.shape[1] // HEAD
    chunks = wide // LANES
    scale = (7.0 * HEAD) ** (-0.5)
    tok = tok_ref[...]
    q_ref[...] = dot_nn(tok, wq_ref[...]).astype(jnp.bfloat16)
    k_ref[...] = dot_nn(tok, wk_ref[...]).astype(jnp.bfloat16)
    v_ref[...] = dot_nn(tok, wv_ref[...]).astype(jnp.bfloat16)
    rel = rel_ref[...]
    krel_ref[...] = dot_nn(rel, wk_ref[...]).astype(jnp.bfloat16)
    qrel_ref[...] = dot_nn(rel, wq_ref[...]).astype(jnp.bfloat16)
    kv_ref[...] = jnp.zeros_like(kv_ref)
    kv_ref[0, :slots, :] = k_ref[...]
    kv_ref[1, :slots, :] = v_ref[...]
    if wide > slots:
        col_part_ref[slots:, :] = jnp.zeros((wide - slots, wide), jnp.float32)

    block = 32
    length = length_ref[0]

    @pl.loop(0, slots // block)
    def _(step):
        at = pl.ds(pl.multiple_of(step * block, block), block)
        for kind in range(2):
            own = col_ref[at, kind : kind + 1]
            other = row_ref[kind : kind + 1, :]
            bucket = jnp.clip((own - other) >> 3, -(NB // 2), NB // 2 - 1) + NB // 2
            idx_ref[kind, at, :] = bucket

    for head in range(heads):
        cols = slice(head * HEAD, (head + 1) * HEAD)
        q_h = q_ref[:, cols]
        tq_ref[...] = dot_nt(q_h, krel_ref[:, cols])
        tk_ref[...] = dot_nt(k_ref[:, cols], qrel_ref[:, cols])
        log_ref[...] = dot_nt(q_h, kv_ref[0, :, cols])

        for big in range(chunks):
            rows_here = min(LANES, slots - big * LANES)

            @pl.loop(0, rows_here // block)
            def _(step, big=big):
                start = pl.multiple_of(big * LANES + step * block, block)
                at = pl.ds(start, block)
                tq = [tq_ref[at, t * NB : (t + 1) * NB] for t in range(3)]
                tk = [tk_ref[at, t * NB : (t + 1) * NB] for t in range(3)]
                for chunk in range(chunks):
                    lanes = slice(chunk * LANES, (chunk + 1) * LANES)
                    if big - chunk >= 2:
                        far = NB - 1
                        s1, s2 = tq[0][:, far : far + 1], tk[0][:, far : far + 1]
                    elif chunk - big >= 2:
                        s1, s2 = tq[0][:, 0:1], tk[0][:, 0:1]
                    else:
                        i_at = lax.broadcasted_iota(jnp.int32, (block, LANES), 0) + start
                        j_at = lax.broadcasted_iota(jnp.int32, (block, LANES), 1) + chunk * LANES
                        near = jnp.clip(i_at - j_at, -(NB // 2), NB // 2 - 1) + NB // 2
                        s1, s2 = lane_gather(tq[0], near), lane_gather(tk[0], near)
                    for kind in range(2):
                        index = idx_ref[kind, at, lanes]
                        s1 = s1 + lane_gather(tq[kind + 1], index)
                        s2 = s2 + lane_gather(tk[kind + 1], index)
                    log_ref[at, lanes] += s1
                    col_part_ref[at, lanes] = s2

        for big in range(chunks):
            rows_here = min(LANES, slots - big * LANES)
            at = slice(big * LANES, big * LANES + rows_here)
            for chunk in range(chunks):
                lanes = slice(chunk * LANES, (chunk + 1) * LANES)
                turned = col_part_ref[lanes, big * LANES : (big + 1) * LANES].T
                log_ref[at, lanes] += turned[:rows_here]

        @pl.loop(0, slots // block)
        def _(step, head=head):
            at = pl.ds(pl.multiple_of(step * block, block), block)
            j_at = lax.broadcasted_iota(jnp.int32, (block, wide), 1)
            masked = jnp.where(j_at < length, log_ref[at, :] * scale, NEG_FILL)
            peak = jnp.max(masked, axis=-1, keepdims=True)
            grown = jnp.exp(masked - peak)
            total = jnp.sum(grown, axis=-1, keepdims=True)
            attend_ref[head, at, :] = (grown / total).astype(jnp.bfloat16)

        ctx_ref[:, cols] = dot_nn(attend_ref[head], kv_ref[1, :, cols]).astype(jnp.bfloat16)
    part_ref[...] = dot_nn(ctx_ref[...], wo_ref[...])


def attention_forward(tokens, length, corner_col, corner_row, w_query, w_key, w_value, rel, w_output):
    slots, width = tokens.shape
    mine = w_query.shape[1]
    heads = mine // HEAD
    wide = corner_row.shape[1]
    low = jnp.bfloat16
    vmem = pl.BlockSpec(memory_space=pltpu.VMEM)
    return pl.pallas_call(
        attention_forward_kernel,
        out_shape=(
            jax.ShapeDtypeStruct((slots, mine), low),
            jax.ShapeDtypeStruct((slots, mine), low),
            jax.ShapeDtypeStruct((slots, mine), low),
            jax.ShapeDtypeStruct((3 * NB, mine), low),
            jax.ShapeDtypeStruct((3 * NB, mine), low),
            jax.ShapeDtypeStruct((heads, slots, wide), low),
            jax.ShapeDtypeStruct((slots, mine), low),
            jax.ShapeDtypeStruct((slots, width), jnp.float32),
        ),
        in_specs=[pl.BlockSpec(memory_space=pltpu.SMEM)] + [vmem] * 8,
        out_specs=(vmem,) * 8,
        scratch_shapes=[
            pltpu.VMEM((2, slots, wide), jnp.int32),
            pltpu.VMEM((slots, wide), jnp.float32),
            pltpu.VMEM((wide, wide), jnp.float32),
            pltpu.VMEM((slots, 3 * NB), jnp.float32),
            pltpu.VMEM((slots, 3 * NB), jnp.float32),
            pltpu.VMEM((2, wide, mine), low),
        ],
        compiler_params=pltpu.CompilerParams(vmem_limit_bytes=VMEM_LIMIT),
        name="attention_forward",
    )(length, tokens, w_query, w_key, w_value, rel, corner_col, corner_row, w_output)
def attention_backward_kernel(
    grad_ref, tok_ref, wq_ref, wk_ref, wv_ref, wo_ref, rel_ref, col_ref,
    q_ref, k_ref, v_ref, krel_ref, qrel_ref, attend_ref, ctx_ref,
    gwq_ref, gwk_ref, gwv_ref, gwo_ref, gin_ref, grel_ref,
    gc_ref, step_ref, kv_ref, mat_ref, fold_ref, hist_ref, gq_ref, gk_ref, gv_ref,
    gkrel_ref, gqrel_ref,
):
    slots = tok_ref.shape[0]
    wide = mat_ref.shape[1]
    heads = wq_ref.shape[1] // HEAD
    chunks = wide // LANES
    scale = (7.0 * HEAD) ** (-0.5)
    low = jnp.bfloat16
    block = 32
    gc_ref[...] = dot_nt(grad_ref[...], wo_ref[...]).astype(low)
    gwo_ref[...] = dot_tn(ctx_ref[...], grad_ref[...])
    kv_ref[...] = jnp.zeros_like(kv_ref)
    kv_ref[0, :slots, :] = k_ref[...]
    kv_ref[1, :slots, :] = v_ref[...]
    mat_ref[...] = jnp.zeros_like(mat_ref)
    step_ref[...] = jnp.zeros_like(step_ref)

    @pl.loop(0, slots // block)
    def _(step):
        at = pl.ds(pl.multiple_of(step * block, block), block)
        quotient = lax.broadcasted_iota(jnp.int32, (block, NB), 1) * BOX_STEP
        for kind in range(2):
            own = col_ref[at, kind : kind + 1]
            for rest in range(BOX_STEP):
                lanes = slice(rest * NB, (rest + 1) * NB)
                step_ref[kind, at, lanes] = (own <= quotient + rest).astype(jnp.float32).astype(low)

    for head in range(heads):
        cols = slice(head * HEAD, (head + 1) * HEAD)
        gc_h = gc_ref[:, cols]
        grad_attend = dot_nt(gc_h, kv_ref[1, :, cols])
        mean = jnp.sum(gc_h.astype(jnp.float32) * ctx_ref[:, cols].astype(jnp.float32), axis=-1, keepdims=True)
        mat_ref[0, :slots, :] = (attend_ref[head].astype(jnp.float32) * (grad_attend - mean)).astype(low)
        gv_ref[:, cols] = dot_tn(attend_ref[head], gc_h)[:slots].astype(low)
        for big in range(chunks):
            for chunk in range(chunks):
                here = slice(big * LANES, (big + 1) * LANES)
                there = slice(chunk * LANES, (chunk + 1) * LANES)
                mat_ref[1, there, here] = mat_ref[0, here, there].T

        for side in range(2):
            for kind in range(2):
                fold_ref[kind] = dot_nn(mat_ref[side, :slots, :], step_ref[kind])

            for big in range(chunks):
                rows_here = min(LANES, slots - big * LANES)

                @pl.loop(0, rows_here // block)
                def _(step, big=big, side=side):
                    local = step * block
                    at = pl.ds(pl.multiple_of(big * LANES + local, block), block)
                    lane = lax.broadcasted_iota(jnp.int32, (block, NB), 1)
                    row = lax.broadcasted_iota(jnp.int32, (block, NB), 0) + local
                    part = [
                        mat_ref[side, at, c * LANES : (c + 1) * LANES].astype(jnp.float32)
                        for c in range(chunks)
                    ]
                    zero = jnp.zeros((block, LANES), jnp.float32)
                    before = part[big - 1] if big >= 1 else zero
                    after = part[big + 1] if big + 1 < chunks else zero
                    mid = part[big]
                    delta = lane - row
                    window = jnp.where(
                        delta > NB // 2, before, jnp.where(delta < 1 - NB // 2, after, mid)
                    )
                    spread = lane_gather(window, (row + NB // 2 - lane) & (NB - 1))
                    under = jnp.where(delta <= NB // 2 + 1, before, 0.0) + jnp.where(
                        delta <= 1 - NB // 2, mid, 0.0
                    )
                    over = jnp.where(delta >= NB // 2, mid, 0.0) + jnp.where(
                        delta >= -(NB // 2), after, 0.0
                    )
                    for c in range(big - 1):
                        under = under + part[c]
                    for c in range(big + 2, chunks):
                        over = over + part[c]
                    under = jnp.sum(under, axis=-1, keepdims=True)
                    over = jnp.sum(over, axis=-1, keepdims=True)
                    spread = jnp.where(lane == 0, over, jnp.where(lane == NB - 1, under, spread))
                    hist_ref[side, at, 0:NB] = spread.astype(low)
                    for kind in range(2):
                        own = col_ref[at, kind : kind + 1]
                        rest = jnp.broadcast_to(own & (BOX_STEP - 1), (block, NB))
                        whole = jnp.broadcast_to(own >> 3, (block, NB))
                        groups = [
                            fold_ref[kind, at, r * NB : (r + 1) * NB] for r in range(BOX_STEP)
                        ]
                        every = groups[-1][:, NB - 1 : NB]
                        for bit in range(3):
                            odd = (rest & (1 << bit)) != 0
                            groups = [
                                jnp.where(odd, groups[g + 1], groups[g])
                                for g in range(0, len(groups), 2)
                            ]
                        index = whole + NB // 2 - lane
                        found = lane_gather(groups[0], index & (NB - 1))
                        found = jnp.where(index < 0, 0.0, found)
                        found = jnp.where((index >= NB) | (lane == 0), every, found)
                        following = pltpu.roll(found, NB - 1, 1)
                        found = found - jnp.where(lane == NB - 1, 0.0, following)
                        hist_ref[side, at, (kind + 1) * NB : (kind + 2) * NB] = found.astype(low)

        q_h, k_h = q_ref[:, cols], k_ref[:, cols]
        gq = dot_nn(mat_ref[0, :slots, :], kv_ref[0, :, cols]) + dot_nn(hist_ref[0], krel_ref[:, cols])
        gk = dot_nn(mat_ref[1, :slots, :slots], q_h) + dot_nn(hist_ref[1], qrel_ref[:, cols])
        gq_ref[:, cols] = (gq * scale).astype(low)
        gk_ref[:, cols] = (gk * scale).astype(low)
        gkrel_ref[:, cols] = (dot_tn(hist_ref[0], q_h) * scale).astype(low)
        gqrel_ref[:, cols] = (dot_tn(hist_ref[1], k_h) * scale).astype(low)

    tok, rel = tok_ref[...], rel_ref[...]
    gwq_ref[...] = dot_tn(tok, gq_ref[...]) + dot_tn(rel, gqrel_ref[...])
    gwk_ref[...] = dot_tn(tok, gk_ref[...]) + dot_tn(rel, gkrel_ref[...])
    gwv_ref[...] = dot_tn(tok, gv_ref[...])
    gin_ref[...] = (
        dot_nt(gq_ref[...], wq_ref[...])
        + dot_nt(gk_ref[...], wk_ref[...])
        + dot_nt(gv_ref[...], wv_ref[...])
    )
    grel_ref[...] = dot_nt(gkrel_ref[...], wk_ref[...]) + dot_nt(gqrel_ref[...], wq_ref[...])


def attention_backward(
    grad, tokens, w_query, w_key, w_value, w_output, rel, corner_col, q, k, v, krel, qrel, attend, ctx
):
    slots, width = tokens.shape
    mine = w_query.shape[1]
    wide = attend.shape[2]
    low, full = jnp.bfloat16, jnp.float32
    vmem = pl.BlockSpec(memory_space=pltpu.VMEM)
    return pl.pallas_call(
        attention_backward_kernel,
        out_shape=(
            jax.ShapeDtypeStruct((width, mine), full),
            jax.ShapeDtypeStruct((width, mine), full),
            jax.ShapeDtypeStruct((width, mine), full),
            jax.ShapeDtypeStruct((mine, width), full),
            jax.ShapeDtypeStruct((slots, width), full),
            jax.ShapeDtypeStruct((3 * NB, width), full),
        ),
        in_specs=[vmem] * 15,
        out_specs=(vmem,) * 6,
        scratch_shapes=[
            pltpu.VMEM((slots, mine), low),
            pltpu.VMEM((2, wide, BOX_STEP * NB), low),
            pltpu.VMEM((2, wide, mine), low),
            pltpu.VMEM((2, wide, wide), low),
            pltpu.VMEM((2, slots, BOX_STEP * NB), full),
            pltpu.VMEM((2, slots, 3 * NB), low),
            pltpu.VMEM((slots, mine), low),
            pltpu.VMEM((slots, mine), low),
            pltpu.VMEM((slots, mine), low),
            pltpu.VMEM((3 * NB, mine), low),
            pltpu.VMEM((3 * NB, mine), low),
        ],
        compiler_params=pltpu.CompilerParams(vmem_limit_bytes=VMEM_LIMIT),
        name="attention_backward",
    )(grad, tokens, w_query, w_key, w_value, w_output, rel, corner_col, q, k, v, krel, qrel, attend, ctx)


def layer_stats(values):
    average = jnp.mean(values, axis=-1, keepdims=True)
    centered = values - average
    spread_squared = jnp.mean(centered * centered, axis=-1, keepdims=True)
    scaling = lax.rsqrt(spread_squared + 1e-05)
    return (centered * scaling, scaling)


def norm_back(upstream, normed, scaling, gain_in):
    scaled = upstream * gain_in
    inward = scaling * (
        scaled
        - jnp.mean(scaled, axis=-1, keepdims=True)
        - normed * jnp.mean(scaled * normed, axis=-1, keepdims=True)
    )
    return (inward, jnp.sum(upstream * normed, axis=0), jnp.sum(upstream, axis=0))


def shards(
    tokens,
    page_lengths,
    corners,
    w_query,
    w_key,
    w_value,
    w_output,
    b_output,
    gain_attn,
    shift_attn,
    w_inner,
    b_inner,
    w_outer,
    b_outer,
    gain_ffn,
    shift_ffn,
    rel_tables,
    cotangent,
):
    slots_page = tokens.shape[0]
    wide = -(-slots_page // LANES) * LANES
    rel_rows = rel_tables.reshape(3 * NB, rel_tables.shape[2])
    corner_col = corners.T
    corner_row = jnp.pad(corners, ((0, 0), (0, wide - slots_page)))
    kept = attention_forward(
        tokens, page_lengths, corner_col, corner_row, w_query, w_key, w_value, rel_rows, w_output
    )
    partial_attn = kept[7]
    token_float = tokens.astype(jnp.float32)
    attention_total = lax.psum(partial_attn, "head")
    normed_one, scale_one = layer_stats(attention_total + b_output + token_float)
    hidden_one = normed_one * gain_attn + shift_attn
    hidden_low = hidden_one.astype(jnp.bfloat16)
    inner_pre = jnp.dot(hidden_low, w_inner, preferred_element_type=jnp.float32) + b_inner
    active = jax.nn.gelu(inner_pre, approximate=False).astype(jnp.bfloat16)
    partial_ffn = jnp.dot(active, w_outer, preferred_element_type=jnp.float32)
    ffn_total = lax.psum(partial_ffn, "head")
    normed_two, scale_two = layer_stats(ffn_total + b_outer + hidden_one)
    output = (normed_two * gain_ffn + shift_ffn).astype(jnp.bfloat16)
    grad_out = cotangent.astype(jnp.float32)
    grad_mid, grad_gain_ffn, grad_shift_ffn = norm_back(grad_out, normed_two, scale_two, gain_ffn)
    grad_b_outer = jnp.sum(grad_mid, axis=0)
    grad_mid_low = grad_mid.astype(jnp.bfloat16)
    grad_w_outer = jnp.einsum("tf,td->fd", active, grad_mid_low, preferred_element_type=jnp.float32)
    grad_active = jnp.einsum("td,fd->tf", grad_mid_low, w_outer, preferred_element_type=jnp.float32)
    _, gelu_pull = jax.vjp(lambda pre_value: jax.nn.gelu(pre_value, approximate=False), inner_pre)
    grad_inner = gelu_pull(grad_active)[0]
    grad_b_inner = jnp.sum(grad_inner, axis=0)
    grad_inner_low = grad_inner.astype(jnp.bfloat16)
    grad_w_inner = jnp.einsum(
        "td,tf->df", hidden_low, grad_inner_low, preferred_element_type=jnp.float32
    )
    partial_hidden = jnp.einsum(
        "tf,df->td", grad_inner_low, w_inner, preferred_element_type=jnp.float32
    )
    grad_hidden = lax.psum(partial_hidden, "head") + grad_mid
    grad_attn, grad_gain_attn, grad_shift_attn = norm_back(
        grad_hidden, normed_one, scale_one, gain_attn
    )
    grad_b_output = jnp.sum(grad_attn, axis=0)
    grad_attn_low = grad_attn.astype(jnp.bfloat16)
    grad_w_query, grad_w_key, grad_w_value, grad_w_output, partial_input, partial_rel = (
        attention_backward(
            grad_attn_low, tokens, w_query, w_key, w_value, w_output, rel_rows, corner_col, *kept[:7]
        )
    )
    grad_tokens = (lax.psum(partial_input, "head") + grad_attn).astype(jnp.bfloat16)
    grad_rel = lax.psum(partial_rel, ("batch", "head")).reshape(rel_tables.shape)
    summed_weights = (
        lax.psum_scatter(grad_w_query, "batch", scatter_dimension=0, tiled=True),
        lax.psum_scatter(grad_w_key, "batch", scatter_dimension=0, tiled=True),
        lax.psum_scatter(grad_w_value, "batch", scatter_dimension=0, tiled=True),
        lax.psum_scatter(grad_w_output, "batch", scatter_dimension=1, tiled=True),
        lax.psum_scatter(grad_w_inner, "batch", scatter_dimension=0, tiled=True),
        lax.psum_scatter(grad_w_outer, "batch", scatter_dimension=1, tiled=True),
    )
    summed_small = lax.psum(
        (
            grad_b_output,
            grad_gain_attn,
            grad_shift_attn,
            grad_b_inner,
            grad_b_outer,
            grad_gain_ffn,
            grad_shift_ffn,
        ),
        "batch",
    )
    return (
        output,
        grad_tokens,
        summed_weights[0],
        summed_weights[1],
        summed_weights[2],
        summed_weights[3],
        summed_small[0],
        summed_small[1],
        summed_small[2],
        summed_weights[4],
        summed_small[3],
        summed_weights[5],
        summed_small[4],
        summed_small[5],
        summed_small[6],
        grad_rel,
    )


def solution(mesh):
    in_specs = (
        P("batch", None),
        P("batch"),
        P(None, "batch"),
        P(None, "head"),
        P(None, "head"),
        P(None, "head"),
        P("head", None),
        P(),
        P(),
        P(),
        P(None, "head"),
        P("head"),
        P("head", None),
        P(),
        P(),
        P(),
        P(),
        P("batch", None),
    )
    out_specs = (
        P("batch", None),
        P("batch", None),
        P("batch", "head"),
        P("batch", "head"),
        P("batch", "head"),
        P("head", "batch"),
        P(),
        P(),
        P(),
        P("batch", "head"),
        P("head"),
        P("head", "batch"),
        P(),
        P(),
        P(),
        P(),
    )
    return jax.shard_map(shards, mesh=mesh, in_specs=in_specs, out_specs=out_specs, check_vma=False)
```

time: 2200 us -> 979 us (0.45)
  matrix products: 1300 us -> 27.4 us
  Pallas kernels: 0 us -> 124 us
  local copies, waits for them, and re-layouts: 108 us -> 11.7 us
  waiting for transfers between devices: 703 us -> 748 us
    dot_general x92 -> x0, matrix products: 1280 us -> none  [the longest x26 398 us: mixed(): jnp.einsum(form, lower, narrow, preferred_element_type=jnp.float32)]
    pallas_call x0 -> x2, Pallas kernels: none -> 124 us  [the longest x1 70.4 us: attention_backward(): pl.pallas_call(attention_backward_kernel, out_shape=(jax.ShapeDtypeStruct...]
    psum x1, waiting for transfers between devices: 96.4 us -> 56.5 us  [shards(): lax.psum(partial_input, 'head') + grad_attn]
    reduce_scatter x1, waiting for transfers between devices: 0.01 us -> 39.8 us  [shards(): lax.psum_scatter(grad_w_query, 'batch', scatter_dimension=0, tiled=True)]
    reduce_scatter x1, waiting for transfers between devices: 0.01 us -> 39.4 us  [shards(): lax.psum_scatter(grad_w_value, 'batch', scatter_dimension=0, tiled=True)]
  transfers between devices with their start and end apart: 11 -> 11, of which waited for: 9 -> 11; matrix products, arithmetic and copies ran while one was open for 2% -> 2% of each run, Pallas kernels for 0% -> 0%
where the time goes in v1:
time: 979 us; the launch traced here: 970 us
  waiting for transfers between devices  748 us (76%)
  Pallas kernels  124 us (13%)
  matrix products  27.4 us (3%)
  blocking collectives  23.1 us (2%)
  other arithmetic  19.2 us (2%)
  between operations  15.2 us (2%)
  local copies, waits for them, and re-layouts  11.7 us (1%)
    psum x1, waiting for transfers between devices, shards(): lax.psum(partial_rel, ('batch', 'head')).reshape(rel_tables.shape)  132 us
    psum x1, waiting for transfers between devices, shards(): attention_total = lax.psum(partial_attn, 'head')  97.3 us
    psum x1, waiting for transfers between devices, shards(): grad_hidden = lax.psum(partial_hidden, 'head') + grad_mid  94.8 us
    psum x1, waiting for transfers between devices, shards(): ffn_total = lax.psum(partial_ffn, 'head')  94.8 us
    pallas_call x1, Pallas kernels, attention_backward(): pl.pallas_call(attention_backward_kernel, out_shape=(jax.ShapeDtypeStruct...  70.4 us
    psum x1, waiting for transfers between devices, shards(): lax.psum(partial_input, 'head') + grad_attn  56.5 us
    reduce_scatter x1, waiting for transfers between devices, shards(): lax.psum_scatter(grad_w_outer, 'batch', scatter_dimension=1, tiled=True)  55.7 us
    reduce_scatter x1, waiting for transfers between devices, shards(): lax.psum_scatter(grad_w_inner, 'batch', scatter_dimension=0, tiled=True)  55.2 us
  transfers between devices with their start and end apart: 11, of which 11 were waited for; matrix products, arithmetic and copies ran while one was open for 2% of the time, Pallas kernels for 0%

profile of v1, /device:TPU:1, one launch (start us, length us, event | category | flops | bytes accessed | tf_op | source)
XLA Modules:
  0.0 969.8 jit_solution(1566788101620693250)
XLA Ops:
  7.2 1.7 copy.34
  8.9 1.3 pad.4.row_ref
  10.9 53.4 %attention_forward.1 = (bf16[576,256]{1,0:T(8,128)(2,1)}, bf16[576,256]{1,0:T(8,128)(2,1)}, bf16[576,256]{1,0:T(8,128)(2,1)}, bf16[384,256]{1,0:T(8,128)(2,1)}, ...) custom-call(s32[1]{0:T(128)S(6)} %copy.40.length_ref, ...), custom_call_target="tpu_custom_call" | custom-call | tf_op jit(solution)/shard_map/attention_forward/pallas_call | solution.py:133
  64.9 97.3 %all-reduce.8.cloned.1.call-done = f32[576,1024]{1,0:T(8,128)} async-done(((f32[576,1024]{1,0:T(8,128)}), f32[576,1024]{1,0:T(8,128)}) %all-reduce.8.cloned.1.call-update) | async-done | bytes 2359312 | tf_op jit(solution)/shard_map/psum | solution.py:371
  162.2 2.1 fusion.32
  165.1 8.0 multiply_convert_fusion
  173.1 2.8 fusion.34
  175.9 94.8 %all-reduce.10.cloned.1.call-done = f32[576,1024]{1,0:T(8,128)} async-done(((f32[576,1024]{1,0:T(8,128)}), f32[576,1024]{1,0:T(8,128)}) %all-reduce.10.cloned.1.call-update) | async-done | bytes 2359312 | tf_op jit(solution)/shard_map/psum | solution.py:378
  270.7 3.2 fusion.30
  275.2 1.1 fusion.7
  276.3 1.9 fusion.27
  279.0 1.6 copy-done.17
  280.6 2.2 fusion.33
  283.8 2.8 fusion.16
  286.7 94.8 %all-reduce.12.cloned.1.call-done = f32[576,1024]{1,0:T(8,128)} async-done(((f32[576,1024]{1,0:T(8,128)}), f32[576,1024]{1,0:T(8,128)}) %all-reduce.12.cloned.1.call-update) | async-done | bytes 2359312 | tf_op jit(solution)/shard_map/psum | solution.py:397
  381.4 4.4 multiply_reduce_fusion
  386.7 1.4 copy-done.3
  388.1 1.2 convert_element_type.34.grad_ref
  389.3 70.4 %attention_backward.1 = (f32[1024,256]{1,0:T(8,128)}, f32[1024,256]{1,0:T(8,128)}, f32[1024,256]{1,0:T(8,128)}, f32[256,1024]{1,0:T(8,128)}, f32[576,1024]{1,0:T(8,128)}, /*index=5*/f32[384,1024]{1,0:T(8,128)}) custom-call(bf16[576,1024]{1,0:T(8,128)(2,1)} %convert_element_type.34.grad_ref, bf16[576,1024]{1,0:T(8,128)(2,1)} %tok_ref.3, ...), custom_call_target="tpu_custom_call" | custom-call | tf_op jit(solution)/shard_map/attention_backward/pallas_call | solution.py:293
  463.1 6.2 fusion.14
  469.4 5.5 fusion.18
  474.9 23.1 %all-reduce.1 = (f32[1024]{0:T(1024)}, f32[1024]{0:T(1024)}, f32[1024]{0:T(1024)}, f32[1024]{0:T(1024)}, f32[1024]{0:T(1024)}, /*index=5*/f32[1024]{0:T(1024)}, f32[1024]{0:T(1024)}) all-reduce(f32[1024]{0:T(1024)S(1)} %get-tuple-element.61, f32[1024]{0:T(1024)S(1)} %get-tuple-element.44, ...), channel_id=1, replica_groups=mesh['batch'=8,'head'=4] {'batch'}, use_global_device_ids=true, to_apply=%region_17.18 | all-reduce | flops 7168 | bytes 57344 | tf_op jit(solution)/shard_map/psum | solution.py:418
  498.0 56.5 %all-reduce.14.cloned.1.call-done = f32[576,1024]{1,0:T(8,128)} async-done(((f32[576,1024]{1,0:T(8,128)}), f32[576,1024]{1,0:T(8,128)}) %all-reduce.14.cloned.1.call-update) | async-done | bytes 2359312 | tf_op jit(solution)/shard_map/psum | solution.py:408
  554.5 3.8 add_convert_fusion
  558.3 132.1 %all-reduce.16.cloned.1.call-done = f32[3,128,1024]{2,1,0:T(8,128)} async-done(((f32[3,128,1024]{2,1,0:T(8,128)}), f32[3,128,1024]{2,1,0:T(8,128)}) %all-reduce.16.cloned.1.call-update) | async-done | bytes 1572880 | tf_op jit(solution)/shard_map/psum | solution.py:409
  690.4 39.4 %reduce-scatter.11.cloned.1.call-done = f32[128,256]{1,0:T(8,128)} async-done(((f32[1024,256]{1,0:T(8,128)}), f32[128,256]{1,0:T(8,128)}) %reduce-scatter.11.cloned.1.call-update) | async-done | bytes 131088 | tf_op jit(solution)/shard_map/reduce_scatter | solution.py:413
  729.7 39.8 %reduce-scatter.13.cloned.1.call-done = f32[256,128]{1,0:T(8,128)} async-done(((f32[256,1024]{1,0:T(8,128)}), f32[256,128]{1,0:T(8,128)}) %reduce-scatter.13.cloned.1.call-update) | async-done | bytes 131088 | tf_op jit(solution)/shard_map/reduce_scatter | solution.py:414
  769.5 39.8 %reduce-scatter.7.cloned.1.call-done = f32[128,256]{1,0:T(8,128)} async-done(((f32[1024,256]{1,0:T(8,128)}), f32[128,256]{1,0:T(8,128)}) %reduce-scatter.7.cloned.1.call-update) | async-done | bytes 131088 | tf_op jit(solution)/shard_map/reduce_scatter | solution.py:411
  809.3 39.8 %reduce-scatter.9.cloned.1.call-done = f32[128,256]{1,0:T(8,128)} async-done(((f32[1024,256]{1,0:T(8,128)}), f32[128,256]{1,0:T(8,128)}) %reduce-scatter.9.cloned.1.call-update) | async-done | bytes 131088 | tf_op jit(solution)/shard_map/reduce_scatter | solution.py:412
  849.1 55.2 %reduce-scatter.15.cloned.1.call-done = f32[128,1024]{1,0:T(8,128)} async-done(((f32[1024,1024]{1,0:T(8,128)}), f32[128,1024]{1,0:T(8,128)}) %reduce-scatter.15.cloned.1.call-update) | async-done | bytes 524304 | tf_op jit(solution)/shard_map/reduce_scatter | solution.py:415
  904.4 55.7 %reduce-scatter.17.cloned.1.call-done = f32[1024,128]{1,0:T(8,128)} async-done(((f32[1024,1024]{1,0:T(8,128)}), f32[1024,128]{1,0:T(8,128)}) %reduce-scatter.17.cloned.1.call-update) | async-done | bytes 524304 | tf_op jit(solution)/shard_map/reduce_scatter | solution.py:416
  960.1 2.7 copy.41
  (68 shorter events, 8.7 us)
Async XLA Ops:
  7.2 157.5 %copy-start = (bf16[1024,1024]{1,0:T(8,128)(2,1)S(1)}, bf16[1024,1024]{1,0:T(8,128)(2,1)}, u32[]{:S(2)}) copy-start(bf16[1024,1024]{1,0:T(8,128)(2,1)} %param.28) | copy-start | bytes 6291460
  7.2 155.0 %all-reduce.8.cloned.1.call-start = ((), (), s32[]{:S(2)}) async-start(), calls=%async_computation.6 | async-start | bytes 4718592 | tf_op jit(solution)/shard_map/psum | solution.py:371
  10.9 151.3 %copy-start.4 = (bf16[576,1024]{1,0:T(8,128)(2,1)S(1)}, bf16[576,1024]{1,0:T(8,128)(2,1)}, u32[]{:S(2)}) copy-start(bf16[576,1024]{1,0:T(8,128)(2,1)} %tok_ref.3) | copy-start | bytes 3538948
  10.9 151.3 %copy-start.12 = (f32[1024]{0:T(1024)S(1)}, f32[1024]{0:T(1024)}, u32[]{:S(2)}) copy-start(f32[1024]{0:T(1024)} %param.25) | copy-start | bytes 12292
  64.3 206.4 %all-reduce.10.cloned.1.call-start = ((), (), s32[]{:S(2)}) async-start(), calls=%async_computation.7 | async-start | bytes 4718592 | tf_op jit(solution)/shard_map/psum | solution.py:378
  164.2 8.8 copy-start.1
  164.2 0.7 copy-start.7
  164.3 0.7 copy-start.11
  164.3 0.8 copy-start.15
  165.1 8.0 copy-start.13
  175.9 94.8 %copy-start.9 = (f32[1024]{0:T(1024)S(1)}, f32[1024]{0:T(1024)}, u32[]{:S(2)}) copy-start(f32[1024]{0:T(1024)} %param.31) | copy-start | bytes 12292
  175.9 205.5 %all-reduce.12.cloned.1.call-start = ((), (), s32[]{:S(2)}) async-start(), calls=%async_computation.8 | async-start | bytes 4718592 | tf_op jit(solution)/shard_map/psum | solution.py:397
  273.9 1.3 copy-start.6
  273.9 1.3 copy-start.8
  274.3 2.0 copy-start.10
  276.3 2.0 copy-start.14
  276.3 2.7 copy-start.16
  276.3 4.3 copy-start.17
  278.3 4.5 copy-start.5
  282.8 1.0 copy-start.18
  286.6 267.9 %all-reduce.14.cloned.1.call-start = ((), (), s32[]{:S(2)}) async-start(), calls=%async_computation.9 | async-start | bytes 4718592 | tf_op jit(solution)/shard_map/psum | solution.py:408
  381.4 4.5 copy-start.2
  386.7 1.4 copy-start.3
  459.7 230.7 %all-reduce.16.cloned.1.call-start = ((), (), s32[]{:S(2)}) async-start(), calls=%async_computation.16 | async-start | bytes 3145728 | tf_op jit(solution)/shard_map/psum | solution.py:409
  460.3 269.5 %reduce-scatter.11.cloned.1.call-start = ((), (), s32[]{:S(2)}) async-start(), calls=%async_computation.12 | async-start | bytes 1179648 | tf_op jit(solution)/shard_map/reduce_scatter | solution.py:413
  460.8 308.7 %reduce-scatter.13.cloned.1.call-start = ((), (), s32[]{:S(2)}) async-start(), calls=%async_computation.13 | async-start | bytes 1179648 | tf_op jit(solution)/shard_map/reduce_scatter | solution.py:414
  461.6 347.7 %reduce-scatter.7.cloned.1.call-start = ((), (), s32[]{:S(2)}) async-start(), calls=%async_computation.10 | async-start | bytes 1179648 | tf_op jit(solution)/shard_map/reduce_scatter | solution.py:411
  462.3 386.8 %reduce-scatter.9.cloned.1.call-start = ((), (), s32[]{:S(2)}) async-start(), calls=%async_computation.11 | async-start | bytes 1179648 | tf_op jit(solution)/shard_map/reduce_scatter | solution.py:412
  463.1 441.3 %reduce-scatter.15.cloned.1.call-start = ((), (), s32[]{:S(2)}) async-start(), calls=%async_computation.14 | async-start | bytes 4718592 | tf_op jit(solution)/shard_map/reduce_scatter | solution.py:415
  469.3 490.7 %reduce-scatter.17.cloned.1.call-start = ((), (), s32[]{:S(2)}) async-start(), calls=%async_computation.15 | async-start | bytes 4718592 | tf_op jit(solution)/shard_map/reduce_scatter | solution.py:416
Sparse Core Ops, SparseCore 0:
  64.5 97.6 all-reduce.7
  176.0 94.6 all-reduce.9
  286.7 94.6 all-reduce.11
  459.8 94.6 all-reduce.13
  560.2 130.1 all-reduce.15
  694.0 35.7 reduce-scatter.10
  733.5 35.9 reduce-scatter.12
  773.3 35.9 reduce-scatter.6
  813.1 36.0 reduce-scatter.8
  852.9 51.4 reduce-scatter.14
  908.7 51.3 reduce-scatter.16

commit v2 on v1

--- a/solution.py
+++ b/solution.py
@@ -32,8 +32,8 @@
 
 
 def attention_forward_kernel(
-    length_ref, tok_ref, wq_ref, wk_ref, wv_ref, rel_ref, col_ref, row_ref, wo_ref,
-    q_ref, k_ref, v_ref, krel_ref, qrel_ref, attend_ref, ctx_ref, part_ref,
+    length_ref, tok_ref, wq_ref, wk_ref, wv_ref, rel_ref, col_ref, row_ref,
+    q_ref, k_ref, v_ref, krel_ref, qrel_ref, attend_ref, ctx_ref,
     idx_ref, log_ref, col_part_ref, tq_ref, tk_ref, kv_ref,
 ):
     slots = tok_ref.shape[0]
@@ -120,10 +120,9 @@
             attend_ref[head, at, :] = (grown / total).astype(jnp.bfloat16)
 
         ctx_ref[:, cols] = dot_nn(attend_ref[head], kv_ref[1, :, cols]).astype(jnp.bfloat16)
-    part_ref[...] = dot_nn(ctx_ref[...], wo_ref[...])
-
-
-def attention_forward(tokens, length, corner_col, corner_row, w_query, w_key, w_value, rel, w_output):
+
+
+def attention_forward(tokens, length, corner_col, corner_row, w_query, w_key, w_value, rel):
     slots, width = tokens.shape
     mine = w_query.shape[1]
     heads = mine // HEAD
@@ -140,10 +139,9 @@
             jax.ShapeDtypeStruct((3 * NB, mine), low),
             jax.ShapeDtypeStruct((heads, slots, wide), low),
             jax.ShapeDtypeStruct((slots, mine), low),
-            jax.ShapeDtypeStruct((slots, width), jnp.float32),
         ),
-        in_specs=[pl.BlockSpec(memory_space=pltpu.SMEM)] + [vmem] * 8,
-        out_specs=(vmem,) * 8,
+        in_specs=[pl.BlockSpec(memory_space=pltpu.SMEM)] + [vmem] * 7,
+        out_specs=(vmem,) * 7,
         scratch_shapes=[
             pltpu.VMEM((2, slots, wide), jnp.int32),
             pltpu.VMEM((slots, wide), jnp.float32),
@@ -154,7 +152,9 @@
         ],
         compiler_params=pltpu.CompilerParams(vmem_limit_bytes=VMEM_LIMIT),
         name="attention_forward",
-    )(length, tokens, w_query, w_key, w_value, rel, corner_col, corner_row, w_output)
+    )(length, tokens, w_query, w_key, w_value, rel, corner_col, corner_row)
+
+
 def attention_backward_kernel(
     grad_ref, tok_ref, wq_ref, wk_ref, wv_ref, wo_ref, rel_ref, col_ref,
     q_ref, k_ref, v_ref, krel_ref, qrel_ref, attend_ref, ctx_ref,
@@ -170,7 +170,7 @@
     low = jnp.bfloat16
     block = 32
     gc_ref[...] = dot_nt(grad_ref[...], wo_ref[...]).astype(low)
-    gwo_ref[...] = dot_tn(ctx_ref[...], grad_ref[...])
+    gwo_ref[...] = dot_tn(grad_ref[...], ctx_ref[...])
     kv_ref[...] = jnp.zeros_like(kv_ref)
     kv_ref[0, :slots, :] = k_ref[...]
     kv_ref[1, :slots, :] = v_ref[...]
@@ -296,7 +296,7 @@
             jax.ShapeDtypeStruct((width, mine), full),
             jax.ShapeDtypeStruct((width, mine), full),
             jax.ShapeDtypeStruct((width, mine), full),
-            jax.ShapeDtypeStruct((mine, width), full),
+            jax.ShapeDtypeStruct((width, mine), full),
             jax.ShapeDtypeStruct((slots, width), full),
             jax.ShapeDtypeStruct((3 * NB, width), full),
         ),
@@ -320,22 +320,537 @@
     )(grad, tokens, w_query, w_key, w_value, w_output, rel, corner_col, q, k, v, krel, qrel, attend, ctx)
 
 
-def layer_stats(values):
+MESH = pl.DeviceIdType.MESH
+
+
+class Line:
+    def __init__(self, axis, own, inner, outer, sems):
+        self.axis, self.own, self.inner, self.outer = axis, own, inner, outer
+        self.in_send, self.in_recv, self.out_send, self.out_recv = sems
+        self.n = lax.axis_size(axis)
+        me = lax.axis_index(axis)
+        left = me < self.n // 2
+        self.depth = jnp.where(left, me, self.n - 1 - me)
+        self.inward = jnp.where(left, me + 1, me - 1)
+        self.outward = jnp.where(self.depth == 0, self.inward, jnp.where(left, me - 1, me + 1))
+        self.last = self.n // 2 - 1
+
+    def greet(self, barrier):
+        pl.semaphore_signal(barrier, inc=1, device_id={self.axis: self.inward}, device_id_type=MESH)
+
+        @pl.when(self.depth > 0)
+        def _():
+            pl.semaphore_signal(
+                barrier, inc=1, device_id={self.axis: self.outward}, device_id_type=MESH
+            )
+
+    def greeted(self):
+        return jnp.where(self.depth > 0, 2, 1)
+
+    def copy(self, source, target, send, recv, to):
+        return pltpu.make_async_remote_copy(
+            src_ref=source,
+            dst_ref=target,
+            send_sem=send,
+            recv_sem=recv,
+            device_id={self.axis: to},
+            device_id_type=MESH,
+        )
+
+    def send_in(self, u, source):
+        @pl.when(self.depth < self.last)
+        def _():
+            self.copy(
+                source, self.inner.at[u], self.in_send.at[u], self.in_recv.at[u], self.inward
+            ).start()
+
+        @pl.when(self.depth == self.last)
+        def _():
+            self.copy(
+                source, self.outer.at[u], self.in_send.at[u], self.out_recv.at[u], self.inward
+            ).start()
+
+    def step(self, slot, count):
+        here = slot - self.depth
+
+        @pl.when((here >= 0) & (here < count))
+        def _():
+            u = here
+
+            @pl.when(self.depth == 0)
+            def _():
+                self.send_in(u, self.own.at[u])
+
+            @pl.when(self.depth > 0)
+            def _():
+                self.copy(
+                    self.own.at[u], self.inner.at[u], self.in_send.at[u], self.in_recv.at[u], self.inward
+                ).wait_recv()
+                self.inner[u] += self.own[u]
+                self.send_in(u, self.inner.at[u])
+
+        back = slot - (self.n - 1 - self.depth)
+
+        @pl.when((back >= 0) & (back < count))
+        def _():
+            u = back
+            self.copy(
+                self.own.at[u], self.outer.at[u], self.out_send.at[u], self.out_recv.at[u], self.outward
+            ).wait_recv()
+
+            @pl.when(self.depth == self.last)
+            def _():
+                self.outer[u] += self.inner[u] if self.last > 0 else self.own[u]
+
+            @pl.when(self.depth > 0)
+            def _():
+                self.copy(
+                    self.outer.at[u],
+                    self.outer.at[u],
+                    self.out_send.at[u],
+                    self.out_recv.at[u],
+                    self.outward,
+                ).start()
+
+    def drain(self, count):
+        @pl.loop(0, count)
+        def _(u):
+            self.copy(
+                self.own.at[u], self.inner.at[u], self.in_send.at[u], self.in_recv.at[u], self.inward
+            ).wait_send()
+
+            @pl.when(self.depth > 0)
+            def _():
+                self.copy(
+                    self.outer.at[u],
+                    self.outer.at[u],
+                    self.out_send.at[u],
+                    self.out_recv.at[u],
+                    self.outward,
+                ).wait_send()
+
+
+def centre(values):
     average = jnp.mean(values, axis=-1, keepdims=True)
     centered = values - average
-    spread_squared = jnp.mean(centered * centered, axis=-1, keepdims=True)
-    scaling = lax.rsqrt(spread_squared + 1e-05)
-    return (centered * scaling, scaling)
-
-
-def norm_back(upstream, normed, scaling, gain_in):
-    scaled = upstream * gain_in
-    inward = scaling * (
+    spread = jnp.mean(centered * centered, axis=-1, keepdims=True)
+    scaling = lax.rsqrt(spread + 1e-05)
+    return centered * scaling, scaling
+
+
+def norm_inward(scaled, normed, scaling):
+    return scaling * (
         scaled
         - jnp.mean(scaled, axis=-1, keepdims=True)
         - normed * jnp.mean(scaled * normed, axis=-1, keepdims=True)
     )
-    return (inward, jnp.sum(upstream * normed, axis=0), jnp.sum(upstream, axis=0))
+
+
+def fold_rows(values):
+    rows, width = values.shape
+    return jnp.sum(values.reshape(rows // 8, 8, width), axis=0)
+
+
+CHUNK = 64
+
+
+def middle_kernel(
+    ctx_ref, wo_ref, tok_ref, cot_ref, wi_ref, wu_ref,
+    bo_ref, ga_ref, sa_ref, bi_ref, bu_ref, gf_ref, sf_ref,
+    out_ref, grad_ref, grad_low_ref, hidden_ref, active_ref, mid_low_ref, inner_low_ref, small_ref,
+    own, inner, outer, normed_ref, scale_ref, pre_ref, mid_ref, sums_ref,
+    in_send, in_recv, out_send, out_recv,
+):
+    slots = tok_ref.shape[0]
+    chunks = slots // CHUNK
+    low, full = jnp.bfloat16, jnp.float32
+    line = Line("head", own, inner, outer, (in_send, in_recv, out_send, out_recv))
+    barrier = pltpu.get_barrier_semaphore()
+    line.greet(barrier)
+    sums_ref[...] = jnp.zeros_like(sums_ref)
+    pl.semaphore_wait(barrier, line.greeted())
+    root = 0.5**0.5
+    bell = (0.5 / jnp.pi) ** 0.5
+
+    def rows(c):
+        return pl.ds(pl.multiple_of(c * CHUNK, CHUNK), CHUNK)
+
+    def project(c):
+        own[c] = dot_nn(ctx_ref[rows(c), :], wo_ref[...])
+
+    def after_attention(c, u):
+        at = rows(c)
+        normed, scaling = centre(outer[u] + bo_ref[...] + tok_ref[at, :].astype(full))
+        normed_ref[at, :] = normed
+        scale_ref[at, :] = scaling
+        hidden_low = (normed * ga_ref[...] + sa_ref[...]).astype(low)
+        hidden_ref[at, :] = hidden_low
+        pre = dot_nn(hidden_low, wi_ref[...]) + bi_ref[...]
+        pre_ref[at, :] = pre
+        active = (pre * (1.0 + lax.erf(pre * root)) * 0.5).astype(low)
+        active_ref[at, :] = active
+        own[u + chunks] = dot_nn(active, wu_ref[...])
+
+    def after_ffn(c, u):
+        at = rows(c)
+        hidden = normed_ref[at, :] * ga_ref[...] + sa_ref[...]
+        normed, scaling = centre(outer[u] + bu_ref[...] + hidden)
+        out_ref[at, :] = (normed * gf_ref[...] + sf_ref[...]).astype(low)
+        upstream = cot_ref[at, :].astype(full)
+        grad_mid = norm_inward(upstream * gf_ref[...], normed, scaling)
+        sums_ref[4] += fold_rows(grad_mid)
+        sums_ref[5] += fold_rows(upstream * normed)
+        sums_ref[6] += fold_rows(upstream)
+        mid_ref[at, :] = grad_mid
+        mid_low = grad_mid.astype(low)
+        mid_low_ref[at, :] = mid_low
+        grad_active = dot_nt(mid_low, wu_ref[...])
+        pre = pre_ref[at, :]
+        slope = (1.0 + lax.erf(pre * root)) * 0.5 + pre * jnp.exp(-0.5 * pre * pre) * bell
+        inner_low = (grad_active * slope).astype(low)
+        sums_ref[3] += fold_rows(inner_low.astype(full))
+        inner_low_ref[at, :] = inner_low
+        own[u + chunks] = dot_nt(inner_low, wi_ref[...])
+
+    def after_hidden(c, u):
+        at = rows(c)
+        upstream = outer[u] + mid_ref[at, :]
+        normed = normed_ref[at, :]
+        grad_attn = norm_inward(upstream * ga_ref[...], normed, scale_ref[at, :])
+        sums_ref[0] += fold_rows(grad_attn)
+        sums_ref[1] += fold_rows(upstream * normed)
+        sums_ref[2] += fold_rows(upstream)
+        grad_ref[at, :] = grad_attn
+        grad_low_ref[at, :] = grad_attn.astype(low)
+
+    @pl.loop(0, 3 * chunks + line.n - 1)
+    def _(slot):
+        @pl.when(slot < chunks)
+        def _():
+            project(slot)
+
+        line.step(slot, 3 * chunks)
+        done = slot - (line.n - 1)
+
+        @pl.when((done >= 0) & (done < chunks))
+        def _():
+            after_attention(done, done)
+
+        @pl.when((done >= chunks) & (done < 2 * chunks))
+        def _():
+            after_ffn(done - chunks, done)
+
+        @pl.when(done >= 2 * chunks)
+        def _():
+            after_hidden(done - 2 * chunks, done)
+
+    for at in range(7):
+        small_ref[at : at + 1, :] = jnp.sum(sums_ref[at], axis=0, keepdims=True)
+    small_ref[7:8, :] = jnp.zeros_like(small_ref[7:8, :])
+    line.drain(3 * chunks)
+
+
+def middle(ctx, w_output, tokens, cotangent, w_inner, w_outer, vectors):
+    slots, width = tokens.shape
+    units = w_inner.shape[1]
+    assert units == width
+    low, full = jnp.bfloat16, jnp.float32
+    vmem = pl.BlockSpec(memory_space=pltpu.VMEM)
+    steps = 3 * (slots // CHUNK)
+    return pl.pallas_call(
+        middle_kernel,
+        out_shape=(
+            jax.ShapeDtypeStruct((slots, width), low),
+            jax.ShapeDtypeStruct((slots, width), full),
+            jax.ShapeDtypeStruct((slots, width), low),
+            jax.ShapeDtypeStruct((slots, width), low),
+            jax.ShapeDtypeStruct((slots, units), low),
+            jax.ShapeDtypeStruct((slots, width), low),
+            jax.ShapeDtypeStruct((slots, units), low),
+            jax.ShapeDtypeStruct((8, width), full),
+        ),
+        in_specs=[vmem] * 13,
+        out_specs=(vmem,) * 8,
+        scratch_shapes=[
+            pltpu.VMEM((steps, CHUNK, width), full),
+            pltpu.VMEM((steps, CHUNK, width), full),
+            pltpu.VMEM((steps, CHUNK, width), full),
+            pltpu.VMEM((slots, width), full),
+            pltpu.VMEM((slots, 1), full),
+            pltpu.VMEM((slots, units), full),
+            pltpu.VMEM((slots, width), full),
+            pltpu.VMEM((7, 8, width), full),
+        ]
+        + [pltpu.SemaphoreType.DMA((steps,))] * 4,
+        compiler_params=pltpu.CompilerParams(
+            vmem_limit_bytes=VMEM_LIMIT, collective_id=1, has_side_effects=True
+        ),
+        name="middle",
+    )(ctx, w_output, tokens, cotangent, w_inner, w_outer, *[v.reshape(1, -1) for v in vectors])
+
+
+class Halving:
+    def __init__(self, order, source, got, out, send, recv):
+        self.order, self.source, self.got, self.out = order, source, got, out
+        self.send, self.recv = send, recv
+        self.b = lax.axis_index("batch")
+
+    def part(self, stage, flip):
+        bit = self.order[stage]
+        rest = sorted(self.order[stage:], reverse=True)
+        mine = (self.b >> bit) & 1
+        pick = 1 - mine if flip else mine
+        return tuple(pick if k == bit else slice(None) for k in rest)
+
+    def copy(self, stage):
+        source = self.source if stage == 0 else self.got[stage - 1]
+        return pltpu.make_async_remote_copy(
+            src_ref=source.at[self.part(stage, True)],
+            dst_ref=self.got[stage],
+            send_sem=self.send.at[stage],
+            recv_sem=self.recv.at[stage],
+            device_id={"batch": self.b ^ (1 << self.order[stage])},
+            device_id_type=MESH,
+        )
+
+    def start(self):
+        self.copy(0).start()
+
+    def turn(self, stage):
+        self.copy(stage).wait_recv()
+        kept = self.source if stage == 0 else self.got[stage - 1]
+        value = kept[self.part(stage, False)] + self.got[stage][...]
+        if stage + 1 < len(self.order):
+            self.got[stage][...] = value
+            self.copy(stage + 1).start()
+        else:
+            self.out[...] = value
+
+    def drain(self):
+        for stage in range(len(self.order)):
+            self.copy(stage).wait_send()
+
+
+def final_kernel(
+    gin_ref, grad_ref, gwq_ref, gwk_ref, gwv_ref, gwo_ref,
+    hidden_ref, active_ref, mid_low_ref, inner_low_ref, grel_ref, small_ref,
+    gtok_ref, owq_ref, owk_ref, owv_ref, owo_ref, owi_ref, owu_ref, orel_ref, osmall_ref,
+    inner, outer, gwi_ref, gwu_ref, rel_own, rel_in, rel_out, rel_all, small_sum, small_got,
+    *rest,
+    bits, pieces,
+):
+    got = [rest[at * bits : (at + 1) * bits] for at in range(len(pieces) + 1)]
+    (in_send, in_recv, out_send, out_recv, rin_send, rin_recv, rout_send, rout_recv,
+     piece_send, piece_recv, back_send, back_recv, small_send, small_recv) = rest[(len(pieces) + 1) * bits :]
+    chunks = gin_ref.shape[0]
+    low, full = jnp.bfloat16, jnp.float32
+    line = Line("head", gin_ref, inner, outer, (in_send, in_recv, out_send, out_recv))
+    rel_line = Line("head", rel_own, rel_in, rel_out, (rin_send, rin_recv, rout_send, rout_recv))
+    b = lax.axis_index("batch")
+    barrier = pltpu.get_barrier_semaphore()
+    line.greet(barrier)
+    for k in range(bits):
+        pl.semaphore_signal(barrier, inc=1, device_id={"batch": b ^ (1 << k)}, device_id_type=MESH)
+    pl.semaphore_wait(barrier, line.greeted() + bits)
+
+    orders = (list(range(bits)), [0] + list(range(bits - 1, 0, -1)))
+    sources = (gwq_ref, gwk_ref, gwv_ref, gwo_ref, gwi_ref, gwu_ref)
+    outs = (owq_ref, owk_ref, owv_ref, owo_ref, owi_ref, owu_ref)
+    whole = (slice(None),) * (bits + 1)
+    jobs = []
+    for at, (which, start, size) in enumerate(pieces):
+        lanes = slice(start, start + size)
+        jobs.append(
+            Halving(
+                orders[at % 2],
+                sources[which].at[whole + (lanes,)],
+                got[at],
+                outs[which].at[:, lanes],
+                piece_send.at[at],
+                piece_recv.at[at],
+            )
+        )
+    rel_job = Halving(
+        orders[0], grel_ref, got[-1], rel_own.at[0], piece_send.at[len(pieces)], piece_recv.at[len(pieces)]
+    )
+
+    def make(at):
+        which, start, size = pieces[at]
+        lanes = slice(start, start + size)
+        if which == 4:
+            value = dot_tn(hidden_ref[...], inner_low_ref[:, lanes])
+        elif which == 5:
+            value = dot_tn(mid_low_ref[...], active_ref[:, lanes])
+        else:
+            return
+        target = sources[which]
+        target[whole + (lanes,)] = value.reshape(target.shape[:-1] + (size,))
+
+    def small_copy(k):
+        return pltpu.make_async_remote_copy(
+            src_ref=small_sum.at[k],
+            dst_ref=small_got.at[k],
+            send_sem=small_send.at[k],
+            recv_sem=small_recv.at[k],
+            device_id={"batch": b ^ (1 << k)},
+            device_id_type=MESH,
+        )
+
+    def small_turn(k):
+        small_copy(k).wait_recv()
+        value = small_sum[k] + small_got[k]
+        if k + 1 < bits:
+            small_sum[k + 1] = value
+            small_copy(k + 1).start()
+        else:
+            osmall_ref[...] = value
+
+    def back_copy(k):
+        region = tuple(
+            slice(None) if other > k else (b >> other) & 1 for other in range(bits - 1, -1, -1)
+        )
+        return pltpu.make_async_remote_copy(
+            src_ref=rel_all.at[region],
+            dst_ref=rel_all.at[region],
+            send_sem=back_send.at[k],
+            recv_sem=back_recv.at[k],
+            device_id={"batch": b ^ (1 << k)},
+            device_id_type=MESH,
+        )
+
+    def back_turn(k):
+        back_copy(k).wait_recv()
+        if k > 0:
+            back_copy(k - 1).start()
+
+    def rel_step(slot):
+        rel_line.step(slot, 1)
+        if slot == rel_line.n - 1:
+            region = tuple((b >> other) & 1 for other in range(bits - 1, -1, -1))
+            rel_all[region] = rel_out[0]
+            back_copy(bits - 1).start()
+
+    def tokens_step(done):
+        gtok_ref[done] = (outer[done] + grad_ref[done]).astype(low)
+
+    small_sum[0] = small_ref[...]
+    small_copy(0).start()
+    rel_job.start()
+    for at in range(len(pieces)):
+        if pieces[at][0] < 4:
+            jobs[at].start()
+
+    early = [at for at in range(len(pieces)) if pieces[at][0] < 4]
+    late = [at for at in range(len(pieces)) if pieces[at][0] >= 4]
+    tasks = {}
+
+    def add(slot, task):
+        tasks.setdefault(slot, []).append(task)
+
+    total = chunks + line.n - 1
+    for at in late:
+        add(0, lambda at=at: (make(at), jobs[at].start()))
+    add(1, lambda: rel_job.turn(0))
+    add(1, lambda: small_turn(0))
+    for at in early:
+        add(1, lambda at=at: jobs[at].turn(0))
+    for at in late:
+        add(2, lambda at=at: jobs[at].turn(0))
+    for k in range(1, bits):
+        add(1 + k, lambda k=k: rel_job.turn(k))
+        add(1 + k, lambda k=k: small_turn(k))
+    for step in range(line.n):
+        add(1 + bits + step, lambda step=step: rel_step(step))
+    for k in range(bits - 1, -1, -1):
+        add(1 + bits + line.n + bits - k, lambda k=k: back_turn(k))
+    for stage in range(1, bits):
+        for place, at in enumerate(early):
+            add(1 + 2 * stage + place // 2, lambda at=at, stage=stage: jobs[at].turn(stage))
+        for place, at in enumerate(late):
+            add(2 + 3 * stage + 2 * (place // 2) , lambda at=at, stage=stage: jobs[at].turn(stage))
+
+    for slot in range(max(total, max(tasks) + 1)):
+        if slot < total:
+            line.step(jnp.int32(slot), chunks)
+            if slot >= line.n - 1:
+                tokens_step(slot - (line.n - 1))
+        for task in tasks.get(slot, ()):
+            task()
+    orel_ref[...] = rel_all[...]
+    line.drain(chunks)
+    rel_line.drain(1)
+    for job in jobs:
+        job.drain()
+    rel_job.drain()
+    for k in range(bits):
+        small_copy(k).wait_send()
+        back_copy(k).wait_send()
+
+
+def final(gin, grad, gwq, gwk, gwv, gwo, hidden, active, mid_low, inner_low, grel, small, batch):
+    slots, width = gin.shape
+    mine, units = gwq.shape[1], active.shape[1]
+    bits = batch.bit_length() - 1
+    assert 1 << bits == batch
+    low, full = jnp.bfloat16, jnp.float32
+    vmem = pl.BlockSpec(memory_space=pltpu.VMEM)
+    chunks = slots // CHUNK
+    split = (2,) * bits
+    part = width // batch
+    rel_part = grel.shape[0] // batch
+    piece = 512
+    pieces = [(which, 0, mine) for which in range(4)]
+    for start in range(0, units, piece):
+        pieces += [(4, start, piece), (5, start, piece)]
+    shape = jax.ShapeDtypeStruct
+    got = []
+    for _, _, size in pieces:
+        got += [pltpu.VMEM((2,) * (bits - 1 - s) + (part, size), full) for s in range(bits)]
+    got += [pltpu.VMEM((2,) * (bits - 1 - s) + (rel_part, width), full) for s in range(bits)]
+    dma = pltpu.SemaphoreType.DMA
+    by_block = lambda a: a.reshape(split + (a.shape[0] // batch, a.shape[1]))
+    by_chunk = lambda a: a.reshape(chunks, CHUNK, width)
+    outs = pl.pallas_call(
+        functools.partial(final_kernel, bits=bits, pieces=pieces),
+        out_shape=(
+            shape((chunks, CHUNK, width), low),
+            shape((part, mine), full),
+            shape((part, mine), full),
+            shape((part, mine), full),
+            shape((part, mine), full),
+            shape((part, units), full),
+            shape((part, units), full),
+            shape(split + (rel_part, width), full),
+            shape((8, width), full),
+        ),
+        in_specs=[vmem] * 12,
+        out_specs=(vmem,) * 9,
+        scratch_shapes=[
+            pltpu.VMEM((chunks, CHUNK, width), full),
+            pltpu.VMEM((chunks, CHUNK, width), full),
+            pltpu.VMEM(split + (part, units), full),
+            pltpu.VMEM(split + (part, units), full),
+            pltpu.VMEM((1, rel_part, width), full),
+            pltpu.VMEM((1, rel_part, width), full),
+            pltpu.VMEM((1, rel_part, width), full),
+            pltpu.VMEM(split + (rel_part, width), full),
+            pltpu.VMEM((bits, 8, width), full),
+            pltpu.VMEM((bits, 8, width), full),
+        ]
+        + got
+        + [dma((chunks,))] * 4
+        + [dma((1,))] * 4
+        + [dma((len(pieces) + 1, bits))] * 2
+        + [dma((bits,))] * 4,
+        compiler_params=pltpu.CompilerParams(
+            vmem_limit_bytes=VMEM_LIMIT, collective_id=2, has_side_effects=True
+        ),
+        name="final",
+    )(
+        by_chunk(gin), by_chunk(grad), by_block(gwq), by_block(gwk), by_block(gwv), by_block(gwo),
+        hidden, active, mid_low, inner_low, by_block(grel), small,
+    )
+    return (outs[0].reshape(slots, width),) + tuple(outs[1:7]) + (outs[7].reshape(grel.shape), outs[8])
 
 
 def shards(
@@ -364,86 +879,37 @@
     corner_col = corners.T
     corner_row = jnp.pad(corners, ((0, 0), (0, wide - slots_page)))
     kept = attention_forward(
-        tokens, page_lengths, corner_col, corner_row, w_query, w_key, w_value, rel_rows, w_output
-    )
-    partial_attn = kept[7]
-    token_float = tokens.astype(jnp.float32)
-    attention_total = lax.psum(partial_attn, "head")
-    normed_one, scale_one = layer_stats(attention_total + b_output + token_float)
-    hidden_one = normed_one * gain_attn + shift_attn
-    hidden_low = hidden_one.astype(jnp.bfloat16)
-    inner_pre = jnp.dot(hidden_low, w_inner, preferred_element_type=jnp.float32) + b_inner
-    active = jax.nn.gelu(inner_pre, approximate=False).astype(jnp.bfloat16)
-    partial_ffn = jnp.dot(active, w_outer, preferred_element_type=jnp.float32)
-    ffn_total = lax.psum(partial_ffn, "head")
-    normed_two, scale_two = layer_stats(ffn_total + b_outer + hidden_one)
-    output = (normed_two * gain_ffn + shift_ffn).astype(jnp.bfloat16)
-    grad_out = cotangent.astype(jnp.float32)
-    grad_mid, grad_gain_ffn, grad_shift_ffn = norm_back(grad_out, normed_two, scale_two, gain_ffn)
-    grad_b_outer = jnp.sum(grad_mid, axis=0)
-    grad_mid_low = grad_mid.astype(jnp.bfloat16)
-    grad_w_outer = jnp.einsum("tf,td->fd", active, grad_mid_low, preferred_element_type=jnp.float32)
-    grad_active = jnp.einsum("td,fd->tf", grad_mid_low, w_outer, preferred_element_type=jnp.float32)
-    _, gelu_pull = jax.vjp(lambda pre_value: jax.nn.gelu(pre_value, approximate=False), inner_pre)
-    grad_inner = gelu_pull(grad_active)[0]
-    grad_b_inner = jnp.sum(grad_inner, axis=0)
-    grad_inner_low = grad_inner.astype(jnp.bfloat16)
-    grad_w_inner = jnp.einsum(
-        "td,tf->df", hidden_low, grad_inner_low, preferred_element_type=jnp.float32
-    )
-    partial_hidden = jnp.einsum(
-        "tf,df->td", grad_inner_low, w_inner, preferred_element_type=jnp.float32
-    )
-    grad_hidden = lax.psum(partial_hidden, "head") + grad_mid
-    grad_attn, grad_gain_attn, grad_shift_attn = norm_back(
-        grad_hidden, normed_one, scale_one, gain_attn
-    )
-    grad_b_output = jnp.sum(grad_attn, axis=0)
-    grad_attn_low = grad_attn.astype(jnp.bfloat16)
-    grad_w_query, grad_w_key, grad_w_value, grad_w_output, partial_input, partial_rel = (
-        attention_backward(
-            grad_attn_low, tokens, w_query, w_key, w_value, w_output, rel_rows, corner_col, *kept[:7]
-        )
-    )
-    grad_tokens = (lax.psum(partial_input, "head") + grad_attn).astype(jnp.bfloat16)
-    grad_rel = lax.psum(partial_rel, ("batch", "head")).reshape(rel_tables.shape)
-    summed_weights = (
-        lax.psum_scatter(grad_w_query, "batch", scatter_dimension=0, tiled=True),
-        lax.psum_scatter(grad_w_key, "batch", scatter_dimension=0, tiled=True),
-        lax.psum_scatter(grad_w_value, "batch", scatter_dimension=0, tiled=True),
-        lax.psum_scatter(grad_w_output, "batch", scatter_dimension=1, tiled=True),
-        lax.psum_scatter(grad_w_inner, "batch", scatter_dimension=0, tiled=True),
-        lax.psum_scatter(grad_w_outer, "batch", scatter_dimension=1, tiled=True),
-    )
-    summed_small = lax.psum(
-        (
-            grad_b_output,
-            grad_gain_attn,
-            grad_shift_attn,
-            grad_b_inner,
-            grad_b_outer,
-            grad_gain_ffn,
-            grad_shift_ffn,
-        ),
-        "batch",
-    )
+        tokens, page_lengths, corner_col, corner_row, w_query, w_key, w_value, rel_rows
+    )
+    vectors = (b_output, gain_attn, shift_attn, b_inner, b_outer, gain_ffn, shift_ffn)
+    output, grad_attn, grad_low, hidden, active, mid_low, inner_low, small = middle(
+        kept[6], w_output, tokens, cotangent, w_inner, w_outer, vectors
+    )
+    grads = attention_backward(
+        grad_low, tokens, w_query, w_key, w_value, w_output, rel_rows, corner_col, *kept
+    )
+    done = final(
+        grads[4], grad_attn, *grads[:4], hidden, active, mid_low, inner_low, grads[5], small,
+        lax.axis_size("batch"),
+    )
+    small = done[8]
     return (
         output,
-        grad_tokens,
-        summed_weights[0],
-        summed_weights[1],
-        summed_weights[2],
-        summed_weights[3],
-        summed_small[0],
-        summed_small[1],
-        summed_small[2],
-        summed_weights[4],
-        summed_small[3],
-        summed_weights[5],
-        summed_small[4],
-        summed_small[5],
-        summed_small[6],
-        grad_rel,
+        done[0],
+        done[1],
+        done[2],
+        done[3],
+        done[4].T,
+        small[0],
+        small[1],
+        small[2],
+        done[5],
+        small[3],
+        done[6].T,
+        small[4],
+        small[5],
+        small[6],
+        done[7].reshape(rel_tables.shape),
     )
 
 

time: 979 us -> 431 us (0.44)
  waiting for transfers between devices: 748 us -> 0 us
  Pallas kernels: 124 us -> 406 us
  matrix products: 27.4 us -> 0 us
  blocking collectives: 23.1 us -> 0 us
  other arithmetic: 19.2 us -> 0 us
  between operations: 15.2 us -> 1.77 us
    psum x5 -> x0, waiting for transfers between devices: 476 us -> none  [the longest x1 132 us: shards(): lax.psum(partial_rel, ('batch', 'head')).reshape(rel_tables.shape)]
    pallas_call x0 -> x2, Pallas kernels: none -> 283 us  [the longest x1 175 us: middle(): pl.pallas_call(middle_kernel, out_shape=(jax.ShapeDtypeStruct((slots, wid...]
    reduce_scatter x6 -> x0, waiting for transfers between devices: 270 us -> none  [the longest x1 55.7 us: shards(): lax.psum_scatter(grad_w_outer, 'batch', scatter_dimension=1, tiled=True)]
    dot_general x6 -> x0, matrix products: 27.4 us -> none  [the longest x1 8 us: shards(): jnp.dot(hidden_low, w_inner, preferred_element_type=jnp.float32) + b_inner]
    psum x1 -> x0, blocking collectives: 23.1 us -> none  [shards(): lax.psum((grad_b_output, grad_gain_attn, grad_shift_attn, grad_b_inner, g...]
    reduce_sum x8 -> x0, other arithmetic: 14.2 us -> none  [the longest x2 5.53 us: norm_back(): jnp.sum(upstream * normed, axis=0)]
  transfers between devices with their start and end apart: 11 -> 0, of which waited for: 11 -> 0; matrix products, arithmetic and copies ran while one was open for 2% -> 0% of each run, Pallas kernels for 0% -> 0%
where the time goes in v2:
time: 431 us; the launch traced here: 422 us
  Pallas kernels  406 us (94%)
  local copies, waits for them, and re-layouts  14.8 us (3%)
    pallas_call x1, Pallas kernels, middle(): pl.pallas_call(middle_kernel, out_shape=(jax.ShapeDtypeStruct((slots, wid...  175 us
    pallas_call x1, Pallas kernels, final(): pl.pallas_call(functools.partial(final_kernel, bits=bits, pieces=pieces),...  108 us
    pallas_call x1, Pallas kernels, attention_backward(): pl.pallas_call(attention_backward_kernel, out_shape=(jax.ShapeDtypeStruct...  70.2 us
    pallas_call x1, Pallas kernels, attention_forward(): pl.pallas_call(attention_forward_kernel, out_shape=(jax.ShapeDtypeStruct(...  52.5 us
    unnamed x24, local copies, waits for them, and re-layouts  11.9 us

profile of v2, /device:TPU:1, one launch (start us, length us, event | category | flops | bytes accessed | tf_op | source)
XLA Modules:
  0.0 422.3 jit_solution(13075315607384057673)
XLA Ops:
  1.3 1.3 pad.4.row_ref
  2.6 1.6 copy.34
  4.1 52.5 %attention_forward.1 = (bf16[576,256]{1,0:T(8,128)(2,1)}, bf16[576,256]{1,0:T(8,128)(2,1)}, bf16[576,256]{1,0:T(8,128)(2,1)}, bf16[384,256]{1,0:T(8,128)(2,1)}, ...) custom-call(s32[1]{0:T(128)S(6)} %copy.44.length_ref, bf16[576,1024]{1,0:T(8,128)(2,1)} %tok_ref.5, ...), custom_call_target="tpu_custom_call" | custom-call | tf_op jit(solution)/shard_map/attention_forward/pallas_call | solution.py:132
  56.7 174.9 %middle.1 = (bf16[576,1024]{1,0:T(8,128)(2,1)}, f32[576,1024]{1,0:T(8,128)}, bf16[576,1024]{1,0:T(8,128)(2,1)}, bf16[576,1024]{1,0:T(8,128)(2,1)}, bf16[576,1024...) custom-call(bf16[576,256]{1,0:T(8,128)(2,1)} %get-tuple-element.46.ctx_ref, ...), custom_call_target="tpu_custom_call" | custom-call | tf_op jit(solution)/shard_map/middle/pallas_call | solution.py:560
  231.5 70.2 %attention_backward.1 = (f32[1024,256]{1,0:T(8,128)}, f32[1024,256]{1,0:T(8,128)}, f32[1024,256]{1,0:T(8,128)}, f32[1024,256]{1,0:T(8,128)}, f32[576,1024]{1,0:T(8,128)}, /*index=5*/f32[384,1024]{1,0:T(8,128)}) custom-call(bf16[576,1024]{1,0:T(8,128)(2,1)} %get-tuple-element.48.grad_ref, bf16[576,1024]{1,0:T(8,128)(2,1)} %tok_ref.5, ...), custom_call_target="tpu_custom_call" | custom-call | tf_op jit(solution)/shard_map/attention_backward/pallas_call | solution.py:293
  301.8 108.1 %final.1 = (bf16[9,64,1024]{2,1,0:T(8,128)(2,1)}, f32[128,256]{1,0:T(8,128)}, f32[128,256]{1,0:T(8,128)}, f32[128,256]{1,0:T(8,128)}, f32[128,256]{1,0:T(8,128)}...) custom-call(f32[9,64,1024]{2,1,0:T(8,128)} %bitcast.32, ...), custom_call_target="tpu_custom_call" | custom-call | tf_op jit(solution)/shard_map/final/pallas_call | solution.py:813
  409.9 0.0 copy-start.1
  409.9 1.6 fusion
  411.5 1.7 copy.35
  413.2 2.0 copy.36
  415.2 0.0 copy-done.1
  415.2 0.0 copy-start.2
  415.2 1.0 copy.45
  416.2 0.7 copy-done.2
  416.9 0.0 copy-start.6
  416.9 0.0 copy-start.5
  416.9 0.0 copy-start.4
  416.9 0.0 copy-start.3
  416.9 1.0 copy.46
  418.0 0.0 copy-done.6
  418.0 0.0 copy-start
  418.0 0.7 copy.47
  418.6 0.0 copy-done.5
  418.6 0.7 copy.48
  419.3 0.0 copy-done.4
  419.3 0.7 copy.49
  419.9 0.0 copy-done.3
  419.9 0.8 copy.50
  420.7 0.0 copy-done
  420.7 1.1 copy.51
Async XLA Ops:
  409.9 5.3 %copy-start.1 = (bf16[576,1024]{1,0:T(8,128)(2,1)S(1)}, bf16[576,1024]{1,0:T(8,128)(2,1)}, u32[]{:S(2)}) copy-start(bf16[576,1024]{1,0:T(8,128)(2,1)} %get-tuple-element.115) | copy-start | bytes 3538948
  415.2 1.7 copy-start.2
  416.9 1.0 copy-start.6
  416.9 1.7 copy-start.5
  416.9 2.3 copy-start.4
  416.9 3.0 copy-start.3
  418.0 2.8 copy-start

commit v3 on v2

--- a/solution.py
+++ b/solution.py
@@ -31,135 +31,391 @@
     return jnp.take_along_axis(table, index, axis=1, mode="promise_in_bounds")
 
 
-def attention_forward_kernel(
-    length_ref, tok_ref, wq_ref, wk_ref, wv_ref, rel_ref, col_ref, row_ref,
-    q_ref, k_ref, v_ref, krel_ref, qrel_ref, attend_ref, ctx_ref,
-    idx_ref, log_ref, col_part_ref, tq_ref, tk_ref, kv_ref,
-):
+def bucket(step):
+    return jnp.clip(step, -(NB // 2), NB // 2 - 1) + NB // 2
+
+
+def attention_setup(tok_ref, wq_ref, wk_ref, wv_ref, rel_ref, col_ref, row_ref,
+                    q_ref, k_ref, v_ref, krel_ref, qrel_ref, tq_ref, tk_ref, idx_ref):
     slots = tok_ref.shape[0]
-    wide = row_ref.shape[1]
-    heads = wq_ref.shape[1] // HEAD
-    chunks = wide // LANES
-    scale = (7.0 * HEAD) ** (-0.5)
-    tok = tok_ref[...]
-    q_ref[...] = dot_nn(tok, wq_ref[...]).astype(jnp.bfloat16)
-    k_ref[...] = dot_nn(tok, wk_ref[...]).astype(jnp.bfloat16)
-    v_ref[...] = dot_nn(tok, wv_ref[...]).astype(jnp.bfloat16)
-    rel = rel_ref[...]
-    krel_ref[...] = dot_nn(rel, wk_ref[...]).astype(jnp.bfloat16)
-    qrel_ref[...] = dot_nn(rel, wq_ref[...]).astype(jnp.bfloat16)
-    kv_ref[...] = jnp.zeros_like(kv_ref)
-    kv_ref[0, :slots, :] = k_ref[...]
-    kv_ref[1, :slots, :] = v_ref[...]
-    if wide > slots:
-        col_part_ref[slots:, :] = jnp.zeros((wide - slots, wide), jnp.float32)
-
-    block = 32
-    length = length_ref[0]
+    heads, wide = q_ref.shape[0], q_ref.shape[1]
+    low = jnp.bfloat16
+    for weight, target in ((wq_ref, q_ref), (wk_ref, k_ref), (wv_ref, v_ref)):
+        value = dot_nn(tok_ref[...], weight[...]).astype(low)
+        for head in range(heads):
+            target[head, :slots, :] = value[:, head * HEAD : (head + 1) * HEAD]
+            if wide > slots:
+                target[head, slots:, :] = jnp.zeros((wide - slots, HEAD), low)
+    for weight, target in ((wk_ref, krel_ref), (wq_ref, qrel_ref)):
+        value = dot_nn(rel_ref[...], weight[...]).astype(low)
+        for head in range(heads):
+            target[head] = value[:, head * HEAD : (head + 1) * HEAD]
+    for head in range(heads):
+        tq_ref[head] = dot_nt(q_ref[head], krel_ref[head])
+        tk_ref[head] = dot_nt(k_ref[head], qrel_ref[head])
+
+    block = 64
 
     @pl.loop(0, slots // block)
     def _(step):
         at = pl.ds(pl.multiple_of(step * block, block), block)
         for kind in range(2):
-            own = col_ref[at, kind : kind + 1]
-            other = row_ref[kind : kind + 1, :]
-            bucket = jnp.clip((own - other) >> 3, -(NB // 2), NB // 2 - 1) + NB // 2
-            idx_ref[kind, at, :] = bucket
-
-    for head in range(heads):
-        cols = slice(head * HEAD, (head + 1) * HEAD)
-        q_h = q_ref[:, cols]
-        tq_ref[...] = dot_nt(q_h, krel_ref[:, cols])
-        tk_ref[...] = dot_nt(k_ref[:, cols], qrel_ref[:, cols])
-        log_ref[...] = dot_nt(q_h, kv_ref[0, :, cols])
-
-        for big in range(chunks):
-            rows_here = min(LANES, slots - big * LANES)
-
-            @pl.loop(0, rows_here // block)
-            def _(step, big=big):
-                start = pl.multiple_of(big * LANES + step * block, block)
-                at = pl.ds(start, block)
-                tq = [tq_ref[at, t * NB : (t + 1) * NB] for t in range(3)]
-                tk = [tk_ref[at, t * NB : (t + 1) * NB] for t in range(3)]
-                for chunk in range(chunks):
-                    lanes = slice(chunk * LANES, (chunk + 1) * LANES)
-                    if big - chunk >= 2:
-                        far = NB - 1
-                        s1, s2 = tq[0][:, far : far + 1], tk[0][:, far : far + 1]
-                    elif chunk - big >= 2:
-                        s1, s2 = tq[0][:, 0:1], tk[0][:, 0:1]
-                    else:
-                        i_at = lax.broadcasted_iota(jnp.int32, (block, LANES), 0) + start
-                        j_at = lax.broadcasted_iota(jnp.int32, (block, LANES), 1) + chunk * LANES
-                        near = jnp.clip(i_at - j_at, -(NB // 2), NB // 2 - 1) + NB // 2
-                        s1, s2 = lane_gather(tq[0], near), lane_gather(tk[0], near)
-                    for kind in range(2):
-                        index = idx_ref[kind, at, lanes]
-                        s1 = s1 + lane_gather(tq[kind + 1], index)
-                        s2 = s2 + lane_gather(tk[kind + 1], index)
-                    log_ref[at, lanes] += s1
-                    col_part_ref[at, lanes] = s2
-
-        for big in range(chunks):
-            rows_here = min(LANES, slots - big * LANES)
-            at = slice(big * LANES, big * LANES + rows_here)
-            for chunk in range(chunks):
-                lanes = slice(chunk * LANES, (chunk + 1) * LANES)
-                turned = col_part_ref[lanes, big * LANES : (big + 1) * LANES].T
-                log_ref[at, lanes] += turned[:rows_here]
-
-        @pl.loop(0, slots // block)
-        def _(step, head=head):
-            at = pl.ds(pl.multiple_of(step * block, block), block)
+            own = jnp.broadcast_to(col_ref[at, kind : kind + 1], (block, LANES))
+            for chunk in range(wide // LANES):
+                other = row_ref[kind : kind + 1, chunk * LANES : (chunk + 1) * LANES]
+                idx_ref[kind, chunk, at, :] = bucket((own - other) >> 3)
+
+    if wide > slots:
+        idx_ref[:, :, slots:, :] = jnp.zeros_like(idx_ref[:, :, slots:, :])
+
+
+def attention_block(big, length, q_ref, k_ref, v_ref, tq_ref, tk_ref, idx_ref, log_ref, attend_ref, ctx_ref):
+    heads, wide = q_ref.shape[0], q_ref.shape[1]
+    chunks = wide // LANES
+    slots = attend_ref.shape[1]
+    scale = (7.0 * HEAD) ** (-0.5)
+    rows = min(LANES, slots - big * LANES)
+    here = slice(big * LANES, (big + 1) * LANES)
+    some = slice(big * LANES, big * LANES + rows)
+    slant = lax.broadcasted_iota(jnp.int32, (LANES, LANES), 0) - lax.broadcasted_iota(
+        jnp.int32, (LANES, LANES), 1
+    )
+
+    @pl.loop(0, heads)
+    def _(head):
+        log_ref[:rows, :] = dot_nt(q_ref[head, some, :], k_ref[head])
+        for chunk in range(chunks):
+            there = slice(chunk * LANES, (chunk + 1) * LANES)
+            away = (big - chunk) * LANES
+            toward = log_ref[:rows, there]
+            if abs(big - chunk) >= 2:
+                lane = NB - 1 if away > 0 else 0
+                toward = toward + tq_ref[head, some, lane : lane + 1]
+                lane = NB - 1 - lane
+                beside = jnp.broadcast_to(tk_ref[head, there, lane : lane + 1], (LANES, LANES))
+            else:
+                toward = toward + lane_gather(tq_ref[head, some, :NB], bucket(slant + away)[:rows])
+                beside = lane_gather(tk_ref[head, there, :NB], bucket(slant - away))
+            for kind in range(2):
+                lanes = slice((kind + 1) * NB, (kind + 2) * NB)
+                toward = toward + lane_gather(tq_ref[head, some, lanes], idx_ref[kind, chunk, some, :])
+                beside = beside + lane_gather(tk_ref[head, there, lanes], idx_ref[kind, big, there, :])
+            log_ref[:rows, there] = toward + beside.T[:rows]
+        block = 32
+        for start in range(0, rows, block):
+            at = slice(start, start + block)
             j_at = lax.broadcasted_iota(jnp.int32, (block, wide), 1)
-            masked = jnp.where(j_at < length, log_ref[at, :] * scale, NEG_FILL)
+            masked = jnp.where(j_at < length, log_ref[at, :], NEG_FILL)
             peak = jnp.max(masked, axis=-1, keepdims=True)
-            grown = jnp.exp(masked - peak)
+            grown = jnp.exp((masked - peak) * scale)
             total = jnp.sum(grown, axis=-1, keepdims=True)
-            attend_ref[head, at, :] = (grown / total).astype(jnp.bfloat16)
-
-        ctx_ref[:, cols] = dot_nn(attend_ref[head], kv_ref[1, :, cols]).astype(jnp.bfloat16)
-
-
-def attention_forward(tokens, length, corner_col, corner_row, w_query, w_key, w_value, rel):
+            attend_ref[head, big * LANES + start : big * LANES + start + block, :] = (
+                grown * (1.0 / total)
+            ).astype(jnp.bfloat16)
+        ctx_ref[head, some, :] = dot_nn(attend_ref[head, some, :], v_ref[head]).astype(jnp.bfloat16)
+
+
+MESH = pl.DeviceIdType.MESH
+
+
+class Line:
+    def __init__(self, axis, own, inner, outer, sems):
+        self.axis, self.own, self.inner, self.outer = axis, own, inner, outer
+        self.in_send, self.in_recv, self.out_send, self.out_recv = sems
+        self.ring = own.shape[0]
+        self.n = lax.axis_size(axis)
+        me = lax.axis_index(axis)
+        left = me < self.n // 2
+        self.depth = jnp.where(left, me, self.n - 1 - me)
+        self.inward = jnp.where(left, me + 1, me - 1)
+        self.outward = jnp.where(self.depth == 0, self.inward, jnp.where(left, me - 1, me + 1))
+        self.last = self.n // 2 - 1
+
+    def greet(self, barrier):
+        pl.semaphore_signal(barrier, inc=1, device_id={self.axis: self.inward}, device_id_type=MESH)
+
+        @pl.when(self.depth > 0)
+        def _():
+            pl.semaphore_signal(
+                barrier, inc=1, device_id={self.axis: self.outward}, device_id_type=MESH
+            )
+
+    def greeted(self):
+        return jnp.where(self.depth > 0, 2, 1)
+
+    def copy(self, source, target, send, recv, to):
+        return pltpu.make_async_remote_copy(
+            src_ref=source,
+            dst_ref=target,
+            send_sem=send,
+            recv_sem=recv,
+            device_id={self.axis: to},
+            device_id_type=MESH,
+        )
+
+    def out_copy(self, u):
+        return self.copy(
+            self.outer.at[u], self.outer.at[u], self.out_send.at[u], self.out_recv.at[u], self.outward
+        )
+
+    def in_copy(self, c, source):
+        return self.copy(
+            source, self.inner.at[c], self.in_send.at[c], self.in_recv.at[c], self.inward
+        )
+
+    def send_in(self, u, c, source):
+        @pl.when(self.depth < self.last)
+        def _():
+            self.in_copy(c, source).start()
+
+        @pl.when(self.depth == self.last)
+        def _():
+            self.copy(
+                source, self.outer.at[u], self.in_send.at[c], self.out_recv.at[u], self.inward
+            ).start()
+
+    def step(self, slot, count):
+        here = slot - self.depth
+
+        @pl.when((here >= 0) & (here < count))
+        def _():
+            u = here
+            c = lax.rem(u, self.ring)
+
+            @pl.when(self.depth == 0)
+            def _():
+                self.send_in(u, c, self.own.at[c])
+
+            @pl.when(self.depth > 0)
+            def _():
+                self.in_copy(c, self.own.at[c]).wait_recv()
+                self.inner[c] += self.own[c]
+                self.send_in(u, c, self.inner.at[c])
+
+        back = slot - (self.n - 1 - self.depth)
+
+        @pl.when((back >= 0) & (back < count))
+        def _():
+            u = back
+            c = lax.rem(u, self.ring)
+            self.in_copy(c, self.own.at[c]).wait_send()
+            self.out_copy(u).wait_recv()
+
+            @pl.when(self.depth == self.last)
+            def _():
+                self.outer[u] += self.inner[c] if self.last > 0 else self.own[c]
+
+            @pl.when(self.depth > 0)
+            def _():
+                self.out_copy(u).start()
+
+    def drain(self, count):
+        @pl.when(self.depth > 0)
+        def _():
+            @pl.loop(0, count)
+            def _(u):
+                self.out_copy(u).wait_send()
+
+
+def centre(values):
+    average = jnp.mean(values, axis=-1, keepdims=True)
+    centered = values - average
+    spread = jnp.mean(centered * centered, axis=-1, keepdims=True)
+    scaling = lax.rsqrt(spread + 1e-05)
+    return centered * scaling, scaling
+
+
+def norm_inward(scaled, normed, scaling):
+    return scaling * (
+        scaled
+        - jnp.mean(scaled, axis=-1, keepdims=True)
+        - normed * jnp.mean(scaled * normed, axis=-1, keepdims=True)
+    )
+
+
+def fold_rows(values):
+    rows, width = values.shape
+    return jnp.sum(values.reshape(rows // 8, 8, width), axis=0)
+
+
+CHUNK = 64
+
+
+def layer_kernel(
+    length_ref, tok_ref, wq_ref, wk_ref, wv_ref, rel_ref, col_ref, row_ref,
+    wo_ref, cot_ref, wi_ref, wu_ref, bo_ref, ga_ref, sa_ref, bi_ref, bu_ref, gf_ref, sf_ref,
+    q_ref, k_ref, v_ref, krel_ref, qrel_ref, attend_ref, ctx_ref,
+    out_ref, grad_ref, grad_low_ref, hidden_ref, active_ref, mid_low_ref, inner_low_ref, small_ref,
+    tq_ref, tk_ref, idx_ref, log_ref,
+    own, inner, outer, normed_ref, scale_ref, pre_ref, sums_ref,
+    in_send, in_recv, out_send, out_recv,
+):
+    slots = tok_ref.shape[0]
+    chunks = slots // CHUNK
+    heads, wide = q_ref.shape[0], q_ref.shape[1]
+    low, full = jnp.bfloat16, jnp.float32
+    line = Line("head", own, inner, outer, (in_send, in_recv, out_send, out_recv))
+    barrier = pltpu.get_barrier_semaphore()
+    line.greet(barrier)
+    sums_ref[...] = jnp.zeros_like(sums_ref)
+    attention_setup(tok_ref, wq_ref, wk_ref, wv_ref, rel_ref, col_ref, row_ref,
+                    q_ref, k_ref, v_ref, krel_ref, qrel_ref, tq_ref, tk_ref, idx_ref)
+    pl.semaphore_wait(barrier, line.greeted())
+    root = 0.5**0.5
+    bell = (0.5 / jnp.pi) ** 0.5
+
+    def rows(c):
+        return pl.ds(pl.multiple_of(c * CHUNK, CHUNK), CHUNK)
+
+    def project(c):
+        context = jnp.concatenate([ctx_ref[head, rows(c), :] for head in range(heads)], axis=1)
+        own[c] = dot_nn(context, wo_ref[...])
+
+    def after_attention(c, u):
+        at = rows(c)
+        normed, scaling = centre(outer[u] + bo_ref[...] + tok_ref[at, :].astype(full))
+        normed_ref[at, :] = normed
+        scale_ref[at, :] = scaling
+        hidden_low = (normed * ga_ref[...] + sa_ref[...]).astype(low)
+        hidden_ref[at, :] = hidden_low
+        pre = dot_nn(hidden_low, wi_ref[...]) + bi_ref[...]
+        pre_ref[at, :] = pre
+        active = (pre * (1.0 + lax.erf(pre * root)) * 0.5).astype(low)
+        active_ref[at, :] = active
+        own[c] = dot_nn(active, wu_ref[...])
+
+    def after_ffn(c, u):
+        at = rows(c)
+        hidden = normed_ref[at, :] * ga_ref[...] + sa_ref[...]
+        normed, scaling = centre(outer[u] + bu_ref[...] + hidden)
+        out_ref[at, :] = (normed * gf_ref[...] + sf_ref[...]).astype(low)
+        upstream = cot_ref[at, :].astype(full)
+        grad_mid = norm_inward(upstream * gf_ref[...], normed, scaling)
+        sums_ref[4] += fold_rows(grad_mid)
+        sums_ref[5] += fold_rows(upstream * normed)
+        sums_ref[6] += fold_rows(upstream)
+        grad_ref[c] = grad_mid
+        mid_low = grad_mid.astype(low)
+        mid_low_ref[at, :] = mid_low
+        grad_active = dot_nt(mid_low, wu_ref[...])
+        pre = pre_ref[at, :]
+        slope = (1.0 + lax.erf(pre * root)) * 0.5 + pre * jnp.exp(-0.5 * pre * pre) * bell
+        inner_low = (grad_active * slope).astype(low)
+        sums_ref[3] += fold_rows(inner_low.astype(full))
+        inner_low_ref[at, :] = inner_low
+        own[c] = dot_nt(inner_low, wi_ref[...])
+
+    def after_hidden(c, u):
+        at = rows(c)
+        upstream = outer[u] + grad_ref[c]
+        normed = normed_ref[at, :]
+        grad_attn = norm_inward(upstream * ga_ref[...], normed, scale_ref[at, :])
+        sums_ref[0] += fold_rows(grad_attn)
+        sums_ref[1] += fold_rows(upstream * normed)
+        sums_ref[2] += fold_rows(upstream)
+        grad_ref[c] = grad_attn
+        grad_low_ref[at, :] = grad_attn.astype(low)
+
+    per = LANES // CHUNK
+
+    @pl.loop(0, 3 * chunks + line.n - 1)
+    def _(slot):
+        for big in range(wide // LANES):
+
+            @pl.when(slot == big * per)
+            def _(big=big):
+                attention_block(big, length_ref[0], q_ref, k_ref, v_ref, tq_ref, tk_ref, idx_ref, log_ref,
+                                attend_ref, ctx_ref)
+
+        @pl.when(slot < chunks)
+        def _():
+            project(slot)
+
+        line.step(slot, 3 * chunks)
+        done = slot - (line.n - 1)
+
+        @pl.when((done >= 0) & (done < chunks))
+        def _():
+            after_attention(done, done)
+
+        @pl.when((done >= chunks) & (done < 2 * chunks))
+        def _():
+            after_ffn(done - chunks, done)
+
+        @pl.when(done >= 2 * chunks)
+        def _():
+            after_hidden(done - 2 * chunks, done)
+
+    for at in range(7):
+        small_ref[at : at + 1, :] = jnp.sum(sums_ref[at], axis=0, keepdims=True)
+    small_ref[7:8, :] = jnp.zeros_like(small_ref[7:8, :])
+    line.drain(3 * chunks)
+
+
+def layer(tokens, length, corner_col, corner_row, w_query, w_key, w_value, rel, w_output, cotangent, w_inner, w_outer, vectors):
     slots, width = tokens.shape
+    units = w_inner.shape[1]
     mine = w_query.shape[1]
     heads = mine // HEAD
     wide = corner_row.shape[1]
-    low = jnp.bfloat16
+    assert units == width
+    low, full = jnp.bfloat16, jnp.float32
     vmem = pl.BlockSpec(memory_space=pltpu.VMEM)
+    chunks = slots // CHUNK
+    steps = 3 * chunks
+    shape = jax.ShapeDtypeStruct
+    dma = pltpu.SemaphoreType.DMA
     return pl.pallas_call(
-        attention_forward_kernel,
+        layer_kernel,
         out_shape=(
-            jax.ShapeDtypeStruct((slots, mine), low),
-            jax.ShapeDtypeStruct((slots, mine), low),
-            jax.ShapeDtypeStruct((slots, mine), low),
-            jax.ShapeDtypeStruct((3 * NB, mine), low),
-            jax.ShapeDtypeStruct((3 * NB, mine), low),
-            jax.ShapeDtypeStruct((heads, slots, wide), low),
-            jax.ShapeDtypeStruct((slots, mine), low),
+            shape((heads, wide, HEAD), low),
+            shape((heads, wide, HEAD), low),
+            shape((heads, wide, HEAD), low),
+            shape((heads, 3 * NB, HEAD), low),
+            shape((heads, 3 * NB, HEAD), low),
+            shape((heads, slots, wide), low),
+            shape((heads, slots, HEAD), low),
+            shape((slots, width), low),
+            shape((chunks, CHUNK, width), full),
+            shape((slots, width), low),
+            shape((slots, width), low),
+            shape((slots, units), low),
+            shape((slots, width), low),
+            shape((slots, units), low),
+            shape((8, width), full),
         ),
-        in_specs=[pl.BlockSpec(memory_space=pltpu.SMEM)] + [vmem] * 7,
-        out_specs=(vmem,) * 7,
+        in_specs=[pl.BlockSpec(memory_space=pltpu.SMEM)] + [vmem] * 18,
+        out_specs=(vmem,) * 15,
         scratch_shapes=[
-            pltpu.VMEM((2, slots, wide), jnp.int32),
-            pltpu.VMEM((slots, wide), jnp.float32),
-            pltpu.VMEM((wide, wide), jnp.float32),
-            pltpu.VMEM((slots, 3 * NB), jnp.float32),
-            pltpu.VMEM((slots, 3 * NB), jnp.float32),
-            pltpu.VMEM((2, wide, mine), low),
+            pltpu.VMEM((heads, wide, 3 * NB), full),
+            pltpu.VMEM((heads, wide, 3 * NB), full),
+            pltpu.VMEM((2, wide // LANES, wide, LANES), jnp.int32),
+            pltpu.VMEM((LANES, wide), full),
+            pltpu.VMEM((chunks, CHUNK, width), full),
+            pltpu.VMEM((chunks, CHUNK, width), full),
+            pltpu.VMEM((steps, CHUNK, width), full),
+            pltpu.VMEM((slots, width), full),
+            pltpu.VMEM((slots, 1), full),
+            pltpu.VMEM((slots, units), full),
+            pltpu.VMEM((7, 8, width), full),
+            dma((chunks,)),
+            dma((chunks,)),
+            dma((steps,)),
+            dma((steps,)),
         ],
-        compiler_params=pltpu.CompilerParams(vmem_limit_bytes=VMEM_LIMIT),
-        name="attention_forward",
-    )(length, tokens, w_query, w_key, w_value, rel, corner_col, corner_row)
+        compiler_params=pltpu.CompilerParams(
+            vmem_limit_bytes=VMEM_LIMIT, collective_id=1, has_side_effects=True
+        ),
+        name="layer",
+    )(length, tokens, w_query, w_key, w_value, rel, corner_col, corner_row,
+      w_output, cotangent, w_inner, w_outer, *[v.reshape(1, -1) for v in vectors])
 
 
 def attention_backward_kernel(
     grad_ref, tok_ref, wq_ref, wk_ref, wv_ref, wo_ref, rel_ref, col_ref,
     q_ref, k_ref, v_ref, krel_ref, qrel_ref, attend_ref, ctx_ref,
     gwq_ref, gwk_ref, gwv_ref, gwo_ref, gin_ref, grel_ref,
-    gc_ref, step_ref, kv_ref, mat_ref, fold_ref, hist_ref, gq_ref, gk_ref, gv_ref,
+    gc_ref, step_ref, mat_ref, fold_ref, hist_ref, gq_ref, gk_ref, gv_ref,
     gkrel_ref, gqrel_ref,
 ):
     slots = tok_ref.shape[0]
@@ -170,10 +426,9 @@
     low = jnp.bfloat16
     block = 32
     gc_ref[...] = dot_nt(grad_ref[...], wo_ref[...]).astype(low)
-    gwo_ref[...] = dot_tn(grad_ref[...], ctx_ref[...])
-    kv_ref[...] = jnp.zeros_like(kv_ref)
-    kv_ref[0, :slots, :] = k_ref[...]
-    kv_ref[1, :slots, :] = v_ref[...]
+    gwo_ref[...] = dot_tn(
+        grad_ref[...], jnp.concatenate([ctx_ref[head] for head in range(heads)], axis=1)
+    )
     mat_ref[...] = jnp.zeros_like(mat_ref)
     step_ref[...] = jnp.zeros_like(step_ref)
 
@@ -190,8 +445,8 @@
     for head in range(heads):
         cols = slice(head * HEAD, (head + 1) * HEAD)
         gc_h = gc_ref[:, cols]
-        grad_attend = dot_nt(gc_h, kv_ref[1, :, cols])
-        mean = jnp.sum(gc_h.astype(jnp.float32) * ctx_ref[:, cols].astype(jnp.float32), axis=-1, keepdims=True)
+        grad_attend = dot_nt(gc_h, v_ref[head])
+        mean = jnp.sum(gc_h.astype(jnp.float32) * ctx_ref[head].astype(jnp.float32), axis=-1, keepdims=True)
         mat_ref[0, :slots, :] = (attend_ref[head].astype(jnp.float32) * (grad_attend - mean)).astype(low)
         gv_ref[:, cols] = dot_tn(attend_ref[head], gc_h)[:slots].astype(low)
         for big in range(chunks):
@@ -262,9 +517,9 @@
                         found = found - jnp.where(lane == NB - 1, 0.0, following)
                         hist_ref[side, at, (kind + 1) * NB : (kind + 2) * NB] = found.astype(low)
 
-        q_h, k_h = q_ref[:, cols], k_ref[:, cols]
-        gq = dot_nn(mat_ref[0, :slots, :], kv_ref[0, :, cols]) + dot_nn(hist_ref[0], krel_ref[:, cols])
-        gk = dot_nn(mat_ref[1, :slots, :slots], q_h) + dot_nn(hist_ref[1], qrel_ref[:, cols])
+        q_h, k_h = q_ref[head, :slots, :], k_ref[head, :slots, :]
+        gq = dot_nn(mat_ref[0, :slots, :], k_ref[head]) + dot_nn(hist_ref[0], krel_ref[head])
+        gk = dot_nn(mat_ref[1, :slots, :slots], q_h) + dot_nn(hist_ref[1], qrel_ref[head])
         gq_ref[:, cols] = (gq * scale).astype(low)
         gk_ref[:, cols] = (gk * scale).astype(low)
         gkrel_ref[:, cols] = (dot_tn(hist_ref[0], q_h) * scale).astype(low)
@@ -305,7 +560,6 @@
         scratch_shapes=[
             pltpu.VMEM((slots, mine), low),
             pltpu.VMEM((2, wide, BOX_STEP * NB), low),
-            pltpu.VMEM((2, wide, mine), low),
             pltpu.VMEM((2, wide, wide), low),
             pltpu.VMEM((2, slots, BOX_STEP * NB), full),
             pltpu.VMEM((2, slots, 3 * NB), low),
@@ -318,275 +572,6 @@
         compiler_params=pltpu.CompilerParams(vmem_limit_bytes=VMEM_LIMIT),
         name="attention_backward",
     )(grad, tokens, w_query, w_key, w_value, w_output, rel, corner_col, q, k, v, krel, qrel, attend, ctx)
-
-
-MESH = pl.DeviceIdType.MESH
-
-
-class Line:
-    def __init__(self, axis, own, inner, outer, sems):
-        self.axis, self.own, self.inner, self.outer = axis, own, inner, outer
-        self.in_send, self.in_recv, self.out_send, self.out_recv = sems
-        self.n = lax.axis_size(axis)
-        me = lax.axis_index(axis)
-        left = me < self.n // 2
-        self.depth = jnp.where(left, me, self.n - 1 - me)
-        self.inward = jnp.where(left, me + 1, me - 1)
-        self.outward = jnp.where(self.depth == 0, self.inward, jnp.where(left, me - 1, me + 1))
-        self.last = self.n // 2 - 1
-
-    def greet(self, barrier):
-        pl.semaphore_signal(barrier, inc=1, device_id={self.axis: self.inward}, device_id_type=MESH)
-
-        @pl.when(self.depth > 0)
-        def _():
-            pl.semaphore_signal(
-                barrier, inc=1, device_id={self.axis: self.outward}, device_id_type=MESH
-            )
-
-    def greeted(self):
-        return jnp.where(self.depth > 0, 2, 1)
-
-    def copy(self, source, target, send, recv, to):
-        return pltpu.make_async_remote_copy(
-            src_ref=source,
-            dst_ref=target,
-            send_sem=send,
-            recv_sem=recv,
-            device_id={self.axis: to},
-            device_id_type=MESH,
-        )
-
-    def send_in(self, u, source):
-        @pl.when(self.depth < self.last)
-        def _():
-            self.copy(
-                source, self.inner.at[u], self.in_send.at[u], self.in_recv.at[u], self.inward
-            ).start()
-
-        @pl.when(self.depth == self.last)
-        def _():
-            self.copy(
-                source, self.outer.at[u], self.in_send.at[u], self.out_recv.at[u], self.inward
-            ).start()
-
-    def step(self, slot, count):
-        here = slot - self.depth
-
-        @pl.when((here >= 0) & (here < count))
-        def _():
-            u = here
-
-            @pl.when(self.depth == 0)
-            def _():
-                self.send_in(u, self.own.at[u])
-
-            @pl.when(self.depth > 0)
-            def _():
-                self.copy(
-                    self.own.at[u], self.inner.at[u], self.in_send.at[u], self.in_recv.at[u], self.inward
-                ).wait_recv()
-                self.inner[u] += self.own[u]
-                self.send_in(u, self.inner.at[u])
-
-        back = slot - (self.n - 1 - self.depth)
-
-        @pl.when((back >= 0) & (back < count))
-        def _():
-            u = back
-            self.copy(
-                self.own.at[u], self.outer.at[u], self.out_send.at[u], self.out_recv.at[u], self.outward
-            ).wait_recv()
-
-            @pl.when(self.depth == self.last)
-            def _():
-                self.outer[u] += self.inner[u] if self.last > 0 else self.own[u]
-
-            @pl.when(self.depth > 0)
-            def _():
-                self.copy(
-                    self.outer.at[u],
-                    self.outer.at[u],
-                    self.out_send.at[u],
-                    self.out_recv.at[u],
-                    self.outward,
-                ).start()
-
-    def drain(self, count):
-        @pl.loop(0, count)
-        def _(u):
-            self.copy(
-                self.own.at[u], self.inner.at[u], self.in_send.at[u], self.in_recv.at[u], self.inward
-            ).wait_send()
-
-            @pl.when(self.depth > 0)
-            def _():
-                self.copy(
-                    self.outer.at[u],
-                    self.outer.at[u],
-                    self.out_send.at[u],
-                    self.out_recv.at[u],
-                    self.outward,
-                ).wait_send()
-
-
-def centre(values):
-    average = jnp.mean(values, axis=-1, keepdims=True)
-    centered = values - average
-    spread = jnp.mean(centered * centered, axis=-1, keepdims=True)
-    scaling = lax.rsqrt(spread + 1e-05)
-    return centered * scaling, scaling
-
-
-def norm_inward(scaled, normed, scaling):
-    return scaling * (
-        scaled
-        - jnp.mean(scaled, axis=-1, keepdims=True)
-        - normed * jnp.mean(scaled * normed, axis=-1, keepdims=True)
-    )
-
-
-def fold_rows(values):
-    rows, width = values.shape
-    return jnp.sum(values.reshape(rows // 8, 8, width), axis=0)
-
-
-CHUNK = 64
-
-
-def middle_kernel(
-    ctx_ref, wo_ref, tok_ref, cot_ref, wi_ref, wu_ref,
-    bo_ref, ga_ref, sa_ref, bi_ref, bu_ref, gf_ref, sf_ref,
-    out_ref, grad_ref, grad_low_ref, hidden_ref, active_ref, mid_low_ref, inner_low_ref, small_ref,
-    own, inner, outer, normed_ref, scale_ref, pre_ref, mid_ref, sums_ref,
-    in_send, in_recv, out_send, out_recv,
-):
-    slots = tok_ref.shape[0]
-    chunks = slots // CHUNK
-    low, full = jnp.bfloat16, jnp.float32
-    line = Line("head", own, inner, outer, (in_send, in_recv, out_send, out_recv))
-    barrier = pltpu.get_barrier_semaphore()
-    line.greet(barrier)
-    sums_ref[...] = jnp.zeros_like(sums_ref)
-    pl.semaphore_wait(barrier, line.greeted())
-    root = 0.5**0.5
-    bell = (0.5 / jnp.pi) ** 0.5
-
-    def rows(c):
-        return pl.ds(pl.multiple_of(c * CHUNK, CHUNK), CHUNK)
-
-    def project(c):
-        own[c] = dot_nn(ctx_ref[rows(c), :], wo_ref[...])
-
-    def after_attention(c, u):
-        at = rows(c)
-        normed, scaling = centre(outer[u] + bo_ref[...] + tok_ref[at, :].astype(full))
-        normed_ref[at, :] = normed
-        scale_ref[at, :] = scaling
-        hidden_low = (normed * ga_ref[...] + sa_ref[...]).astype(low)
-        hidden_ref[at, :] = hidden_low
-        pre = dot_nn(hidden_low, wi_ref[...]) + bi_ref[...]
-        pre_ref[at, :] = pre
-        active = (pre * (1.0 + lax.erf(pre * root)) * 0.5).astype(low)
-        active_ref[at, :] = active
-        own[u + chunks] = dot_nn(active, wu_ref[...])
-
-    def after_ffn(c, u):
-        at = rows(c)
-        hidden = normed_ref[at, :] * ga_ref[...] + sa_ref[...]
-        normed, scaling = centre(outer[u] + bu_ref[...] + hidden)
-        out_ref[at, :] = (normed * gf_ref[...] + sf_ref[...]).astype(low)
-        upstream = cot_ref[at, :].astype(full)
-        grad_mid = norm_inward(upstream * gf_ref[...], normed, scaling)
-        sums_ref[4] += fold_rows(grad_mid)
-        sums_ref[5] += fold_rows(upstream * normed)
-        sums_ref[6] += fold_rows(upstream)
-        mid_ref[at, :] = grad_mid
-        mid_low = grad_mid.astype(low)
-        mid_low_ref[at, :] = mid_low
-        grad_active = dot_nt(mid_low, wu_ref[...])
-        pre = pre_ref[at, :]
-        slope = (1.0 + lax.erf(pre * root)) * 0.5 + pre * jnp.exp(-0.5 * pre * pre) * bell
-        inner_low = (grad_active * slope).astype(low)
-        sums_ref[3] += fold_rows(inner_low.astype(full))
-        inner_low_ref[at, :] = inner_low
-        own[u + chunks] = dot_nt(inner_low, wi_ref[...])
-
-    def after_hidden(c, u):
-        at = rows(c)
-        upstream = outer[u] + mid_ref[at, :]
-        normed = normed_ref[at, :]
-        grad_attn = norm_inward(upstream * ga_ref[...], normed, scale_ref[at, :])
-        sums_ref[0] += fold_rows(grad_attn)
-        sums_ref[1] += fold_rows(upstream * normed)
-        sums_ref[2] += fold_rows(upstream)
-        grad_ref[at, :] = grad_attn
-        grad_low_ref[at, :] = grad_attn.astype(low)
-
-    @pl.loop(0, 3 * chunks + line.n - 1)
-    def _(slot):
-        @pl.when(slot < chunks)
-        def _():
-            project(slot)
-
-        line.step(slot, 3 * chunks)
-        done = slot - (line.n - 1)
-
-        @pl.when((done >= 0) & (done < chunks))
-        def _():
-            after_attention(done, done)
-
-        @pl.when((done >= chunks) & (done < 2 * chunks))
-        def _():
-            after_ffn(done - chunks, done)
-
-        @pl.when(done >= 2 * chunks)
-        def _():
-            after_hidden(done - 2 * chunks, done)
-
-    for at in range(7):
-        small_ref[at : at + 1, :] = jnp.sum(sums_ref[at], axis=0, keepdims=True)
-    small_ref[7:8, :] = jnp.zeros_like(small_ref[7:8, :])
-    line.drain(3 * chunks)
-
-
-def middle(ctx, w_output, tokens, cotangent, w_inner, w_outer, vectors):
-    slots, width = tokens.shape
-    units = w_inner.shape[1]
-    assert units == width
-    low, full = jnp.bfloat16, jnp.float32
-    vmem = pl.BlockSpec(memory_space=pltpu.VMEM)
-    steps = 3 * (slots // CHUNK)
-    return pl.pallas_call(
-        middle_kernel,
-        out_shape=(
-            jax.ShapeDtypeStruct((slots, width), low),
-            jax.ShapeDtypeStruct((slots, width), full),
-            jax.ShapeDtypeStruct((slots, width), low),
-            jax.ShapeDtypeStruct((slots, width), low),
-            jax.ShapeDtypeStruct((slots, units), low),
-            jax.ShapeDtypeStruct((slots, width), low),
-            jax.ShapeDtypeStruct((slots, units), low),
-            jax.ShapeDtypeStruct((8, width), full),
-        ),
-        in_specs=[vmem] * 13,
-        out_specs=(vmem,) * 8,
-        scratch_shapes=[
-            pltpu.VMEM((steps, CHUNK, width), full),
-            pltpu.VMEM((steps, CHUNK, width), full),
-            pltpu.VMEM((steps, CHUNK, width), full),
-            pltpu.VMEM((slots, width), full),
-            pltpu.VMEM((slots, 1), full),
-            pltpu.VMEM((slots, units), full),
-            pltpu.VMEM((slots, width), full),
-            pltpu.VMEM((7, 8, width), full),
-        ]
-        + [pltpu.SemaphoreType.DMA((steps,))] * 4,
-        compiler_params=pltpu.CompilerParams(
-            vmem_limit_bytes=VMEM_LIMIT, collective_id=1, has_side_effects=True
-        ),
-        name="middle",
-    )(ctx, w_output, tokens, cotangent, w_inner, w_outer, *[v.reshape(1, -1) for v in vectors])
 
 
 class Halving:
@@ -878,13 +863,13 @@
     rel_rows = rel_tables.reshape(3 * NB, rel_tables.shape[2])
     corner_col = corners.T
     corner_row = jnp.pad(corners, ((0, 0), (0, wide - slots_page)))
-    kept = attention_forward(
-        tokens, page_lengths, corner_col, corner_row, w_query, w_key, w_value, rel_rows
-    )
     vectors = (b_output, gain_attn, shift_attn, b_inner, b_outer, gain_ffn, shift_ffn)
-    output, grad_attn, grad_low, hidden, active, mid_low, inner_low, small = middle(
-        kept[6], w_output, tokens, cotangent, w_inner, w_outer, vectors
-    )
+    kept = layer(
+        tokens, page_lengths, corner_col, corner_row, w_query, w_key, w_value, rel_rows,
+        w_output, cotangent, w_inner, w_outer, vectors,
+    )
+    output, grad_attn, grad_low, hidden, active, mid_low, inner_low, small = kept[7:]
+    kept = kept[:7]
     grads = attention_backward(
         grad_low, tokens, w_query, w_key, w_value, w_output, rel_rows, corner_col, *kept
     )

time: 431 us -> 410 us (0.951)
  Pallas kernels: 406 us -> 385 us
    pallas_call x2 -> x1, Pallas kernels: 227 us -> 195 us  [layer(): pl.pallas_call(layer_kernel, out_shape=(shape((heads, wide, HEAD), low),...]
    pallas_call x1, Pallas kernels: 108 us -> 119 us  [final(): pl.pallas_call(functools.partial(final_kernel, bits=bits, pieces=pieces),...]
where the time goes in v3:
time: 410 us; the launch traced here: 402 us
  Pallas kernels  385 us (94%)
  local copies, waits for them, and re-layouts  15 us (4%)
    pallas_call x1, Pallas kernels, layer(): pl.pallas_call(layer_kernel, out_shape=(shape((heads, wide, HEAD), low),...  195 us
    pallas_call x1, Pallas kernels, final(): pl.pallas_call(functools.partial(final_kernel, bits=bits, pieces=pieces),...  119 us
    pallas_call x1, Pallas kernels, attention_backward(): pl.pallas_call(attention_backward_kernel, out_shape=(jax.ShapeDtypeStruct...  70.4 us
    unnamed x24, local copies, waits for them, and re-layouts  11.9 us

profile of v3, /device:TPU:1, one launch (start us, length us, event | category | flops | bytes accessed | tf_op | source)
XLA Modules:
  0.0 401.6 jit_solution(16945618449289097051)
XLA Ops:
  1.3 1.3 pad.4.row_ref
  2.6 1.6 copy.34
  4.1 195.2 %layer.1 = (bf16[4,640,64]{2,1,0:T(8,128)(2,1)}, bf16[4,640,64]{2,1,0:T(8,128)(2,1)}, bf16[4,640,64]{2,1,0:T(8,128)(2,1)}, bf16[4,384,64]{2,1,0:T(8,128)(2,1)}, ...) custom-call(s32[1]{0:T(128)S(6)} %copy.44.length_ref, ...), custom_call_target="tpu_custom_call" | custom-call | tf_op jit(solution)/shard_map/layer/pallas_call | solution.py:368
  199.3 70.4 %attention_backward.1 = (f32[1024,256]{1,0:T(8,128)}, f32[1024,256]{1,0:T(8,128)}, f32[1024,256]{1,0:T(8,128)}, f32[1024,256]{1,0:T(8,128)}, f32[576,1024]{1,0:T(8,128)}, /*index=5*/f32[384,1024]{1,0:T(8,128)}) custom-call(bf16[576,1024]{1,0:T(8,128)(2,1)} %get-tuple-element.47.grad_ref, bf16[576,1024]{1,0:T(8,128)(2,1)} %tok_ref.3, ...), custom_call_target="tpu_custom_call" | custom-call | tf_op jit(solution)/shard_map/attention_backward/pallas_call | solution.py:548
  269.7 119.2 %final.1 = (bf16[9,64,1024]{2,1,0:T(8,128)(2,1)}, f32[128,256]{1,0:T(8,128)}, f32[128,256]{1,0:T(8,128)}, f32[128,256]{1,0:T(8,128)}, f32[128,256]{1,0:T(8,128)}...) custom-call(f32[9,64,1024]{2,1,0:T(8,128)} %bitcast.30, ...), custom_call_target="tpu_custom_call" | custom-call | tf_op jit(solution)/shard_map/final/pallas_call | solution.py:798
  389.0 0.0 copy-start.1
  389.0 1.8 fusion
  390.8 1.7 copy.35
  392.4 2.0 copy.36
  394.5 0.0 copy-done.1
  394.5 0.0 copy-start.2
  394.5 1.0 copy.45
  395.5 0.7 copy-done.2
  396.2 0.0 copy-start.6
  396.2 0.0 copy-start.5
  396.2 0.0 copy-start.4
  396.2 0.0 copy-start.3
  396.2 1.0 copy.46
  397.2 0.0 copy-done.6
  397.2 0.0 copy-start
  397.2 0.7 copy.47
  397.9 0.0 copy-done.5
  397.9 0.7 copy.48
  398.5 0.0 copy-done.4
  398.5 0.7 copy.49
  399.2 0.0 copy-done.3
  399.2 0.8 copy.50
  400.0 0.0 copy-done
  400.0 1.1 copy.51
Async XLA Ops:
  389.0 5.5 %copy-start.1 = (bf16[576,1024]{1,0:T(8,128)(2,1)S(1)}, bf16[576,1024]{1,0:T(8,128)(2,1)}, u32[]{:S(2)}) copy-start(bf16[576,1024]{1,0:T(8,128)(2,1)} %get-tuple-element.115) | copy-start | bytes 3538948
  394.5 1.7 copy-start.2
  396.2 1.0 copy-start.6
  396.2 1.7 copy-start.5
  396.2 2.3 copy-start.4
  396.2 3.0 copy-start.3
  397.2 2.8 copy-start

commit v4 on v3

v4 whole, which is shorter than its diff:
```python
import functools

import jax
import jax.numpy as jnp
from jax import lax
from jax.experimental import pallas as pl
from jax.experimental.pallas import tpu as pltpu
from jax.sharding import PartitionSpec as P

HEAD = 64
NB = 128
BOX_STEP = 8
NEG_FILL = -1000000000.0
LANES = 128
HOP = 32
PAIR = 64
LAG = 2
PIECE = 256
VMEM_LIMIT = 60 * 1024 * 1024
MESH = pl.DeviceIdType.MESH
LOW = jnp.bfloat16
FULL = jnp.float32


def dot_nn(a, b):
    return lax.dot_general(a, b, (((1,), (0,)), ((), ())), preferred_element_type=FULL)


def dot_nt(a, b):
    return lax.dot_general(a, b, (((1,), (1,)), ((), ())), preferred_element_type=FULL)


def dot_tn(a, b):
    return lax.dot_general(a, b, (((0,), (0,)), ((), ())), preferred_element_type=FULL)


def lane_gather(table, index):
    return jnp.take_along_axis(table, index, axis=1, mode="promise_in_bounds")


def bucket(step):
    return jnp.clip(step, -(NB // 2), NB // 2 - 1) + NB // 2


def span(start, size):
    return pl.ds(pl.multiple_of(start, size), size)


class Line:
    def __init__(self, axis, own, inner, outer, sems, lag=LAG):
        self.axis, self.own, self.inner, self.outer, self.lag = axis, own, inner, outer, lag
        self.in_send, self.in_recv, self.out_send, self.out_recv = sems
        self.ring, self.wide_ring = own.shape[0], outer.shape[0]
        self.n = lax.axis_size(axis)
        me = lax.axis_index(axis)
        left = me < self.n // 2
        self.depth = jnp.where(left, me, self.n - 1 - me)
        self.inward = jnp.where(left, me + 1, me - 1)
        self.outward = jnp.where(self.depth == 0, self.inward, jnp.where(left, me - 1, me + 1))
        self.last = self.n // 2 - 1
        self.trip = self.lag * (self.n - 1)

    def greet(self, barrier):
        pl.semaphore_signal(barrier, inc=1, device_id={self.axis: self.inward}, device_id_type=MESH)

        @pl.when(self.depth > 0)
        def _():
            pl.semaphore_signal(
                barrier, inc=1, device_id={self.axis: self.outward}, device_id_type=MESH
            )

    def greeted(self):
        return jnp.where(self.depth > 0, 2, 1)

    def copy(self, source, target, send, recv, to):
        return pltpu.make_async_remote_copy(
            src_ref=source,
            dst_ref=target,
            send_sem=send,
            recv_sem=recv,
            device_id={self.axis: to},
            device_id_type=MESH,
        )

    def total(self, u):
        return lax.rem(u, self.wide_ring)

    def out_copy(self, u):
        o = self.total(u)
        return self.copy(
            self.outer.at[o], self.outer.at[o], self.out_send.at[o], self.out_recv.at[o], self.outward
        )

    def in_copy(self, c, source):
        return self.copy(
            source, self.inner.at[c], self.in_send.at[c], self.in_recv.at[c], self.inward
        )

    def send_in(self, u, c, source):
        @pl.when(self.depth < self.last)
        def _():
            self.in_copy(c, source).start()

        @pl.when(self.depth == self.last)
        def _():
            o = self.total(u)
            self.copy(
                source, self.outer.at[o], self.in_send.at[c], self.out_recv.at[o], self.inward
            ).start()

    def step(self, slot, count):
        here = slot - self.lag * self.depth

        @pl.when((here >= 0) & (here < count))
        def _():
            u = here
            c = lax.rem(u, self.ring)

            @pl.when(self.depth == 0)
            def _():
                self.send_in(u, c, self.own.at[c])

            @pl.when(self.depth > 0)
            def _():
                @pl.when(u >= self.ring)
                def _():
                    self.out_copy(u - self.ring).wait_send()

                self.in_copy(c, self.own.at[c]).wait_recv()
                self.inner[c] += self.own[c]
                self.send_in(u, c, self.inner.at[c])

        back = slot - self.lag * (self.n - 1 - self.depth)

        @pl.when((back >= 0) & (back < count))
        def _():
            u = back
            c = lax.rem(u, self.ring)
            self.in_copy(c, self.own.at[c]).wait_send()
            self.out_copy(u).wait_recv()

            @pl.when(self.depth == self.last)
            def _():
                self.outer[self.total(u)] += self.inner[c] if self.last > 0 else self.own[c]

            @pl.when(self.depth > 0)
            def _():
                self.out_copy(u).start()

    def drain(self, count):
        @pl.when(self.depth > 0)
        def _():
            @pl.loop(count - self.ring, count)
            def _(u):
                self.out_copy(u).wait_send()


def centre(values):
    average = jnp.mean(values, axis=-1, keepdims=True)
    centered = values - average
    spread = jnp.mean(centered * centered, axis=-1, keepdims=True)
    scaling = lax.rsqrt(spread + 1e-05)
    return centered * scaling, scaling


def norm_inward(scaled, normed, scaling):
    return scaling * (
        scaled
        - jnp.mean(scaled, axis=-1, keepdims=True)
        - normed * jnp.mean(scaled * normed, axis=-1, keepdims=True)
    )


def fold_rows(values):
    rows, width = values.shape
    return jnp.sum(values.reshape(rows // 8, 8, width), axis=0)


def attention_setup(tok_ref, wq_ref, wk_ref, wv_ref, rel_ref, corner_ref,
                    q_ref, k_ref, v_ref, krel_ref, qrel_ref, tq_ref, tk_ref, idx_ref, col_ref, row_ref):
    slots = tok_ref.shape[0]
    heads, wide = q_ref.shape[0], q_ref.shape[1]
    chunks = wide // LANES
    for weight, target in ((wq_ref, q_ref), (wk_ref, k_ref), (wv_ref, v_ref)):
        value = dot_nn(tok_ref[...], weight[...]).astype(LOW)
        for head in range(heads):
            target[head, :slots, :] = value[:, head * HEAD : (head + 1) * HEAD]
            if wide > slots:
                target[head, slots:, :] = jnp.zeros((wide - slots, HEAD), LOW)
    for weight, target in ((wk_ref, krel_ref), (wq_ref, qrel_ref)):
        value = dot_nn(rel_ref[...], weight[...]).astype(LOW)
        for head in range(heads):
            target[head] = value[:, head * HEAD : (head + 1) * HEAD]
    for head in range(heads):
        tq_ref[head] = dot_nt(q_ref[head], krel_ref[head])
        tk_ref[head] = dot_nt(k_ref[head], qrel_ref[head])
    row_ref[...] = jnp.zeros_like(row_ref)
    row_ref[:, :slots] = corner_ref[...]
    for kind in range(2):
        for big in range(chunks):
            here = slice(big * LANES, (big + 1) * LANES)
            col_ref[kind, here, :] = jnp.broadcast_to(row_ref[kind : kind + 1, here], (LANES, LANES)).T

    @pl.loop(0, chunks)
    def _(big):
        at = span(big * LANES, LANES)
        for kind in range(2):
            own = col_ref[kind, at, :]
            for chunk in range(chunks):
                other = row_ref[kind : kind + 1, chunk * LANES : (chunk + 1) * LANES]
                idx_ref[kind, chunk, at, :] = bucket((own - other) >> 3)


def attention_block(big, head, length, q_ref, k_ref, v_ref, tq_ref, tk_ref, idx_ref, log_ref, attend_ref, ctx_ref):
    wide = q_ref.shape[1]
    chunks = wide // LANES
    slots = attend_ref.shape[1]
    scale = (7.0 * HEAD) ** (-0.5)
    rows = min(LANES, slots - big * LANES)
    some = slice(big * LANES, big * LANES + rows)
    slant = lax.broadcasted_iota(jnp.int32, (LANES, LANES), 0) - lax.broadcasted_iota(
        jnp.int32, (LANES, LANES), 1
    )
    log_ref[:rows, :] = dot_nt(q_ref[head, some, :], k_ref[head])
    for chunk in range(chunks):
        there = slice(chunk * LANES, (chunk + 1) * LANES)
        away = (big - chunk) * LANES
        toward = log_ref[:rows, there]
        if abs(big - chunk) >= 2:
            lane = NB - 1 if away > 0 else 0
            toward = toward + tq_ref[head, some, lane : lane + 1]
            lane = NB - 1 - lane
            beside = jnp.broadcast_to(tk_ref[head, there, lane : lane + 1], (LANES, LANES))
        else:
            toward = toward + lane_gather(tq_ref[head, some, :NB], bucket(slant + away)[:rows])
            beside = lane_gather(tk_ref[head, there, :NB], bucket(slant - away))
        for kind in range(2):
            lanes = slice((kind + 1) * NB, (kind + 2) * NB)
            toward = toward + lane_gather(tq_ref[head, some, lanes], idx_ref[kind, chunk, some, :])
            beside = beside + lane_gather(tk_ref[head, there, lanes], idx_ref[kind, big, there, :])
        log_ref[:rows, there] = toward + beside.T[:rows]
    block = 32
    for start in range(0, rows, block):
        at = slice(start, start + block)
        j_at = lax.broadcasted_iota(jnp.int32, (block, wide), 1)
        masked = jnp.where(j_at < length, log_ref[at, :], NEG_FILL)
        peak = jnp.max(masked, axis=-1, keepdims=True)
        grown = jnp.exp((masked - peak) * scale)
        total = jnp.sum(grown, axis=-1, keepdims=True)
        attend_ref[head, big * LANES + start : big * LANES + start + block, :] = (
            grown * (1.0 / total)
        ).astype(LOW)
    ctx_ref[head, some, :] = dot_nn(attend_ref[head, some, :], v_ref[head]).astype(LOW)


def make_steps(step_ref, col_ref, slots):
    wide = step_ref.shape[1]
    block = 64
    if wide > slots:
        step_ref[:, slots:, :] = jnp.zeros_like(step_ref[:, slots:, :])

    @pl.loop(0, slots // block)
    def _(step):
        at = span(step * block, block)
        quotient = lax.broadcasted_iota(jnp.int32, (block, NB), 1) * BOX_STEP
        for kind in range(2):
            own = col_ref[kind, at, :]
            for rest in range(BOX_STEP):
                lanes = slice(rest * NB, (rest + 1) * NB)
                step_ref[kind, at, lanes] = (own <= quotient + rest).astype(FULL).astype(LOW)


def fold_at(kind, r, at):
    return (kind, at, slice(r % 3 * NB, (r % 3 + 1) * NB))


def bucket_sums(big, rows, mat, step_ref, col_ref, fold_ref, hist_ref):
    chunks = step_ref.shape[1] // LANES
    for kind in range(2):
        value = dot_nn(mat[...], step_ref[kind])
        for r in range(BOX_STEP):
            fold_ref[fold_at(kind, r, slice(r // 3 * LANES, r // 3 * LANES + rows))] = value[
                :, r * NB : (r + 1) * NB
            ]
    block = 32

    @pl.loop(0, rows // block)
    def _(step):
        local = step * block
        at = span(local, block)
        far = span(big * LANES + local, block)
        lane = lax.broadcasted_iota(jnp.int32, (block, NB), 1)
        row = lax.broadcasted_iota(jnp.int32, (block, NB), 0) + local
        part = [mat[at, c * LANES : (c + 1) * LANES].astype(FULL) for c in range(chunks)]
        zero = jnp.zeros((block, LANES), FULL)
        before = part[big - 1] if big >= 1 else zero
        after = part[big + 1] if big + 1 < chunks else zero
        mid = part[big]
        delta = lane - row
        window = jnp.where(delta > NB // 2, before, jnp.where(delta < 1 - NB // 2, after, mid))
        spread = lane_gather(window, (row + NB // 2 - lane) & (NB - 1))
        under = jnp.where(delta <= NB // 2 + 1, before, 0.0) + jnp.where(
            delta <= 1 - NB // 2, mid, 0.0
        )
        over = jnp.where(delta >= NB // 2, mid, 0.0) + jnp.where(delta >= -(NB // 2), after, 0.0)
        for c in range(big - 1):
            under = under + part[c]
        for c in range(big + 2, chunks):
            over = over + part[c]
        under = jnp.sum(under, axis=-1, keepdims=True)
        over = jnp.sum(over, axis=-1, keepdims=True)
        spread = jnp.where(lane == 0, over, jnp.where(lane == NB - 1, under, spread))
        hist_ref[at, 0:NB] = spread.astype(LOW)
        for kind in range(2):
            own = col_ref[kind, far, :]
            groups = [
                fold_ref[fold_at(kind, r, span(r // 3 * LANES + local, block))]
                for r in range(BOX_STEP)
            ]
            every = groups[-1][:, NB - 1 : NB]
            for bit in range(3):
                odd = (own & (1 << bit)) != 0
                groups = [
                    jnp.where(odd, groups[g + 1], groups[g]) for g in range(0, len(groups), 2)
                ]
            index = (own >> 3) + NB // 2 - lane
            found = lane_gather(groups[0], index & (NB - 1))
            found = jnp.where(index < 0, 0.0, found)
            found = jnp.where((index >= NB) | (lane == 0), every, found)
            following = pltpu.roll(found, NB - 1, 1)
            found = found - jnp.where(lane == NB - 1, 0.0, following)
            hist_ref[at, (kind + 1) * NB : (kind + 2) * NB] = found.astype(LOW)


def layer_kernel(
    length_ref, tok_ref, wq_ref, wk_ref, wv_ref, rel_ref, corner_ref,
    wo_ref, cot_ref, wi_ref, wu_ref, bo_ref, ga_ref, sa_ref, bi_ref, bu_ref, gf_ref, sf_ref,
    q_ref, k_ref, qrel_ref, ctx_ref, out_ref, grad_ref, grad_low_ref, hidden_ref, active_ref,
    mid_low_ref, inner_low_ref, small_ref, mat_ref, gq_ref, gv_ref, gkrel_ref, step_ref, col_ref,
    v_ref, krel_ref, attend_ref, tq_ref, tk_ref, idx_ref, row_ref, log_ref,
    own, inner, outer, normed_ref, scale_ref, sums_ref, gc_ref, hist_ref, gv_sum, gkrel_sum,
    in_send, in_recv, out_send, out_recv,
):
    slots = tok_ref.shape[0]
    chunks = slots // HOP
    heads, wide = q_ref.shape[0], q_ref.shape[1]
    blocks = wide // LANES
    per = LANES // HOP
    scale = (7.0 * HEAD) ** (-0.5)
    line = Line("head", own, inner, outer, (in_send, in_recv, out_send, out_recv))
    barrier = pltpu.get_barrier_semaphore()
    line.greet(barrier)
    sums_ref[...] = jnp.zeros_like(sums_ref)
    gv_sum[...] = jnp.zeros_like(gv_sum)
    gkrel_sum[...] = jnp.zeros_like(gkrel_sum)
    if wide > slots:
        mat_ref[:, slots:, :] = jnp.zeros_like(mat_ref[:, slots:, :])
    attention_setup(tok_ref, wq_ref, wk_ref, wv_ref, rel_ref, corner_ref,
                    q_ref, k_ref, v_ref, krel_ref, qrel_ref, tq_ref, tk_ref, idx_ref, col_ref, row_ref)
    pl.semaphore_wait(barrier, line.greeted())
    root = 0.5**0.5
    bell = (0.5 / jnp.pi) ** 0.5

    def forward_head(big, head):
        attention_block(big, head, length_ref[0], q_ref, k_ref, v_ref, tq_ref, tk_ref, idx_ref, log_ref,
                        attend_ref, ctx_ref)

    def put(c, value):
        for part in range(PAIR // HOP):
            own[c * (PAIR // HOP) + part] = value[part * HOP : (part + 1) * HOP]

    def got(u):
        first = line.total(u * (PAIR // HOP))
        return jnp.concatenate([outer[first + part] for part in range(PAIR // HOP)], axis=0)

    def project(c):
        at = span(c * PAIR, PAIR)
        context = jnp.concatenate([ctx_ref[head, at, :] for head in range(heads)], axis=1)
        put(c, dot_nn(context, wo_ref[...]))

    def after_attention(c, u):
        at = span(c * PAIR, PAIR)
        normed, scaling = centre(got(u) + bo_ref[...] + tok_ref[at, :].astype(FULL))
        normed_ref[at, :] = normed
        scale_ref[at, :] = scaling
        hidden_low = (normed * ga_ref[...] + sa_ref[...]).astype(LOW)
        hidden_ref[at, :] = hidden_low
        pre = dot_nn(hidden_low, wi_ref[...]) + bi_ref[...]
        grad_ref[at, :] = pre
        active = (pre * (1.0 + lax.erf(pre * root)) * 0.5).astype(LOW)
        active_ref[at, :] = active
        put(c, dot_nn(active, wu_ref[...]))

    def after_ffn(c, u):
        at = span(c * PAIR, PAIR)
        hidden = normed_ref[at, :] * ga_ref[...] + sa_ref[...]
        normed, scaling = centre(got(u) + bu_ref[...] + hidden)
        out_ref[at, :] = (normed * gf_ref[...] + sf_ref[...]).astype(LOW)
        upstream = cot_ref[at, :].astype(FULL)
        grad_mid = norm_inward(upstream * gf_ref[...], normed, scaling)
        sums_ref[4] += fold_rows(grad_mid)
        sums_ref[5] += fold_rows(upstream * normed)
        sums_ref[6] += fold_rows(upstream)
        pre = grad_ref[at, :]
        grad_ref[at, :] = grad_mid
        mid_low = grad_mid.astype(LOW)
        mid_low_ref[at, :] = mid_low
        grad_active = dot_nt(mid_low, wu_ref[...])
        slope = (1.0 + lax.erf(pre * root)) * 0.5 + pre * jnp.exp(-0.5 * pre * pre) * bell
        inner_low = (grad_active * slope).astype(LOW)
        sums_ref[3] += fold_rows(inner_low.astype(FULL))
        inner_low_ref[at, :] = inner_low
        put(c, dot_nt(inner_low, wi_ref[...]))

    def after_hidden(c, u):
        at = span(c * PAIR, PAIR)
        upstream = got(u) + grad_ref[at, :]
        normed = normed_ref[at, :]
        grad_attn = norm_inward(upstream * ga_ref[...], normed, scale_ref[at, :])
        sums_ref[0] += fold_rows(grad_attn)
        sums_ref[1] += fold_rows(upstream * normed)
        sums_ref[2] += fold_rows(upstream)
        grad_ref[at, :] = grad_attn
        grad_low_ref[at, :] = grad_attn.astype(LOW)

    def backward_block(big):
        rows = min(LANES, slots - big * LANES)
        some = slice(big * LANES, big * LANES + rows)
        value = dot_nt(grad_low_ref[some, :], wo_ref[...]).astype(LOW)
        for head in range(heads):
            gc_ref[head, :rows, :] = value[:, head * HEAD : (head + 1) * HEAD]

    def backward_head(big, head):
        rows = min(LANES, slots - big * LANES)
        some = slice(big * LANES, big * LANES + rows)
        gc = gc_ref[head, :rows, :]
        grad_attend = dot_nt(gc, v_ref[head])
        mean = jnp.sum(gc.astype(FULL) * ctx_ref[head, some, :].astype(FULL), axis=-1, keepdims=True)
        attend = attend_ref[head, some, :]
        mat_ref[head, some, :] = (attend.astype(FULL) * (grad_attend - mean)).astype(LOW)
        gv_sum[head] += dot_tn(attend, gc)
        bucket_sums(big, rows, mat_ref.at[head, some, :], step_ref, col_ref, tq_ref, hist_ref)
        hist = hist_ref[:rows, :]
        gq = dot_nn(mat_ref[head, some, :], k_ref[head]) + dot_nn(hist, krel_ref[head])
        gq_ref[head, some, :] = (gq * scale).astype(LOW)
        gkrel_sum[head] += dot_tn(hist, q_ref[head, some, :])

    for head in range(heads):
        forward_head(0, head)
    count = 3 * chunks
    ratio = PAIR // HOP
    first_back = 2 * chunks + line.trip + per
    last_slot = first_back + (blocks - 1) * per + heads

    @pl.loop(0, max(count + line.trip, last_slot))
    def _(slot):
        @pl.when((slot < chunks) & (lax.rem(slot, ratio) == 0))
        def _():
            project(slot // ratio)

        line.step(slot, count)
        ahead = slot + per
        for big in range(1, blocks):

            @pl.when(ahead // per == big)
            def _(big=big):
                forward_head(big, lax.rem(ahead, per))

        done = slot - line.trip - (ratio - 1)
        pair = done // ratio
        ready = (done >= 0) & (lax.rem(done + ratio, ratio) == 0)
        pairs = chunks // ratio

        @pl.when(ready & (pair < pairs))
        def _():
            after_attention(pair, pair)

        @pl.when(ready & (pair >= pairs) & (pair < 2 * pairs))
        def _():
            after_ffn(pair - pairs, pair)

        @pl.when(ready & (pair >= 2 * pairs) & (pair < 3 * pairs))
        def _():
            after_hidden(pair - 2 * pairs, pair)

        @pl.when(slot == 2 * chunks)
        def _():
            make_steps(step_ref, col_ref, slots)

        since = slot - first_back
        for big in range(blocks):

            @pl.when((since >= 0) & (since // per == big))
            def _(big=big):
                at_head = lax.rem(since, per)

                @pl.when(at_head == 0)
                def _():
                    backward_block(big)

                backward_head(big, at_head)

    for at in range(7):
        small_ref[at : at + 1, :] = jnp.sum(sums_ref[at], axis=0, keepdims=True)
    small_ref[7:8, :] = jnp.zeros_like(small_ref[7:8, :])
    for head in range(heads):
        gv_ref[head] = gv_sum[head, :slots, :].astype(LOW)
        gkrel_ref[head] = (gkrel_sum[head] * scale).astype(LOW)
    line.drain(count)


def layer(tokens, length, corners, w_query, w_key, w_value, rel, w_output, cotangent, w_inner, w_outer, vectors):
    slots, width = tokens.shape
    units = w_inner.shape[1]
    mine = w_query.shape[1]
    heads = mine // HEAD
    wide = -(-slots // LANES) * LANES
    assert units == width and heads == LANES // HOP and slots % PAIR == 0
    vmem = pl.BlockSpec(memory_space=pltpu.VMEM)
    chunks = slots // HOP
    shape = jax.ShapeDtypeStruct
    dma = pltpu.SemaphoreType.DMA
    return pl.pallas_call(
        layer_kernel,
        out_shape=(
            shape((heads, wide, HEAD), LOW),
            shape((heads, wide, HEAD), LOW),
            shape((heads, 3 * NB, HEAD), LOW),
            shape((heads, slots, HEAD), LOW),
            shape((slots, width), LOW),
            shape((slots, width), FULL),
            shape((slots, width), LOW),
            shape((slots, width), LOW),
            shape((slots, units), LOW),
            shape((slots, width), LOW),
            shape((slots, units), LOW),
            shape((8, width), FULL),
            shape((heads, wide, wide), LOW),
            shape((heads, slots, HEAD), LOW),
            shape((heads, slots, HEAD), LOW),
            shape((heads, 3 * NB, HEAD), LOW),
            shape((2, wide, BOX_STEP * NB), LOW),
            shape((2, wide, LANES), jnp.int32),
        ),
        in_specs=[pl.BlockSpec(memory_space=pltpu.SMEM)] + [vmem] * 17,
        out_specs=(vmem,) * 18,
        scratch_shapes=[
            pltpu.VMEM((heads, wide, HEAD), LOW),
            pltpu.VMEM((heads, 3 * NB, HEAD), LOW),
            pltpu.VMEM((heads, slots, wide), LOW),
            pltpu.VMEM((heads, wide, 3 * NB), FULL),
            pltpu.VMEM((heads, wide, 3 * NB), FULL),
            pltpu.VMEM((2, wide // LANES, wide, LANES), jnp.int32),
            pltpu.VMEM((2, wide), jnp.int32),
            pltpu.VMEM((LANES, wide), FULL),
            pltpu.VMEM((chunks, HOP, width), FULL),
            pltpu.VMEM((chunks, HOP, width), FULL),
            pltpu.VMEM((2 * chunks, HOP, width), FULL),
            pltpu.VMEM((slots, width), FULL),
            pltpu.VMEM((slots, 1), FULL),
            pltpu.VMEM((7, 8, width), FULL),
            pltpu.VMEM((heads, LANES, HEAD), LOW),
            pltpu.VMEM((LANES, 3 * NB), LOW),
            pltpu.VMEM((heads, wide, HEAD), FULL),
            pltpu.VMEM((heads, 3 * NB, HEAD), FULL),
            dma((chunks,)),
            dma((chunks,)),
            dma((2 * chunks,)),
            dma((2 * chunks,)),
        ],
        compiler_params=pltpu.CompilerParams(
            vmem_limit_bytes=VMEM_LIMIT, collective_id=1, has_side_effects=True
        ),
        name="layer",
    )(length, tokens, w_query, w_key, w_value, rel, corners,
      w_output, cotangent, w_inner, w_outer, *[v.reshape(1, -1) for v in vectors])


class Halving:
    def __init__(self, order, source, got, out, send, recv):
        self.order, self.source, self.got, self.out = order, source, got, out
        self.send, self.recv = send, recv
        self.b = lax.axis_index("batch")

    def part(self, stage, flip):
        bit = self.order[stage]
        rest = sorted(self.order[stage:], reverse=True)
        mine = (self.b >> bit) & 1
        pick = 1 - mine if flip else mine
        return tuple(pick if k == bit else slice(None) for k in rest)

    def copy(self, stage):
        source = self.source if stage == 0 else self.got[stage - 1]
        return pltpu.make_async_remote_copy(
            src_ref=source.at[self.part(stage, True)],
            dst_ref=self.got[stage],
            send_sem=self.send.at[stage],
            recv_sem=self.recv.at[stage],
            device_id={"batch": self.b ^ (1 << self.order[stage])},
            device_id_type=MESH,
        )

    def start(self):
        self.copy(0).start()

    def turn(self, stage):
        self.copy(stage).wait_recv()
        kept = self.source if stage == 0 else self.got[stage - 1]
        value = kept[self.part(stage, False)] + self.got[stage][...]
        if stage == 0:
            self.copy(0).wait_send()
        if stage + 1 < len(self.order):
            self.got[stage][...] = value
            self.copy(stage + 1).start()
        else:
            self.out[...] = value

    def drain(self):
        for stage in range(1, len(self.order)):
            self.copy(stage).wait_send()


def gradient_kernel(
    tok_ref, wq_ref, wk_ref, wv_ref, rel_ref,
    q_ref, k_ref, qrel_ref, ctx_ref, grad_ref, grad_low_ref, hidden_ref, active_ref,
    mid_low_ref, inner_low_ref, small_ref, mat_ref, gq_ref, gv_ref, gkrel_ref, step_ref, col_ref,
    gtok_ref, owq_ref, owk_ref, owv_ref, owo_ref, owi_ref, owu_ref, orel_ref, osmall_ref,
    own, inner, outer, turned_ref, fold_ref, hist_ref, gk_ref, gk_low_ref, gqrel_sum, gqrel_ref,
    work_ref, grel_ref, rel_own, rel_in, rel_out, rel_all, small_sum, small_got,
    *rest,
    bits, pieces, buffers,
):
    jobs_all = len(pieces) + 2
    got = [rest[at * bits : (at + 1) * bits] for at in range(jobs_all)]
    (in_send, in_recv, out_send, out_recv, rin_send, rin_recv, rout_send, rout_recv,
     piece_send, piece_recv, back_send, back_recv, small_send, small_recv) = rest[jobs_all * bits :]
    slots, width = tok_ref.shape
    chunks = slots // HOP
    heads, wide = q_ref.shape[0], q_ref.shape[1]
    blocks = wide // LANES
    per = LANES // HOP
    scale = (7.0 * HEAD) ** (-0.5)
    line = Line("head", own, inner, outer, (in_send, in_recv, out_send, out_recv))
    rel_line = Line("head", rel_own, rel_in, rel_out, (rin_send, rin_recv, rout_send, rout_recv), 1)
    b = lax.axis_index("batch")
    barrier = pltpu.get_barrier_semaphore()
    line.greet(barrier)
    for k in range(bits):
        pl.semaphore_signal(barrier, inc=1, device_id={"batch": b ^ (1 << k)}, device_id_type=MESH)

    orders = (list(range(bits)), [0] + list(range(bits - 1, 0, -1)))
    outs = (owq_ref, owk_ref, owv_ref, owo_ref, owi_ref, owu_ref)
    whole = (slice(None),) * (bits + 1)
    jobs = []
    for at, (which, start, size) in enumerate(pieces):
        jobs.append(
            Halving(
                orders[at % 2],
                work_ref.at[at % buffers],
                got[at],
                outs[which].at[:, start : start + size],
                piece_send.at[at],
                piece_recv.at[at],
            )
        )
    half = width // 2
    rel_jobs = []
    for side in range(2):
        lanes = slice(side * half, (side + 1) * half)
        at = len(pieces) + side
        rel_jobs.append(
            Halving(
                orders[side],
                grel_ref.at[whole + (lanes,)],
                got[at],
                rel_own.at[0, :, lanes],
                piece_send.at[at],
                piece_recv.at[at],
            )
        )

    def heads_of(ref):
        return jnp.concatenate([ref[head] for head in range(heads)], axis=1)

    def make(at):
        which, start, size = pieces[at]
        lanes = slice(start, start + size)
        if which == 0:
            value = dot_tn(tok_ref[...], heads_of(gq_ref)) + dot_tn(rel_ref[...], heads_of(gqrel_ref))
        elif which == 1:
            value = dot_tn(tok_ref[...], gk_ref[...]) + dot_tn(rel_ref[...], heads_of(gkrel_ref))
        elif which == 2:
            value = dot_tn(tok_ref[...], heads_of(gv_ref))
        elif which == 3:
            value = dot_tn(grad_low_ref[...], heads_of(ctx_ref))
        elif which == 4:
            value = dot_tn(hidden_ref[...], inner_low_ref[:, lanes])
        else:
            value = dot_tn(mid_low_ref[...], active_ref[:, lanes])
        target = work_ref.at[at % buffers]
        target[...] = value.reshape(target.shape)
        jobs[at].start()

    def small_copy(k):
        return pltpu.make_async_remote_copy(
            src_ref=small_sum.at[k],
            dst_ref=small_got.at[k],
            send_sem=small_send.at[k],
            recv_sem=small_recv.at[k],
            device_id={"batch": b ^ (1 << k)},
            device_id_type=MESH,
        )

    def small_turn(k):
        small_copy(k).wait_recv()
        value = small_sum[k] + small_got[k]
        if k + 1 < bits:
            small_sum[k + 1] = value
            small_copy(k + 1).start()
        else:
            osmall_ref[...] = value

    def back_copy(k):
        region = tuple(
            slice(None) if other > k else (b >> other) & 1 for other in range(bits - 1, -1, -1)
        )
        return pltpu.make_async_remote_copy(
            src_ref=rel_all.at[region],
            dst_ref=rel_all.at[region],
            send_sem=back_send.at[k],
            recv_sem=back_recv.at[k],
            device_id={"batch": b ^ (1 << k)},
            device_id_type=MESH,
        )

    def back_turn(k):
        back_copy(k).wait_recv()
        if k > 0:
            back_copy(k - 1).start()

    def rel_start():
        for head in range(heads):
            gqrel_ref[head] = (gqrel_sum[head] * scale).astype(LOW)
        value = dot_nt(heads_of(gkrel_ref), wk_ref[...]) + dot_nt(heads_of(gqrel_ref), wq_ref[...])
        grel_ref[...] = value.reshape(grel_ref.shape)
        for job in rel_jobs:
            job.start()

    def rel_turn(stage):
        for job in rel_jobs:
            job.turn(stage)

    def rel_step(slot):
        rel_line.step(jnp.int32(slot), 1)
        if slot == rel_line.trip:
            region = tuple((b >> other) & 1 for other in range(bits - 1, -1, -1))
            rel_all[region] = rel_out[0]
            back_copy(bits - 1).start()

    def column_head(big, head):
        rows = min(LANES, slots - big * LANES)
        some = slice(big * LANES, big * LANES + rows)
        lanes = slice(big * LANES, (big + 1) * LANES)
        for chunk in range(blocks):
            there = slice(chunk * LANES, (chunk + 1) * LANES)
            turned_ref[:, there] = mat_ref[head, there, lanes].T
        bucket_sums(big, rows, turned_ref.at[:rows, :], step_ref, col_ref, fold_ref, hist_ref)
        hist = hist_ref[:rows, :]
        gk = dot_nn(turned_ref[:rows, :], q_ref[head]) + dot_nn(hist, qrel_ref[head])
        gk_low_ref[head, :rows, :] = (gk * scale).astype(LOW)
        gqrel_sum[head] += dot_tn(hist, k_ref[head, some, :])

    def inputs_block(big):
        rows = min(LANES, slots - big * LANES)
        some = slice(big * LANES, big * LANES + rows)
        gk = jnp.concatenate([gk_low_ref[head, :rows, :] for head in range(heads)], axis=1)
        gk_ref[some, :] = gk
        gq = jnp.concatenate([gq_ref[head, some, :] for head in range(heads)], axis=1)
        gv = jnp.concatenate([gv_ref[head, some, :] for head in range(heads)], axis=1)
        value = dot_nt(gq, wq_ref[...]) + dot_nt(gk, wk_ref[...]) + dot_nt(gv, wv_ref[...])
        for part in range(rows // HOP):
            own[big * per + part] = value[part * HOP : (part + 1) * HOP]

    gqrel_sum[...] = jnp.zeros_like(gqrel_sum)
    small_sum[0] = small_ref[...]
    pl.semaphore_wait(barrier, line.greeted() + bits)
    small_copy(0).start()
    early = len(pieces) - 2
    make(0)
    make(1)

    @pl.loop(0, heads)
    def _(head):
        column_head(0, head)

    inputs_block(0)

    tasks = {}

    def add(slot, task):
        tasks.setdefault(slot, []).append(task)

    for at in range(2, early):
        add(at - 2, lambda at=at: make(at))
    for at in range(early):
        add(at, lambda at=at: jobs[at].turn(0))
        if bits > 1:
            for stage in range(1, bits):
                add(1 + 3 * (at // 2) + 3 * stage, lambda at=at, stage=stage: jobs[at].turn(stage))
    for k in range(bits):
        add(2 + 2 * k, lambda k=k: small_turn(k))
    ended = (blocks - 1) * per
    add(ended, rel_start)
    add(ended, lambda: make(early))
    add(ended, lambda: make(early + 1))
    for stage in range(bits):
        add(ended + 1 + 2 * stage, lambda stage=stage: rel_turn(stage))
    for side in range(2):
        for stage in range(bits):
            add(ended + 2 + 3 * stage, lambda side=side, stage=stage: jobs[early + side].turn(stage))
    for hop in range(rel_line.trip + 1):
        add(ended + 2 * bits + 1 + hop, lambda hop=hop: rel_step(hop))
    for k in range(bits - 1, -1, -1):
        add(ended + 2 * bits + 1 + rel_line.trip + bits - k, lambda k=k: back_turn(k))
    total = chunks + line.trip

    @pl.loop(0, max(total, max(tasks) + 1))
    def _(slot):
        line.step(slot, chunks)
        ahead = slot + per
        for big in range(1, blocks):

            @pl.when(ahead // per == big)
            def _(big=big):
                head = lax.rem(ahead, per)
                column_head(big, head)

                @pl.when(head == per - 1)
                def _():
                    inputs_block(big)

        for when in sorted(tasks):

            @pl.when(slot == when)
            def _(when=when):
                for task in tasks[when]:
                    task()

        done = slot - line.trip

        @pl.when((done >= 0) & (done < chunks))
        def _():
            at = span(done * HOP, HOP)
            gtok_ref[at, :] = (outer[done] + grad_ref[at, :]).astype(LOW)

    orel_ref[...] = rel_all[...]
    line.drain(chunks)
    rel_line.drain(1)
    for job in jobs + rel_jobs:
        job.drain()
    for k in range(bits):
        small_copy(k).wait_send()
        back_copy(k).wait_send()


def gradients(tokens, w_query, w_key, w_value, rel, kept, batch):
    slots, width = tokens.shape
    q, active = kept[0], kept[7]
    heads, wide = q.shape[:2]
    mine, units = heads * HEAD, active.shape[1]
    bits = batch.bit_length() - 1
    assert 1 << bits == batch
    vmem = pl.BlockSpec(memory_space=pltpu.VMEM)
    chunks = slots // HOP
    split = (2,) * bits
    part = width // batch
    rel_part = rel.shape[0] // batch
    assert mine == PIECE
    pieces = [(2, 0, PIECE), (3, 0, PIECE)]
    for start in range(0, units, PIECE):
        pieces += [(4, start, PIECE), (5, start, PIECE)]
    pieces += [(0, 0, PIECE), (1, 0, PIECE)]
    buffers = 4
    shape = jax.ShapeDtypeStruct
    got = []
    for _ in pieces:
        got += [pltpu.VMEM((2,) * (bits - 1 - s) + (part, PIECE), FULL) for s in range(bits)]
    for _ in range(2):
        got += [pltpu.VMEM((2,) * (bits - 1 - s) + (rel_part, width // 2), FULL) for s in range(bits)]
    dma = pltpu.SemaphoreType.DMA
    return pl.pallas_call(
        functools.partial(gradient_kernel, bits=bits, pieces=pieces, buffers=buffers),
        out_shape=(
            shape((slots, width), LOW),
            shape((part, mine), FULL),
            shape((part, mine), FULL),
            shape((part, mine), FULL),
            shape((part, mine), FULL),
            shape((part, units), FULL),
            shape((part, units), FULL),
            shape(split + (rel_part, width), FULL),
            shape((8, width), FULL),
        ),
        in_specs=[vmem] * 22,
        out_specs=(vmem,) * 9,
        scratch_shapes=[
            pltpu.VMEM((chunks, HOP, width), FULL),
            pltpu.VMEM((chunks, HOP, width), FULL),
            pltpu.VMEM((chunks, HOP, width), FULL),
            pltpu.VMEM((LANES, wide), LOW),
            pltpu.VMEM((2, 3 * LANES, 3 * NB), FULL),
            pltpu.VMEM((LANES, 3 * NB), LOW),
            pltpu.VMEM((slots, mine), LOW),
            pltpu.VMEM((heads, LANES, HEAD), LOW),
            pltpu.VMEM((heads, 3 * NB, HEAD), FULL),
            pltpu.VMEM((heads, 3 * NB, HEAD), LOW),
            pltpu.VMEM((buffers,) + split + (part, PIECE), FULL),
            pltpu.VMEM(split + (rel_part, width), FULL),
            pltpu.VMEM((1, rel_part, width), FULL),
            pltpu.VMEM((1, rel_part, width), FULL),
            pltpu.VMEM((1, rel_part, width), FULL),
            pltpu.VMEM(split + (rel_part, width), FULL),
            pltpu.VMEM((bits, 8, width), FULL),
            pltpu.VMEM((bits, 8, width), FULL),
        ]
        + got
        + [dma((chunks,))] * 4
        + [dma((1,))] * 4
        + [dma((len(pieces) + 2, bits))] * 2
        + [dma((bits,))] * 4,
        compiler_params=pltpu.CompilerParams(
            vmem_limit_bytes=VMEM_LIMIT, collective_id=2, has_side_effects=True
        ),
        name="gradients",
    )(tokens, w_query, w_key, w_value, rel, *kept)


def finish_kernel(out, gtok, gwq, gwk, gwv, gwo, gwi, gwu, grel, small, *targets):
    (o_out, o_gtok, o_gwq, o_gwk, o_gwv, o_gwo, o_gwi, o_gwu, o_grel) = targets[:9]
    o_out[...] = out[...]
    o_gtok[...] = gtok[...]
    o_gwq[...] = gwq[...]
    o_gwk[...] = gwk[...]
    o_gwv[...] = gwv[...]
    o_gwo[...] = gwo[...].T
    o_gwi[...] = gwi[...]
    o_gwu[...] = gwu[...].T
    o_grel[...] = grel[...]
    for at, target in enumerate(targets[9:]):
        target[...] = small[at]


def finish(out, gtok, gwq, gwk, gwv, gwo, gwi, gwu, grel, small):
    vmem = pl.BlockSpec(memory_space=pltpu.VMEM)
    shape = jax.ShapeDtypeStruct
    same = lambda a: shape(a.shape, a.dtype)
    turn = lambda a: shape(a.shape[::-1], a.dtype)
    return pl.pallas_call(
        finish_kernel,
        out_shape=(same(out), same(gtok), same(gwq), same(gwk), same(gwv), turn(gwo), same(gwi), turn(gwu), same(grel))
        + (shape(small.shape[1:], FULL),) * 7,
        in_specs=[vmem] * 10,
        out_specs=(vmem,) * 16,
        compiler_params=pltpu.CompilerParams(vmem_limit_bytes=VMEM_LIMIT),
        name="finish",
    )(out, gtok, gwq, gwk, gwv, gwo, gwi, gwu, grel, small)


def shards(
    tokens,
    page_lengths,
    corners,
    w_query,
    w_key,
    w_value,
    w_output,
    b_output,
    gain_attn,
    shift_attn,
    w_inner,
    b_inner,
    w_outer,
    b_outer,
    gain_ffn,
    shift_ffn,
    rel_tables,
    cotangent,
):
    rel = rel_tables.reshape(3 * NB, rel_tables.shape[2])
    vectors = (b_output, gain_attn, shift_attn, b_inner, b_outer, gain_ffn, shift_ffn)
    q, k, qrel, ctx, output, *kept = layer(
        tokens, page_lengths, corners, w_query, w_key, w_value, rel,
        w_output, cotangent, w_inner, w_outer, vectors,
    )
    done = gradients(
        tokens, w_query, w_key, w_value, rel, (q, k, qrel, ctx, *kept), lax.axis_size("batch")
    )
    gtok, gwq, gwk, gwv, gwo, gwi, gwu, grel, small = done
    grel = grel.reshape(rel_tables.shape)
    (output, gtok, gwq, gwk, gwv, gwo, gwi, gwu, grel, gbo, gga, gsa, gbi, gbu, ggf, gsf) = finish(
        output, gtok, gwq, gwk, gwv, gwo, gwi, gwu, grel, small
    )
    return (output, gtok, gwq, gwk, gwv, gwo, gbo, gga, gsa, gwi, gbi, gwu, gbu, ggf, gsf, grel)


def solution(mesh):
    in_specs = (
        P("batch", None),
        P("batch"),
        P(None, "batch"),
        P(None, "head"),
        P(None, "head"),
        P(None, "head"),
        P("head", None),
        P(),
        P(),
        P(),
        P(None, "head"),
        P("head"),
        P("head", None),
        P(),
        P(),
        P(),
        P(),
        P("batch", None),
    )
    out_specs = (
        P("batch", None),
        P("batch", None),
        P("batch", "head"),
        P("batch", "head"),
        P("batch", "head"),
        P("head", "batch"),
        P(),
        P(),
        P(),
        P("batch", "head"),
        P("head"),
        P("head", "batch"),
        P(),
        P(),
        P(),
        P(),
    )
    return jax.shard_map(shards, mesh=mesh, in_specs=in_specs, out_specs=out_specs, check_vma=False)
```

time: 410 us -> 344 us (0.84)
  Pallas kernels: 385 us -> 337 us
  local copies, waits for them, and re-layouts: 15 us -> 0 us
    pallas_call x3, Pallas kernels: 385 us -> 337 us  [the longest x1 200 us: layer(): pl.pallas_call(layer_kernel, out_shape=(shape((heads, wide, HEAD), LOW),...]
    unnamed x24 -> x0, local copies, waits for them, and re-layouts: 11.9 us -> none
where the time goes in v4:
time: 344 us; the launch traced here: 338 us
  Pallas kernels  337 us (98%)
    pallas_call x1, Pallas kernels, layer(): pl.pallas_call(layer_kernel, out_shape=(shape((heads, wide, HEAD), LOW),...  200 us
    pallas_call x1, Pallas kernels, gradients(): pl.pallas_call(functools.partial(gradient_kernel, bits=bits, pieces=piece...  131 us

profile of v4, /device:TPU:1, one launch (start us, length us, event | category | flops | bytes accessed | tf_op | source)
XLA Modules:
  0.0 338.1 jit_solution(11809566010457835745)
XLA Ops:
  1.3 200.0 %layer.1 = (bf16[4,640,64]{2,1,0:T(8,128)(2,1)}, bf16[4,640,64]{2,1,0:T(8,128)(2,1)}, bf16[4,384,64]{2,1,0:T(8,128)(2,1)}, bf16[4,576,64]{2,1,0:T(8,128)(2,1)}, ...) custom-call(s32[1]{0:T(128)S(6)} %copy.34.length_ref, ...), custom_call_target="tpu_custom_call" | custom-call | tf_op jit(solution)/shard_map/layer/pallas_call | solution.py:523
  201.3 131.4 %gradients.1 = (bf16[576,1024]{1,0:T(8,128)(2,1)}, f32[128,256]{1,0:T(8,128)}, f32[128,256]{1,0:T(8,128)}, f32[128,256]{1,0:T(8,128)}, f32[128,256]{1,0:T(8,128)...) custom-call(bf16[576,1024]{1,0:T(8,128)(2,1)} %tok_ref.3, ...), custom_call_target="tpu_custom_call" | custom-call | tf_op jit(solution)/shard_map/gradients/pallas_call | solution.py:891
  332.6 5.3 %finish.1 = (bf16[576,1024]{1,0:T(8,128)(2,1)}, bf16[576,1024]{1,0:T(8,128)(2,1)}, f32[128,256]{1,0:T(8,128)}, f32[128,256]{1,0:T(8,128)}, f32[128,256]{1,0:T(8,...) custom-call(bf16[576,1024]{1,0:T(8,128)(2,1)} %get-tuple-element.59., ...), custom_call_target="tpu_custom_call" | custom-call | tf_op jit(solution)/shard_map/finish/pallas_call | solution.py:958
